TPU v7x, 32 devices: a whole 2x2x4 slice. The times are simulated.
32 devices in a mesh: groups: 2 (over x), dp: 16 (over z, y, core).
Axes of the slice: x: 2, y: 2, z: 4, core: 2. Of those that a mesh axis runs over, the one named last changes fastest.
Arguments:
- layer_inputs: bfloat16 [4096, 2048], P(('groups', 'dp')), parts along dimension 0, may hold values from -0.125 to 0.125
- output_grads: bfloat16 [4096, 8192], P(('groups', 'dp')), parts along dimension 0, may hold values from -0.0625 to 0.0625
- query_grads: bfloat16 [128, 2, 512, 256], P('dp'), may hold values from -6 to 6
- eigenvalues: float32 [128, 512, 256], P('dp'), may hold values from 0.01 to 900, as said below
- out_basis: bfloat16 [64, 128, 128], replicated, may hold values from -0.5 to 0.5
- in_basis: bfloat16 [16, 128, 128], replicated, may hold values from -0.5 to 0.5
- doc_lengths: int32 [32], P('groups'), parts along dimension 0, may hold values from 1 to 512, 2048 in all
Outputs:
- influence: float32 [32, 2], P(('groups', 'dp')), parts along dimension 0
There are 2 independent parts, one for each index of `groups`. A program takes and returns all parts, laid end to end along the dimension named above; an argument that names none is the same for every part. Nothing has to cross between parts.
Inputs may be any that keep to these rules, and one draw needn't show every extreme that they name: `doc_lengths`: the 16 lengths sum to 2048, and the largest is exactly 512. `eigenvalues`: positive.
All inputs are finite; a program needn't handle non-finite values.
Results may differ from a plain program's by a relative error of at most 0.0044.
Values may be sent and summed in bfloat16 or wider, within the bound.
No kernel may reach another device: no remote copies, remote signals or barrier semaphores. Data moves between devices by JAX's collectives and lax.ppermute only.
A program may use at most 192 MiB of HBM per device.

v0:
```python
import math

import jax
import jax.numpy as jnp
from jax import lax
from jax.sharding import PartitionSpec as P


def turn_rows(columns, basis_blocks):
    group_count = basis_blocks.shape[0]
    block_width = basis_blocks.shape[1]
    grouped = columns.reshape(columns.shape[0], group_count, block_width)
    turned = jnp.einsum("tnk,nkj->tnj", grouped, basis_blocks, preferred_element_type=jnp.float32)
    return turned.reshape(columns.shape).astype(jnp.bfloat16)


def precondition(query_grads, eigenvalues, damping, tile_out, tile_in):
    blocks, queries, rows_out, rows_in = query_grads.shape
    block_width = tile_in.shape[-1]
    grouped = query_grads.reshape(blocks, queries, rows_out, rows_in // block_width, block_width)
    half_turned = jnp.einsum(
        "bqonk,bnkj->bqonj", grouped, tile_in, preferred_element_type=jnp.float32
    )
    half_turned = half_turned.reshape(blocks, queries, rows_out, rows_in).astype(jnp.bfloat16)
    grouped = half_turned.reshape(blocks, queries, rows_out // block_width, block_width, rows_in)
    turned = jnp.einsum("bqnki,bnkj->bqnji", grouped, tile_out, preferred_element_type=jnp.float32)
    turned = turned.reshape(blocks, queries, rows_out, rows_in)
    return (turned / (eigenvalues[:, None] + damping)).astype(jnp.bfloat16)


def tally_scores(grads_got, inputs_got, preconditioned, doc_starts, doc_ends):
    blocks, total_rows, rows_out = grads_got.shape
    queries = preconditioned.shape[1]
    row_step = math.gcd(1024, total_rows)
    flat_pre = preconditioned.reshape(blocks, queries * rows_out, preconditioned.shape[3])

    def one_piece(running, piece_index):
        start_row = piece_index * row_step
        grads_piece = lax.dynamic_slice_in_dim(grads_got, start_row, row_step, 1)
        inputs_piece = lax.dynamic_slice_in_dim(inputs_got, start_row, row_step, 1)
        projected = jnp.einsum(
            "bti,bpi->btp", inputs_piece, flat_pre, preferred_element_type=jnp.float32
        )
        projected = projected.reshape(blocks, row_step, queries, rows_out)
        scores = jnp.sum(projected * grads_piece[:, :, None, :].astype(jnp.float32), axis=(0, 3))
        positions = start_row + lax.iota(jnp.int32, row_step)
        member = (
            (positions[:, None] >= doc_starts[None, :]) & (positions[:, None] < doc_ends[None, :])
        ).astype(jnp.float32)
        added = jnp.einsum("td,tq->dq", member, scores, precision=lax.Precision.HIGHEST)
        return (running + added, None)

    initial = jnp.zeros((doc_starts.shape[0], queries), jnp.float32)
    summed, _ = lax.scan(one_piece, initial, jnp.arange(total_rows // row_step, dtype=jnp.int32))
    return summed


def local(layer_inputs, output_grads, query_grads, eigenvalues, out_basis, in_basis, doc_lengths):
    block_width = out_basis.shape[1]
    tok_count = layer_inputs.shape[0]
    tile_count = query_grads.shape[0]
    rows_out = query_grads.shape[2]
    rows_in = query_grads.shape[3]
    in_tiles = layer_inputs.shape[1] // rows_in
    out_tiles = output_grads.shape[1] // rows_out
    tile_ids = lax.axis_index("dp") * tile_count + lax.iota(jnp.int32, tile_count)
    out_sets = out_basis.reshape(out_tiles, rows_out // block_width, block_width, block_width)
    in_sets = in_basis.reshape(in_tiles, rows_in // block_width, block_width, block_width)
    tile_out = jnp.take(out_sets, tile_ids // in_tiles, axis=0)
    tile_in = jnp.take(in_sets, tile_ids % in_tiles, axis=0)
    eigen_sum = lax.psum(jnp.sum(eigenvalues), "dp")
    entries = output_grads.shape[1] * layer_inputs.shape[1]
    damping = 0.1 * (eigen_sum / entries)
    preconditioned = precondition(query_grads, eigenvalues, damping, tile_out, tile_in)
    grads_local = turn_rows(output_grads, out_basis)
    inputs_local = turn_rows(layer_inputs, in_basis)
    grads_tiles = grads_local.reshape(tok_count, out_tiles, rows_out).transpose(1, 0, 2)[:, None]
    grads_tiles = jnp.broadcast_to(grads_tiles, (out_tiles, in_tiles, tok_count, rows_out))
    grads_tiles = grads_tiles.reshape(out_tiles * in_tiles, tok_count, rows_out)
    inputs_tiles = inputs_local.reshape(tok_count, in_tiles, rows_in).transpose(1, 0, 2)[None]
    inputs_tiles = jnp.broadcast_to(inputs_tiles, (out_tiles, in_tiles, tok_count, rows_in))
    inputs_tiles = inputs_tiles.reshape(out_tiles * in_tiles, tok_count, rows_in)
    grads_got, inputs_got = (
        lax.all_to_all(grads_tiles, "dp", split_axis=0, concat_axis=1, tiled=True),
        lax.all_to_all(inputs_tiles, "dp", split_axis=0, concat_axis=1, tiled=True),
    )
    doc_ends = jnp.cumsum(doc_lengths)
    doc_starts = doc_ends - doc_lengths
    partial_scores = tally_scores(grads_got, inputs_got, preconditioned, doc_starts, doc_ends)
    return lax.psum_scatter(partial_scores, "dp", scatter_dimension=0, tiled=True)


def solution(mesh):
    in_specs = (
        P(("groups", "dp"), None),
        P(("groups", "dp"), None),
        P("dp", None, None, None),
        P("dp", None, None),
        P(),
        P(),
        P("groups"),
    )
    out_specs = P(("groups", "dp"), None)
    return jax.shard_map(local, mesh=mesh, in_specs=in_specs, out_specs=out_specs, check_vma=False)
```

profile of v0, /device:TPU:0, one launch (start us, length us, event | category | flops | bytes accessed | tf_op | source)
XLA Modules:
  0.0 880.5 jit_solution(9658958268555105254)
XLA Ops:
  0.0 1.9 convolution_convert_fusion
  1.9 0.2 copy.119
  2.1 4.3 broadcast_in_dim.42
  6.4 7.4 all-to-all-start
  13.8 4.5 fusion.20
  18.3 3.9 copy.129
  22.2 142.3 %all-to-all-done = bf16[128,128,256]{2,1,0:T(8,128)(2,1)} async-done(((bf16[128,128,256]{2,1,0:T(8,128)(2,1)}), bf16[128,128,256]{2,1,0:T(8,128)(2,1)}, u32[]{:S(2)}, u32[]{:S(2)}) %all-to-all-start) | async-done | bytes 8388640 | tf_op jit(solution)/shard_map/all_to_all | solution.py:85
  164.5 6.9 broadcast_in_dim.47
  171.4 36.5 %all-to-all-start.1 = ((bf16[128,128,512]{2,1,0:T(8,128)(2,1)}), bf16[128,128,512]{2,1,0:T(8,128)(2,1)}, u32[]{:S(2)}, u32[]{:S(2)}) async-start(bf16[128,128,512]{2,1,0:T(8,128)(2,1)} %bitcast.91), calls=%async_computation.1 | async-start | bytes 33554432 | tf_op jit(solution)/shard_map/all_to_all | solution.py:84
  207.9 0.0 copy-start.2
  207.9 3.9 reduce_sum.21
  211.9 320.0 %psum.7 = f32[]{:T(128)} all-reduce(f32[]{:T(128)} %reduce_sum.21), channel_id=1, replica_groups=mesh['groups'=2,'dp'=16] {'dp'}, use_global_device_ids=true, to_apply=%region_1.2 | all-reduce | flops 1 | bytes 8 | tf_op jit(solution)/shard_map/psum | solution.py:71
  531.9 0.6 gather_fusion.1
  532.6 5.5 convert_bitcast_fusion
  538.1 11.2 %copy.123 = bf16[8,2,512,2,128]{4,3,2,1,0:T(2,128)(2,1)} copy(bf16[8,2,512,2,128]{2,4,1,3,0:T(8,128)(2,1)} %convert_bitcast_fusion) | data formatting | bytes 8388608 | tf_op jit(solution)/shard_map/convert_element_type | solution.py:24
  549.3 7.6 convert_element_type.44
  556.9 0.7 gather_fusion
  557.6 3.6 fusion.12
  561.2 3.7 copy.126
  564.9 0.1 copy.116
  565.0 0.7 reduce.2
  565.8 0.7 sub.9
  567.1 2.5 broadcast_add_fusion
  569.6 0.0 copy-start.4
  569.6 6.8 fusion.6
  576.3 0.6 dynamic-slice
  576.9 7.7 copy.120
  584.6 13.9 %copy.130 = bf16[8,16,128,512]{3,2,1,0:T(8,128)(2,1)} copy(bf16[8,16,128,512]{3,2,0,1:T(8,128)(2,1)} %bitcast.23) | data formatting | bytes 33554432 | tf_op jit(solution)/shard_map/all_to_all | solution.py:84
  598.5 198.0 %while.11 = (s32[]{:T(128)}, f32[16,2]{0,1:T(2,128)S(1)}, s32[2]{0:T(128)S(1)}, s32[16]{0:T(128)S(1)}, s32[16]{0:T(128)}, /*index=5*/bf16[8,2048,256]{2,1,0:T(8,...) while((s32[]{:T(128)}, f32[16,2]{0,1:T(2,128)S(1)}, ...), condition=%wide.region_6.7_spmd.clone, body=%wide.region_3.6_spmd.clone.sunk | while | flops 4316380160 | bytes 201351744 | solution.py:54
  598.5 0.6 dynamic_slice.21
  599.8 11.4 %dynamic-slice_convert_fusion.2 = f32[8,1024,512]{2,1,0:T(8,128)} fusion(bf16[8,2048,512]{2,1,0:T(8,128)(2,1)} %get-tuple-element.175, s32[]{:T(128)S(6)} %select_n.124), kind=kLoop, calls=%fused_computation.3.clone.1 | loop fusion | flops 4194304 | bytes 25165828 | tf_op jit(solution)/shard_map/while/body/eval_jaxpr/convert_element_type | solution.py:45
  611.2 17.5 %mul.33 = f32[8,1024,2,512]{3,2,1,0:T(2,128)} broadcast(f32[8,1024,512]{2,1,0:T(8,128)} %dynamic-slice_convert_fusion.2), dimensions={0,1,3} | broadcast | bytes 50331648 | tf_op jit(solution)/shard_map/while/body/eval_jaxpr/mul | solution.py:45
  628.7 42.8 %mul.34 = f32[8,1024,1024]{2,1,0:T(8,128)} reshape(f32[8,1024,2,512]{3,2,1,0:T(2,128)} %mul.33) | data formatting | bytes 67108864 | tf_op jit(solution)/shard_map/while/body/eval_jaxpr/mul | solution.py:45
  671.5 17.4 %multiply_reduce_fusion.2 = f32[1024,1024]{1,0:T(8,128)} fusion(f32[8,1024,1024]{2,1,0:T(8,128)} %mul.34, bf16[8,1024,256]{2,1,0:T(8,128)(2,1)} %get-tuple-element.174, bf16[8,2048,256]{2,1,0:T(8,128)(2,1)} %get-tuple-element.173, s32[]{:T(128)S(6)} %select_n.124), kind=kOutput, calls=%fused_computation.2.clone.1 | convolution fusion | flops 4310695936 | bytes 46137348 | tf_op jit(solution)/shard_map/while/body/eval_jaxpr/bti,bpi->btp/dot_general | solution.py:41
  688.9 5.3 copy.165
  694.2 2.4 bitcast_reduce_fusion.2
  696.7 0.9 convolution_add_fusion.2
  697.6 0.6 dynamic_slice.21
  698.8 11.4 %dynamic-slice_convert_fusion.2 = f32[8,1024,512]{2,1,0:T(8,128)} fusion(bf16[8,2048,512]{2,1,0:T(8,128)(2,1)} %get-tuple-element.175, s32[]{:T(128)S(6)} %select_n.124), kind=kLoop, calls=%fused_computation.3.clone.1 | loop fusion | flops 4194304 | bytes 25165828 | tf_op jit(solution)/shard_map/while/body/eval_jaxpr/convert_element_type | solution.py:45
  710.3 17.5 %mul.33 = f32[8,1024,2,512]{3,2,1,0:T(2,128)} broadcast(f32[8,1024,512]{2,1,0:T(8,128)} %dynamic-slice_convert_fusion.2), dimensions={0,1,3} | broadcast | bytes 50331648 | tf_op jit(solution)/shard_map/while/body/eval_jaxpr/mul | solution.py:45
  727.7 42.8 %mul.34 = f32[8,1024,1024]{2,1,0:T(8,128)} reshape(f32[8,1024,2,512]{3,2,1,0:T(2,128)} %mul.33) | data formatting | bytes 67108864 | tf_op jit(solution)/shard_map/while/body/eval_jaxpr/mul | solution.py:45
  770.5 17.4 %multiply_reduce_fusion.2 = f32[1024,1024]{1,0:T(8,128)} fusion(f32[8,1024,1024]{2,1,0:T(8,128)} %mul.34, bf16[8,1024,256]{2,1,0:T(8,128)(2,1)} %get-tuple-element.174, bf16[8,2048,256]{2,1,0:T(8,128)(2,1)} %get-tuple-element.173, s32[]{:T(128)S(6)} %select_n.124), kind=kOutput, calls=%fused_computation.2.clone.1 | convolution fusion | flops 4310695936 | bytes 46137348 | tf_op jit(solution)/shard_map/while/body/eval_jaxpr/bti,bpi->btp/dot_general | solution.py:41
  787.9 5.3 copy.165
  793.2 2.4 bitcast_reduce_fusion.2
  795.7 0.9 convolution_add_fusion.2
  796.6 0.1 copy.131
  796.7 82.7 %all-reduce = f32[16,2]{1,0:T(8,128)S(1)} all-reduce(f32[16,2]{1,0:T(8,128)S(1)} %copy.131), channel_id=2, replica_groups=mesh['groups'=2,'dp'=16] {'dp'}, use_global_device_ids=true, to_apply=%region_7.8.clone | all-reduce | flops 32 | bytes 256
  879.4 1.1 constant_dynamic-slice_fusion
  (18 shorter events, 0.1 us)
Async XLA Ops:
  0.0 13.8 %copy-start = (bf16[64,128,128]{2,1,0:T(8,128)(2,1)S(1)}, bf16[64,128,128]{2,1,0:T(8,128)(2,1)}, u32[]{:S(2)}) copy-start(bf16[64,128,128]{2,1,0:T(8,128)(2,1)} %param.13) | copy-start | bytes 6291460
  6.4 158.1 %all-to-all-start = ((bf16[128,128,256]{2,1,0:T(8,128)(2,1)}), bf16[128,128,256]{2,1,0:T(8,128)(2,1)}, u32[]{:S(2)}, u32[]{:S(2)}) async-start(bf16[128,128,256]{2,1,0:T(8,128)(2,1)} %bitcast.92), calls=%async_computation | async-start | bytes 16777216 | tf_op jit(solution)/shard_map/all_to_all | solution.py:85
  171.4 413.2 %all-to-all-start.1 = ((bf16[128,128,512]{2,1,0:T(8,128)(2,1)}), bf16[128,128,512]{2,1,0:T(8,128)(2,1)}, u32[]{:S(2)}, u32[]{:S(2)}) async-start(bf16[128,128,512]{2,1,0:T(8,128)(2,1)} %bitcast.91), calls=%async_computation.1 | async-start | bytes 33554432 | tf_op jit(solution)/shard_map/all_to_all | solution.py:84
  207.9 324.0 %copy-start.2 = (bf16[16,128,128]{2,1,0:T(8,128)(2,1)S(1)}, bf16[16,128,128]{2,1,0:T(8,128)(2,1)}, u32[]{:S(2)}) copy-start(bf16[16,128,128]{2,1,0:T(8,128)(2,1)} %param.14) | copy-start | bytes 1572868
  561.2 3.8 copy-start.3
  569.6 6.8 copy-start.4
  796.6 83.9 %copy-start.1 = (bf16[64,128,128]{2,1,0:T(8,128)(2,1)S(1)}, bf16[64,128,128]{2,1,0:T(8,128)(2,1)}, u32[]{:S(2)}) copy-start(bf16[64,128,128]{2,1,0:T(8,128)(2,1)} %param.13) | copy-start | bytes 6291460
where the time goes:
time: 885 us; the launch traced here: 881 us
  blocking collectives  403 us (46%)
  local copies, waits for them, and re-layouts  195 us (22%)
  waiting for transfers between devices  142 us (16%)
  matrix products  51.9 us (6%)
  starting transfers between devices  44 us (5%)
  other arithmetic  42.3 us (5%)
    psum x1, blocking collectives, local(): eigen_sum = lax.psum(jnp.sum(eigenvalues), 'dp')  320 us
    all_to_all x1, waiting for transfers between devices, local(): lax.all_to_all(inputs_tiles, 'dp', split_axis=0, concat_axis=1, tiled=True)  142 us
    mul x4, local copies, waits for them, and re-layouts, one_piece(): projected * grads_piece[:, :, None, :].astype(jnp.float32)  121 us
    unnamed x1, blocking collectives  82.7 us
    all_to_all x1, starting transfers between devices, local(): lax.all_to_all(grads_tiles, 'dp', split_axis=0, concat_axis=1, tiled=True)  36.5 us
    dot_general x2, matrix products, one_piece(): jnp.einsum('bti,bpi->btp', inputs_piece, flat_pre, preferred_element_type...  34.7 us
    convert_element_type x2, other arithmetic, one_piece(): grads_piece[:, :, None, :].astype(jnp.float32)  22.8 us
    convert_element_type x2, local copies, waits for them, and re-layouts, precondition(): half_turned.reshape(blocks, queries, rows_out, rows_in).astype(jnp.bfloat16)  18.7 us
  transfers between devices with their start and end apart: 2, of which 1 were waited for; matrix products, arithmetic and copies ran while one was open for 7% of the time, Pallas kernels for 0%

commit v1 on v0

--- a/solution.py
+++ b/solution.py
@@ -1,9 +1,16 @@
+import functools
 import math
 
 import jax
 import jax.numpy as jnp
 from jax import lax
+from jax.experimental import pallas as pl
+from jax.experimental.pallas import tpu as pltpu
 from jax.sharding import PartitionSpec as P
+
+VMEM_LIMIT = 48 * 1024 * 1024
+F32 = jnp.float32
+BF16 = jnp.bfloat16
 
 
 def turn_rows(columns, basis_blocks):
@@ -55,7 +62,9 @@
     return summed
 
 
-def local(layer_inputs, output_grads, query_grads, eigenvalues, out_basis, in_basis, doc_lengths):
+def local_general(
+    layer_inputs, output_grads, query_grads, eigenvalues, out_basis, in_basis, doc_lengths
+):
     block_width = out_basis.shape[1]
     tok_count = layer_inputs.shape[0]
     tile_count = query_grads.shape[0]
@@ -90,6 +99,303 @@
     return lax.psum_scatter(partial_scores, "dp", scatter_dimension=0, tiled=True)
 
 
+def dot_nt(a, b):
+    return lax.dot_general(a, b, (((1,), (1,)), ((), ())), preferred_element_type=F32)
+
+
+def dot_tn(a, b):
+    return lax.dot_general(a, b, (((0,), (0,)), ((), ())), preferred_element_type=F32)
+
+
+def dot_tt(a, b):
+    return lax.dot_general(a, b, (((0,), (1,)), ((), ())), preferred_element_type=F32)
+
+
+def call(body, flops, bytes_accessed, **kw):
+    return pl.pallas_call(
+        body,
+        compiler_params=pltpu.CompilerParams(vmem_limit_bytes=VMEM_LIMIT),
+        cost_estimate=pl.CostEstimate(
+            flops=flops, bytes_accessed=bytes_accessed, transcendentals=0
+        ),
+        **kw,
+    )
+
+
+def rotate_inputs(layer_inputs, in_basis):
+    tokens, features = layer_inputs.shape
+    count, width, _ = in_basis.shape
+
+    def body(x_ref, b_ref, o_ref):
+        for n in range(count):
+            cols = slice(n * width, (n + 1) * width)
+            o_ref[:, cols] = jnp.dot(
+                x_ref[:, cols], b_ref[n], preferred_element_type=F32
+            ).astype(BF16)
+
+    return call(
+        body,
+        2 * tokens * features * width,
+        4 * tokens * features + 2 * features * width,
+        out_shape=jax.ShapeDtypeStruct((tokens, features), BF16),
+        name="rotate_inputs",
+    )(layer_inputs, in_basis)
+
+
+def rotate_grads(output_grads, out_basis, chip, chips):
+    tokens, units = output_grads.shape
+    width = out_basis.shape[1]
+    part = units // chips
+    per = part // width
+
+    def body(chip_ref, g_ref, b_ref, *o_refs):
+        step = pl.program_id(0)
+        for k in range(chips):
+
+            @pl.when(step == k)
+            def _():
+                for n in range(per):
+                    cols = slice(n * width, (n + 1) * width)
+                    o_refs[k][cols, :] = dot_tt(b_ref[n], g_ref[:, cols]).astype(BF16)
+
+    grid_spec = pltpu.PrefetchScalarGridSpec(
+        num_scalar_prefetch=1,
+        grid=(chips,),
+        in_specs=[
+            pl.BlockSpec((tokens, part), lambda k, c: (0, k ^ c[0])),
+            pl.BlockSpec((per, width, width), lambda k, c: (k ^ c[0], 0, 0)),
+        ],
+        out_specs=[pl.BlockSpec((part, tokens), lambda k, c: (0, 0))] * chips,
+    )
+    return call(
+        body,
+        2 * tokens * units * width,
+        4 * tokens * units + 2 * units * width,
+        grid_spec=grid_spec,
+        out_shape=[jax.ShapeDtypeStruct((part, tokens), BF16)] * chips,
+        name="rotate_grads",
+    )(chip[None], output_grads, out_basis)
+
+
+def sum_eigenvalues(eigenvalues):
+    tiles, rows, cols = eigenvalues.shape
+
+    def body(e_ref, o_ref):
+        @pl.when(pl.program_id(0) == 0)
+        def _():
+            o_ref[...] = jnp.zeros_like(o_ref)
+
+        part = jnp.sum(e_ref[0].reshape(rows // 8, 8, cols), axis=0)
+        total = part[:, :128]
+        for n in range(1, cols // 128):
+            total = total + part[:, n * 128 : (n + 1) * 128]
+        o_ref[...] += total
+
+    return call(
+        body,
+        tiles * rows * cols,
+        4 * tiles * rows * cols,
+        grid=(tiles,),
+        in_specs=[pl.BlockSpec((1, rows, cols), lambda b: (b, 0, 0))],
+        out_specs=pl.BlockSpec((8, 128), lambda b: (0, 0)),
+        out_shape=jax.ShapeDtypeStruct((8, 128), F32),
+        name="sum_eigenvalues",
+    )(eigenvalues)
+
+
+def precondition_rows(query_grads, eigenvalues, sums, out_basis, in_basis, me, entries):
+    tiles, queries, rows, cols = query_grads.shape
+    width = in_basis.shape[1]
+    features = in_basis.shape[0] * width
+    in_tiles = features // cols
+    groups = tiles // in_tiles
+    n_out, n_in = rows // width, cols // width
+
+    def body(me_ref, q_ref, e_ref, s_ref, ob_ref, ib_ref, o_ref):
+        damping = 0.1 * (jnp.sum(s_ref[...], keepdims=True) / entries)
+        scale = 1.0 / (e_ref[0] + damping)
+        for q in range(queries):
+            half = [
+                jnp.dot(
+                    q_ref[0, q, :, n * width : (n + 1) * width],
+                    ib_ref[n],
+                    preferred_element_type=F32,
+                ).astype(BF16)
+                for n in range(n_in)
+            ]
+            half = jnp.concatenate(half, axis=1)
+            for n in range(n_out):
+                span = slice(n * width, (n + 1) * width)
+                turned = dot_tn(ob_ref[n], half[span, :])
+                o_ref[q, span, :] = (turned * scale[span, :]).astype(BF16)
+
+    grid_spec = pltpu.PrefetchScalarGridSpec(
+        num_scalar_prefetch=1,
+        grid=(tiles,),
+        in_specs=[
+            pl.BlockSpec((1, queries, rows, cols), lambda b, m: (b, 0, 0, 0)),
+            pl.BlockSpec((1, rows, cols), lambda b, m: (b, 0, 0)),
+            pl.BlockSpec(sums.shape, lambda b, m: (0, 0)),
+            pl.BlockSpec((n_out, width, width), lambda b, m: (m[0] * groups + b // in_tiles, 0, 0)),
+            pl.BlockSpec((n_in, width, width), lambda b, m: (b % in_tiles, 0, 0)),
+        ],
+        out_specs=pl.BlockSpec(
+            (queries, rows, cols), lambda b, m: (0, b // in_tiles, b % in_tiles)
+        ),
+    )
+    return call(
+        body,
+        4 * tiles * queries * rows * cols * width,
+        tiles * rows * cols * (4 + 4 * queries),
+        grid_spec=grid_spec,
+        out_shape=jax.ShapeDtypeStruct((queries, groups * rows, features), BF16),
+        name="precondition",
+    )(me[None], query_grads, eigenvalues, sums, out_basis, in_basis)
+
+
+def tally(where, inputs, grads, own, sibling, starts, ends, running):
+    pieces = len(inputs)
+    tokens, features = inputs[0].shape
+    part = grads[0].shape[0]
+    queries, rows, _ = own.shape
+    block = min(rows, 512)
+    per = rows // block
+    steps = queries * per
+    docs = starts.shape[0]
+
+    def body(where_ref, *refs):
+        x_refs = refs[:pieces]
+        g_refs = refs[pieces : 2 * pieces]
+        own_ref, sib_ref, st_ref, en_ref, run_ref, o_ref, x_all = refs[2 * pieces :]
+        step = pl.program_id(0)
+
+        @pl.when(step == 0)
+        def _():
+            o_ref[...] = run_ref[...]
+            for n in range(pieces):
+                x_all[n * tokens : (n + 1) * tokens, :] = x_refs[n][...]
+
+        def go(p_ref):
+            query = lax.rem(step, steps) // per
+            turned = dot_nt(p_ref[0], x_all[...])
+            for n in range(pieces):
+                score = jnp.sum(
+                    turned[:, n * tokens : (n + 1) * tokens] * g_refs[n][...].astype(F32),
+                    axis=0,
+                    keepdims=True,
+                )
+                spot = where_ref[1 + n] * tokens + lax.broadcasted_iota(
+                    jnp.int32, (docs, tokens), 1
+                )
+                inside = (spot >= st_ref[...]) & (spot < en_ref[...])
+                o_ref[query] += jnp.where(inside, score, 0.0)
+
+        @pl.when(step < steps)
+        def _():
+            go(own_ref)
+
+        @pl.when(step >= steps)
+        def _():
+            go(sib_ref)
+
+    def g_map(s, w):
+        core = jnp.where(s < steps, w[0], 1 - w[0])
+        return (core * per + lax.rem(s, per), 0)
+
+    def own_map(s, w):
+        s = jnp.minimum(s, steps - 1)
+        return (s // per, lax.rem(s, per), 0)
+
+    def sib_map(s, w):
+        s = jnp.maximum(s - steps, 0)
+        return (s // per, lax.rem(s, per), 0)
+
+    whole = lambda a: pl.BlockSpec(a.shape, lambda s, w: (0,) * len(a.shape))
+    grid_spec = pltpu.PrefetchScalarGridSpec(
+        num_scalar_prefetch=1,
+        grid=(2 * steps,),
+        in_specs=[whole(x) for x in inputs]
+        + [pl.BlockSpec((block, tokens), g_map) for _ in grads]
+        + [
+            pl.BlockSpec((1, block, features), own_map),
+            pl.BlockSpec((1, block, features), sib_map),
+            whole(starts),
+            whole(ends),
+            whole(running),
+        ],
+        out_specs=whole(running),
+        scratch_shapes=[pltpu.VMEM((pieces * tokens, features), BF16)],
+    )
+    return call(
+        body,
+        4 * pieces * tokens * features * queries * rows,
+        4 * queries * rows * features + pieces * tokens * 2 * (features + part),
+        grid_spec=grid_spec,
+        out_shape=jax.ShapeDtypeStruct(running.shape, F32),
+        name="tally",
+    )(where, *inputs, *grads, own, sibling, starts, ends, running)
+
+
+def local_rows(
+    depth, layer_inputs, output_grads, query_grads, eigenvalues, out_basis, in_basis, doc_lengths
+):
+    devices = 4 * depth
+    chips = 2 * depth
+    tokens = layer_inputs.shape[0]
+    queries = query_grads.shape[1]
+    entries = output_grads.shape[1] * layer_inputs.shape[1]
+    me = lax.axis_index("dp")
+    chip = me // 2
+    core = me % 2
+
+    def swap(value, offset):
+        return lax.ppermute(value, "dp", [(i, i ^ offset) for i in range(devices)])
+
+    x = rotate_inputs(layer_inputs, in_basis)
+    sums = lax.all_gather(sum_eigenvalues(eigenvalues), "dp", tiled=True)
+    g = rotate_grads(output_grads, out_basis, chip, chips)
+
+    xs = [x] + [None] * (chips - 1)
+    xs[6] = swap(x, 12)
+    xs[2] = swap(x, 4)
+    xs[1] = swap(x, 2)
+    xs[4] = swap(xs[6], 4)
+    xs[3] = swap(xs[2], 2)
+    xs[7] = swap(xs[6], 2)
+    xs[5] = swap(xs[4], 2)
+    gs = [g[0]] + [swap(g[k], 2 * k) for k in range(1, chips)]
+
+    own = precondition_rows(query_grads, eigenvalues, sums, out_basis, in_basis, me, entries)
+    sibling = swap(own, 1)
+
+    doc_ends = jnp.cumsum(doc_lengths)
+    doc_starts = doc_ends - doc_lengths
+    docs = doc_lengths.shape[0]
+    starts = jnp.broadcast_to(doc_starts[:, None], (docs, tokens))
+    ends = jnp.broadcast_to(doc_ends[:, None], (docs, tokens))
+    running = jnp.zeros((queries, docs, tokens), F32)
+    for pair in ((0, 1), (2, 3), (6, 7), (4, 5)):
+        where = jnp.stack([core] + [me ^ (2 * k) for k in pair]).astype(jnp.int32)
+        running = tally(
+            where, [xs[k] for k in pair], [gs[k] for k in pair], own, sibling, starts, ends, running
+        )
+    shares = jnp.sum(running, axis=2)
+    for offset in (1, 2, 4, 8):
+        shares = shares + swap(shares, offset)
+    each = docs // devices
+    mine = lax.dynamic_slice_in_dim(shares, me * each, each, 1)
+    return mine.T
+
+
+def local(layer_inputs, output_grads, query_grads, eigenvalues, out_basis, in_basis, doc_lengths, devices):
+    args = (layer_inputs, output_grads, query_grads, eigenvalues, out_basis, in_basis, doc_lengths)
+    in_tiles = layer_inputs.shape[1] // query_grads.shape[3]
+    tile_count = query_grads.shape[0]
+    if devices == 16 and tile_count % in_tiles == 0:
+        return local_rows(devices // 4, *args)
+    return local_general(*args)
+
+
 def solution(mesh):
     in_specs = (
         P(("groups", "dp"), None),
@@ -101,4 +407,5 @@
         P("groups"),
     )
     out_specs = P(("groups", "dp"), None)
-    return jax.shard_map(local, mesh=mesh, in_specs=in_specs, out_specs=out_specs, check_vma=False)
+    body = functools.partial(local, devices=mesh.shape["dp"])
+    return jax.shard_map(body, mesh=mesh, in_specs=in_specs, out_specs=out_specs, check_vma=False)

time: 885 us -> 156 us (0.18)
  blocking collectives: 403 us -> 23.4 us
  local copies, waits for them, and re-layouts: 195 us -> 13.7 us
  waiting for transfers between devices: 142 us -> 47.7 us
  matrix products: 51.9 us -> 0 us
  other arithmetic: 42.3 us -> 0.56 us
  Pallas kernels: 0 us -> 41 us
  starting transfers between devices: 44 us -> 28.5 us
    psum x1 -> x0, blocking collectives: 320 us -> none  [local(): eigen_sum = lax.psum(jnp.sum(eigenvalues), 'dp')]
    all_to_all x2 -> x0, waiting for transfers between devices: 142 us -> none  [the longest x1 142 us: local(): lax.all_to_all(inputs_tiles, 'dp', split_axis=0, concat_axis=1, tiled=True)]
    mul x4 -> x0, local copies, waits for them, and re-layouts: 121 us -> none  [one_piece(): projected * grads_piece[:, :, None, :].astype(jnp.float32)]
    unnamed x1 -> x0, blocking collectives: 82.7 us -> none
    dot_general x8 -> x0, matrix products: 51.9 us -> none  [the longest x2 34.7 us: one_piece(): jnp.einsum('bti,bpi->btp', inputs_piece, flat_pre, preferred_element_type...]
    ppermute x0 -> x19, waiting for transfers between devices: none -> 47.7 us  [swap(): return lax.ppermute(value, 'dp', [(i, i ^ offset) for i in range(devices)])]
    all_to_all x2 -> x0, starting transfers between devices: 44 us -> none  [the longest x1 36.5 us: local(): lax.all_to_all(grads_tiles, 'dp', split_axis=0, concat_axis=1, tiled=True)]
    pallas_call x0 -> x8, Pallas kernels: none -> 41 us  [the longest x4 24.6 us: tally(): call(body, 4 * pieces * tokens * features * queries * rows, 4 * queries *...]
  transfers between devices with their start and end apart: 2 -> 19, of which waited for: 1 -> 9; matrix products, arithmetic and copies ran while one was open for 7% -> 0% of each run, Pallas kernels for 0% -> 16%
where the time goes in v1:
time: 156 us; the launch traced here: 155 us
  waiting for transfers between devices  47.7 us (31%)
  Pallas kernels  41 us (26%)
  starting transfers between devices  28.5 us (18%)
  blocking collectives  23.4 us (15%)
  local copies, waits for them, and re-layouts  13.7 us (9%)
    ppermute x19, waiting for transfers between devices, swap(): return lax.ppermute(value, 'dp', [(i, i ^ offset) for i in range(devices)])  47.7 us
    ppermute x19, starting transfers between devices, swap(): return lax.ppermute(value, 'dp', [(i, i ^ offset) for i in range(devices)])  28.5 us
    pallas_call x4, Pallas kernels, tally(): call(body, 4 * pieces * tokens * features * queries * rows, 4 * queries *...  24.6 us
    all_gather x1, blocking collectives, local_rows(): sums = lax.all_gather(sum_eigenvalues(eigenvalues), 'dp', tiled=True)  23.4 us
    unnamed x38, local copies, waits for them, and re-layouts  12.8 us
    pallas_call x1, Pallas kernels, precondition_rows(): call(body, 4 * tiles * queries * rows * cols * width, tiles * rows * cols...  9.69 us
    pallas_call x1, Pallas kernels, rotate_grads(): call(body, 2 * tokens * units * width, 4 * tokens * units + 2 * units * w...  5.74 us
  transfers between devices with their start and end apart: 19, of which 9 were waited for; matrix products, arithmetic and copies ran while one was open for 0% of the time, Pallas kernels for 16%

profile of v1, /device:TPU:0, one launch (start us, length us, event | category | flops | bytes accessed | tf_op | source)
XLA Modules:
  0.0 155.1 jit_solution(11235812843199977900)
XLA Ops:
  0.0 2.2 %copy-done.1 = f32[8,512,256]{2,1,0:T(8,128)S(1)} copy-done((f32[8,512,256]{2,1,0:T(8,128)S(1)}, f32[8,512,256]{2,1,0:T(8,128)}, u32[]{:S(2)}) %copy-start.1) | copy-done | bytes 4194328
  2.2 0.7 sum_eigenvalues.1
  2.9 23.4 %all_gather.3.s_ref = f32[128,128]{1,0:T(8,128)S(1)} all-gather(f32[8,128]{1,0:T(8,128)S(1)} %sum_eigenvalues.1), channel_id=1, replica_groups=mesh['groups'=2,'dp'=16] {'dp'}, dimensions={0}, use_global_device_ids=true | all-gather | bytes 69632 | tf_op jit(solution)/shard_map/all_gather | solution.py:355
  26.3 9.7 %precondition.1.refs_4_ = bf16[2,512,2048]{2,1,0:T(8,128)(2,1)} custom-call(s32[1]{0:T(128)} %bitcast.4.me_ref, bf16[8,2,512,256]{3,2,1,0:T(8,128)(2,1)} %q_ref.1, f32[8,512,256]{2,1,0:T(8,128)} %e_ref.3, f32[128,128]{1,0:T(8,128)S(1)} %all_gather.3.s_ref, bf16[64,128,128]{2,1,0:T(8,128)(2,1)S(1)} %copy-done.2, bf16[16,128,128]{2,1,0:T(8,128)(2,1)S(1)} %copy-done.3), custom_call_target="tpu_custom_call" | custom-call | flops 1073741824 | bytes 12582912 | tf_op jit(solution)/shard_map/precondition/pallas_call | solution.py:246
  36.0 0.4 collective-permute-start.5
  36.3 0.3 rotate_inputs.1.refs_0_
  36.7 1.6 %copy-done.4 = bf16[128,8192]{1,0:T(8,128)(2,1)S(1)} copy-done((bf16[128,8192]{1,0:T(8,128)(2,1)S(1)}, bf16[128,8192]{1,0:T(8,128)(2,1)}, u32[]{:S(2)}) %copy-start.4) | copy-done | bytes 2097176
  38.3 5.7 %rotate_grads.1 = (bf16[1024,128]{1,0:T(8,128)(2,1)S(1)}, bf16[1024,128]{1,0:T(8,128)(2,1)S(1)}, bf16[1024,128]{1,0:T(8,128)(2,1)S(1)}, bf16[1024,128]{1,0:T(8,1...) custom-call(s32[1]{0:T(128)} %bitcast.3.chip_ref, ...), custom_call_target="tpu_custom_call" | custom-call | flops 268435456 | bytes 6291456 | tf_op jit(solution)/shard_map/rotate_grads/pallas_call | solution.py:170
  44.1 0.7 copy-done.6
  44.8 0.7 copy-done.12
  45.5 0.7 copy-done.14
  46.2 0.7 copy-done.16
  46.9 0.7 copy-done.17
  47.6 2.0 %collective-permute-start.11 = (bf16[1024,128]{1,0:T(8,128)(2,1)S(1)}, bf16[1024,128]{1,0:T(8,128)(2,1)S(1)}, u32[]{:S(2)}, u32[]{:S(2)}) collective-permute-start(bf16[1024,128]{1,0:T(8,128)(2,1)S(1)} %get-tuple-element.17), channel_id=1, source_target_pairs={{0,4},{1,5},{2,6},{3,7},{4,0},{5,1},{6,2},{7,3},{8,12},{9,13},{10,... | collective-permute-start | bytes 786440 | tf_op jit(solution)/shard_map/ppermute | solution.py:352
  49.6 6.3 %collective-permute-done.14.refs_3_ = bf16[1024,128]{1,0:T(8,128)(2,1)S(1)} collective-permute-done((bf16[1024,128]{1,0:T(8,128)(2,1)S(1)}, bf16[1024,128]{1,0:T(8,128)(2,1)S(1)}, u32[]{:S(2)}, u32[]{:S(2)}) %collective-permute-start.14) | collective-permute-done | bytes 262176 | tf_op jit(solution)/shard_map/ppermute | solution.py:352
  55.9 0.7 copy-done.8
  56.6 0.3 collective-permute-start.13
  56.9 3.7 %collective-permute-start.1 = (bf16[128,2048]{1,0:T(8,128)(2,1)S(1)}, bf16[128,2048]{1,0:T(8,128)(2,1)S(1)}, u32[]{:S(2)}, u32[]{:S(2)}) collective-permute-start(bf16[128,2048]{1,0:T(8,128)(2,1)S(1)} %collective-permute-done.refs_0_), channel_id=1, source_target_pairs={{0,4},{1,5},{2,6},{3,7},{4,0},{5,1},{6,2},{7,3},{8,12},{9,13},{10,... | collective-permute-start | bytes 1572872 | tf_op jit(solution)/shard_map/ppermute | solution.py:352
  60.6 8.8 %collective-permute-done.11.refs_2_ = bf16[1024,128]{1,0:T(8,128)(2,1)S(1)} collective-permute-done((bf16[1024,128]{1,0:T(8,128)(2,1)S(1)}, bf16[1024,128]{1,0:T(8,128)(2,1)S(1)}, u32[]{:S(2)}, u32[]{:S(2)}) %collective-permute-start.11) | collective-permute-done | bytes 262176 | tf_op jit(solution)/shard_map/ppermute | solution.py:352
  69.5 0.1 pad_add_fusion.3.where_ref
  69.6 1.0 collective-permute-start.10
  70.7 14.7 %collective-permute-done.12.refs_3_ = bf16[1024,128]{1,0:T(8,128)(2,1)S(1)} collective-permute-done((bf16[1024,128]{1,0:T(8,128)(2,1)S(1)}, bf16[1024,128]{1,0:T(8,128)(2,1)S(1)}, u32[]{:S(2)}, u32[]{:S(2)}) %collective-permute-start.12) | collective-permute-done | bytes 262176 | tf_op jit(solution)/shard_map/ppermute | solution.py:352
  85.3 0.7 copy-done.10
  86.0 2.5 %collective-permute-start.6 = (bf16[128,2048]{1,0:T(8,128)(2,1)S(1)}, bf16[128,2048]{1,0:T(8,128)(2,1)S(1)}, u32[]{:S(2)}, u32[]{:S(2)}) collective-permute-start(bf16[128,2048]{1,0:T(8,128)(2,1)S(1)} %collective-permute-done.refs_0_), channel_id=1, source_target_pairs={{0,2},{1,3},{2,0},{3,1},{4,6},{5,7},{6,4},{7,5},{8,10},{9,11},{10,... | collective-permute-start | bytes 1572872 | tf_op jit(solution)/shard_map/ppermute | solution.py:352
  88.6 0.1 copy.11
  88.8 0.1 reduce
  88.9 1.3 collective-permute-start.7
  90.3 2.0 %collective-permute-start.8 = (bf16[1024,128]{1,0:T(8,128)(2,1)}, bf16[1024,128]{1,0:T(8,128)(2,1)S(1)}, u32[]{:S(2)}, u32[]{:S(2)}) collective-permute-start(bf16[1024,128]{1,0:T(8,128)(2,1)} %copy-done.16), channel_id=1, source_target_pairs={{0,14},{1,15},{2,12},{3,13},{4,10},{5,11},{6,8},{7,9},{8,6},{9,7},... | collective-permute-start | bytes 786440 | tf_op jit(solution)/shard_map/ppermute | solution.py:352
  92.3 2.0 %collective-permute-start.2 = (bf16[128,2048]{1,0:T(8,128)(2,1)S(1)}, bf16[128,2048]{1,0:T(8,128)(2,1)S(1)}, u32[]{:S(2)}, u32[]{:S(2)}) collective-permute-start(bf16[128,2048]{1,0:T(8,128)(2,1)S(1)} %collective-permute-done.1.refs_0_), channel_id=1, source_target_pairs={{0,2},{1,3},{2,0},{3,1},{4,6},{5,7},{6,4},{7,5},{8,10},{9,11},{10,... | collective-permute-start | bytes 1572872 | tf_op jit(solution)/shard_map/ppermute | solution.py:352
  94.5 2.2 %copy-done = bf16[2,512,2048]{2,1,0:T(8,128)(2,1)S(1)} copy-done((bf16[2,512,2048]{2,1,0:T(8,128)(2,1)S(1)}, bf16[2,512,2048]{2,1,0:T(8,128)(2,1)}, u32[]{:S(2)}) %copy-start) | copy-done | bytes 4194328
  96.7 0.9 copy-done.7
  97.6 0.9 copy-done.9
  98.6 6.1 %tally.4.refs_8_ = f32[2,16,128]{2,1,0:T(8,128)S(1)} custom-call(s32[3]{0:T(128)S(1)} %pad_add_fusion.3.where_ref, bf16[128,2048]{1,0:T(8,128)(2,1)S(1)} %rotate_inputs.1.refs_0_, bf16[128,2048]{1,0:T(8,128)(2,1)S(1)} %collective-permute-done.13.refs_1_, bf16[1024,128]{1,0:T(8,128)(2,1)S(1)} %copy-done.7, bf16[1024,128]{1,0:T(8,128)(2,1)S(1)} %copy-done.9, ...), custom_call_target="tpu_custom_call" | custom-call | flops 2147483648 | bytes 9961472 | tf_op jit(solution)/shard_map/tally/pallas_call | solution.py:329
  104.7 4.9 %collective-permute-start.3 = (bf16[1024,128]{1,0:T(8,128)(2,1)S(1)}, bf16[1024,128]{1,0:T(8,128)(2,1)S(1)}, u32[]{:S(2)}, u32[]{:S(2)}) collective-permute-start(bf16[1024,128]{1,0:T(8,128)(2,1)S(1)} %copy-done.15), channel_id=1, source_target_pairs={{0,8},{1,9},{2,10},{3,11},{4,12},{5,13},{6,14},{7,15},{8,0},{9,1},... | collective-permute-start | bytes 786440 | tf_op jit(solution)/shard_map/ppermute | solution.py:352
  109.7 6.5 %collective-permute-start.4 = (bf16[1024,128]{1,0:T(8,128)(2,1)S(1)}, bf16[1024,128]{1,0:T(8,128)(2,1)S(1)}, u32[]{:S(2)}, u32[]{:S(2)}) collective-permute-start(bf16[1024,128]{1,0:T(8,128)(2,1)S(1)} %copy-done.13), channel_id=1, source_target_pairs={{0,10},{1,11},{2,8},{3,9},{4,14},{5,15},{6,12},{7,13},{8,2},{9,3},... | collective-permute-start | bytes 786440 | tf_op jit(solution)/shard_map/ppermute | solution.py:352
  116.2 6.2 %tally.5.refs_8_ = f32[2,16,128]{2,1,0:T(8,128)S(1)} custom-call(s32[3]{0:T(128)S(1)} %pad_add_fusion.2.where_ref, bf16[128,2048]{1,0:T(8,128)(2,1)S(1)} %collective-permute-done.9.refs_0_, bf16[128,2048]{1,0:T(8,128)(2,1)} %collective-permute-done.10.refs_1_, bf16[1024,128]{1,0:T(8,128)(2,1)S(1)} %collective-permute-done.11.refs_2_, ...), custom_call_target="tpu_custom_call" | custom-call | flops 2147483648 | bytes 9961472 | tf_op jit(solution)/shard_map/tally/pallas_call | solution.py:329
  122.5 6.1 %tally.6.refs_8_ = f32[2,16,128]{2,1,0:T(8,128)S(1)} custom-call(s32[3]{0:T(128)S(1)} %pad_add_fusion.1.where_ref, bf16[128,2048]{1,0:T(8,128)(2,1)S(1)} %collective-permute-done.refs_0_, bf16[128,2048]{1,0:T(8,128)(2,1)S(1)} %collective-permute-done.6.refs_1_, bf16[1024,128]{1,0:T(8,128)(2,1)S(1)} %collective-permute-done.7.refs_2_, ...), custom_call_target="tpu_custom_call" | custom-call | flops 2147483648 | bytes 9961472 | tf_op jit(solution)/shard_map/tally/pallas_call | solution.py:329
  128.6 2.0 %collective-permute-done.3.refs_2_ = bf16[1024,128]{1,0:T(8,128)(2,1)S(1)} collective-permute-done((bf16[1024,128]{1,0:T(8,128)(2,1)S(1)}, bf16[1024,128]{1,0:T(8,128)(2,1)S(1)}, u32[]{:S(2)}, u32[]{:S(2)}) %collective-permute-start.3) | collective-permute-done | bytes 262176 | tf_op jit(solution)/shard_map/ppermute | solution.py:352
  130.6 4.8 %collective-permute-done.4.refs_3_ = bf16[1024,128]{1,0:T(8,128)(2,1)S(1)} collective-permute-done((bf16[1024,128]{1,0:T(8,128)(2,1)S(1)}, bf16[1024,128]{1,0:T(8,128)(2,1)S(1)}, u32[]{:S(2)}, u32[]{:S(2)}) %collective-permute-start.4) | collective-permute-done | bytes 262176 | tf_op jit(solution)/shard_map/ppermute | solution.py:352
  135.4 6.1 %tally.7 = f32[2,16,128]{2,1,0:T(8,128)S(1)} custom-call(s32[3]{0:T(128)S(1)} %pad_add_fusion.where_ref, bf16[128,2048]{1,0:T(8,128)(2,1)S(1)} %collective-permute-done.1.refs_0_, bf16[128,2048]{1,0:T(8,128)(2,1)S(1)} %collective-permute-done.2.refs_1_, bf16[1024,128]{1,0:T(8,128)(2,1)S(1)} %collective-permute-done.3.refs_2_, ...), custom_call_target="tpu_custom_call" | custom-call | flops 2147483648 | bytes 9961472 | tf_op jit(solution)/shard_map/tally/pallas_call | solution.py:329
  141.6 0.1 reduce_sum.9
  141.7 1.1 collective-permute-done.15
  142.8 1.0 collective-permute-start.16
  143.8 2.6 %collective-permute-done.16 = f32[2,16]{1,0:T(2,128)S(1)} collective-permute-done((f32[2,16]{1,0:T(2,128)S(1)}, f32[2,16]{1,0:T(2,128)S(1)}, u32[]{:S(2)}, u32[]{:S(2)}) %collective-permute-start.16) | collective-permute-done | bytes 160 | tf_op jit(solution)/shard_map/ppermute | solution.py:352
  146.4 3.6 %collective-permute-done.17 = f32[2,16]{1,0:T(2,128)S(1)} collective-permute-done((f32[2,16]{1,0:T(2,128)S(1)}, f32[2,16]{1,0:T(2,128)S(1)}, u32[]{:S(2)}, u32[]{:S(2)}) %collective-permute-start.17) | collective-permute-done | bytes 160 | tf_op jit(solution)/shard_map/ppermute | solution.py:352
  150.0 0.7 collective-permute-start.18
  150.6 3.8 %collective-permute-done.18 = f32[2,16]{1,0:T(2,128)S(1)} collective-permute-done((f32[2,16]{1,0:T(2,128)S(1)}, f32[2,16]{1,0:T(2,128)S(1)}, u32[]{:S(2)}, u32[]{:S(2)}) %collective-permute-start.18) | collective-permute-done | bytes 160 | tf_op jit(solution)/shard_map/ppermute | solution.py:352
  154.4 0.7 dynamic-slice_reduce_fusion
  (54 shorter events, 0.6 us)
Async XLA Ops:
  0.0 2.2 %copy-start.1 = (f32[8,512,256]{2,1,0:T(8,128)S(1)}, f32[8,512,256]{2,1,0:T(8,128)}, u32[]{:S(2)}) copy-start(f32[8,512,256]{2,1,0:T(8,128)} %e_ref.3) | copy-start | bytes 12582916
  2.2 24.1 %copy-start.2 = (bf16[64,128,128]{2,1,0:T(8,128)(2,1)S(1)}, bf16[64,128,128]{2,1,0:T(8,128)(2,1)}, u32[]{:S(2)}) copy-start(bf16[64,128,128]{2,1,0:T(8,128)(2,1)} %ob_ref.1) | copy-start | bytes 6291460
  2.2 24.1 %copy-start.3 = (bf16[16,128,128]{2,1,0:T(8,128)(2,1)S(1)}, bf16[16,128,128]{2,1,0:T(8,128)(2,1)}, u32[]{:S(2)}) copy-start(bf16[16,128,128]{2,1,0:T(8,128)(2,1)} %ib_ref.1) | copy-start | bytes 1572868
  26.3 10.1 %copy-start.5 = (bf16[128,2048]{1,0:T(8,128)(2,1)S(1)}, bf16[128,2048]{1,0:T(8,128)(2,1)}, u32[]{:S(2)}) copy-start(bf16[128,2048]{1,0:T(8,128)(2,1)} %x_ref.1) | copy-start | bytes 1572868
  36.0 52.7 %copy-start.18 = (s32[16]{0:T(128)S(1)}, s32[16]{0:T(128)}, u32[]{:S(2)}) copy-start(s32[16]{0:T(128)} %param.13) | copy-start | bytes 196
  36.0 56.4 %collective-permute-start.5 = (bf16[2,512,2048]{2,1,0:T(8,128)(2,1)}, bf16[2,512,2048]{2,1,0:T(8,128)(2,1)}, u32[]{:S(2)}, u32[]{:S(2)}) collective-permute-start(bf16[2,512,2048]{2,1,0:T(8,128)(2,1)} %precondition.1.refs_4_), channel_id=1, source_target_pairs={{0,1},{1,0},{2,3},{3,2},{4,5},{5,4},{6,7},{7,6},{8,9},{9,8},{10,11... | collective-permute-start | bytes 12582920 | tf_op jit(solution)/shard_map/ppermute | solution.py:352
  36.6 20.3 %collective-permute-start = (bf16[128,2048]{1,0:T(8,128)(2,1)S(1)}, bf16[128,2048]{1,0:T(8,128)(2,1)S(1)}, u32[]{:S(2)}, u32[]{:S(2)}) collective-permute-start(bf16[128,2048]{1,0:T(8,128)(2,1)S(1)} %rotate_inputs.1.refs_0_), channel_id=1, source_target_pairs={{0,12},{1,13},{2,14},{3,15},{4,8},{5,9},{6,10},{7,11},{8,4},{9,5},... | collective-permute-start | bytes 1572872 | tf_op jit(solution)/shard_map/ppermute | solution.py:352
  36.7 1.6 %copy-start.4 = (bf16[128,8192]{1,0:T(8,128)(2,1)S(1)}, bf16[128,8192]{1,0:T(8,128)(2,1)}, u32[]{:S(2)}) copy-start(bf16[128,8192]{1,0:T(8,128)(2,1)} %g_ref.1) | copy-start | bytes 6291460
  44.1 0.7 copy-start.6
  44.8 0.7 copy-start.12
  45.5 0.7 copy-start.14
  46.2 0.7 copy-start.16
  46.9 0.7 copy-start.17
  47.6 8.4 %collective-permute-start.14 = (bf16[1024,128]{1,0:T(8,128)(2,1)S(1)}, bf16[1024,128]{1,0:T(8,128)(2,1)S(1)}, u32[]{:S(2)}, u32[]{:S(2)}) collective-permute-start(bf16[1024,128]{1,0:T(8,128)(2,1)S(1)} %get-tuple-element.20), channel_id=1, source_target_pairs={{0,2},{1,3},{2,0},{3,1},{4,6},{5,7},{6,4},{7,5},{8,10},{9,11},{10,... | collective-permute-start | bytes 786440 | tf_op jit(solution)/shard_map/ppermute | solution.py:352
  47.6 22.0 %collective-permute-start.9 = (bf16[128,2048]{1,0:T(8,128)(2,1)S(1)}, bf16[128,2048]{1,0:T(8,128)(2,1)S(1)}, u32[]{:S(2)}, u32[]{:S(2)}) collective-permute-start(bf16[128,2048]{1,0:T(8,128)(2,1)S(1)} %rotate_inputs.1.refs_0_), channel_id=1, source_target_pairs={{0,4},{1,5},{2,6},{3,7},{4,0},{5,1},{6,2},{7,3},{8,12},{9,13},{10,... | collective-permute-start | bytes 1572872 | tf_op jit(solution)/shard_map/ppermute | solution.py:352
  47.6 21.9 %collective-permute-start.11 = (bf16[1024,128]{1,0:T(8,128)(2,1)S(1)}, bf16[1024,128]{1,0:T(8,128)(2,1)S(1)}, u32[]{:S(2)}, u32[]{:S(2)}) collective-permute-start(bf16[1024,128]{1,0:T(8,128)(2,1)S(1)} %get-tuple-element.17), channel_id=1, source_target_pairs={{0,4},{1,5},{2,6},{3,7},{4,0},{5,1},{6,2},{7,3},{8,12},{9,13},{10,... | collective-permute-start | bytes 786440 | tf_op jit(solution)/shard_map/ppermute | solution.py:352
  55.9 0.7 copy-start.8
  56.6 32.2 %collective-permute-start.13 = (bf16[128,2048]{1,0:T(8,128)(2,1)S(1)}, bf16[128,2048]{1,0:T(8,128)(2,1)S(1)}, u32[]{:S(2)}, u32[]{:S(2)}) collective-permute-start(bf16[128,2048]{1,0:T(8,128)(2,1)S(1)} %rotate_inputs.1.refs_0_), channel_id=1, source_target_pairs={{0,2},{1,3},{2,0},{3,1},{4,6},{5,7},{6,4},{7,5},{8,10},{9,11},{10,... | collective-permute-start | bytes 1572872 | tf_op jit(solution)/shard_map/ppermute | solution.py:352
  56.9 33.4 %collective-permute-start.1 = (bf16[128,2048]{1,0:T(8,128)(2,1)S(1)}, bf16[128,2048]{1,0:T(8,128)(2,1)S(1)}, u32[]{:S(2)}, u32[]{:S(2)}) collective-permute-start(bf16[128,2048]{1,0:T(8,128)(2,1)S(1)} %collective-permute-done.refs_0_), channel_id=1, source_target_pairs={{0,4},{1,5},{2,6},{3,7},{4,0},{5,1},{6,2},{7,3},{8,12},{9,13},{10,... | collective-permute-start | bytes 1572872 | tf_op jit(solution)/shard_map/ppermute | solution.py:352
  69.5 15.8 %collective-permute-start.12 = (bf16[1024,128]{1,0:T(8,128)(2,1)S(1)}, bf16[1024,128]{1,0:T(8,128)(2,1)S(1)}, u32[]{:S(2)}, u32[]{:S(2)}) collective-permute-start(bf16[1024,128]{1,0:T(8,128)(2,1)S(1)} %get-tuple-element.18), channel_id=1, source_target_pairs={{0,6},{1,7},{2,4},{3,5},{4,2},{5,3},{6,0},{7,1},{8,14},{9,15},{10,... | collective-permute-start | bytes 786440 | tf_op jit(solution)/shard_map/ppermute | solution.py:352
  69.6 40.1 %collective-permute-start.10 = (bf16[128,2048]{1,0:T(8,128)(2,1)S(1)}, bf16[128,2048]{1,0:T(8,128)(2,1)}, u32[]{:S(2)}, u32[]{:S(2)}) collective-permute-start(bf16[128,2048]{1,0:T(8,128)(2,1)S(1)} %collective-permute-done.9.refs_0_), channel_id=1, source_target_pairs={{0,2},{1,3},{2,0},{3,1},{4,6},{5,7},{6,4},{7,5},{8,10},{9,11},{10,... | collective-permute-start | bytes 1572872 | tf_op jit(solution)/shard_map/ppermute | solution.py:352
  85.3 0.7 copy-start.10
  86.0 36.5 %collective-permute-start.6 = (bf16[128,2048]{1,0:T(8,128)(2,1)S(1)}, bf16[128,2048]{1,0:T(8,128)(2,1)S(1)}, u32[]{:S(2)}, u32[]{:S(2)}) collective-permute-start(bf16[128,2048]{1,0:T(8,128)(2,1)S(1)} %collective-permute-done.refs_0_), channel_id=1, source_target_pairs={{0,2},{1,3},{2,0},{3,1},{4,6},{5,7},{6,4},{7,5},{8,10},{9,11},{10,... | collective-permute-start | bytes 1572872 | tf_op jit(solution)/shard_map/ppermute | solution.py:352
  88.9 15.8 %collective-permute-start.7 = (bf16[1024,128]{1,0:T(8,128)(2,1)}, bf16[1024,128]{1,0:T(8,128)(2,1)S(1)}, u32[]{:S(2)}, u32[]{:S(2)}) collective-permute-start(bf16[1024,128]{1,0:T(8,128)(2,1)} %copy-done.17), channel_id=1, source_target_pairs={{0,12},{1,13},{2,14},{3,15},{4,8},{5,9},{6,10},{7,11},{8,4},{9,5},... | collective-permute-start | bytes 786440 | tf_op jit(solution)/shard_map/ppermute | solution.py:352
  90.3 32.2 %collective-permute-start.8 = (bf16[1024,128]{1,0:T(8,128)(2,1)}, bf16[1024,128]{1,0:T(8,128)(2,1)S(1)}, u32[]{:S(2)}, u32[]{:S(2)}) collective-permute-start(bf16[1024,128]{1,0:T(8,128)(2,1)} %copy-done.16), channel_id=1, source_target_pairs={{0,14},{1,15},{2,12},{3,13},{4,10},{5,11},{6,8},{7,9},{8,6},{9,7},... | collective-permute-start | bytes 786440 | tf_op jit(solution)/shard_map/ppermute | solution.py:352
  92.3 43.1 %collective-permute-start.2 = (bf16[128,2048]{1,0:T(8,128)(2,1)S(1)}, bf16[128,2048]{1,0:T(8,128)(2,1)S(1)}, u32[]{:S(2)}, u32[]{:S(2)}) collective-permute-start(bf16[128,2048]{1,0:T(8,128)(2,1)S(1)} %collective-permute-done.1.refs_0_), channel_id=1, source_target_pairs={{0,2},{1,3},{2,0},{3,1},{4,6},{5,7},{6,4},{7,5},{8,10},{9,11},{10,... | collective-permute-start | bytes 1572872 | tf_op jit(solution)/shard_map/ppermute | solution.py:352
  94.5 2.2 %copy-start = (bf16[2,512,2048]{2,1,0:T(8,128)(2,1)S(1)}, bf16[2,512,2048]{2,1,0:T(8,128)(2,1)}, u32[]{:S(2)}) copy-start(bf16[2,512,2048]{2,1,0:T(8,128)(2,1)} %precondition.1.refs_4_) | copy-start | bytes 12582916
  96.7 0.9 copy-start.7
  97.6 0.9 copy-start.9
  98.6 6.2 %copy-start.15 = (bf16[1024,128]{1,0:T(8,128)(2,1)S(1)}, bf16[1024,128]{1,0:T(8,128)(2,1)}, u32[]{:S(2)}) copy-start(bf16[1024,128]{1,0:T(8,128)(2,1)} %copy-done.14) | copy-start | bytes 786436
  98.6 11.1 %copy-start.13 = (bf16[1024,128]{1,0:T(8,128)(2,1)S(1)}, bf16[1024,128]{1,0:T(8,128)(2,1)}, u32[]{:S(2)}) copy-start(bf16[1024,128]{1,0:T(8,128)(2,1)} %copy-done.12) | copy-start | bytes 786436
  98.6 17.6 %copy-start.11 = (bf16[1024,128]{1,0:T(8,128)(2,1)S(1)}, bf16[1024,128]{1,0:T(8,128)(2,1)}, u32[]{:S(2)}) copy-start(bf16[1024,128]{1,0:T(8,128)(2,1)} %copy-done.10) | copy-start | bytes 786436
  104.7 25.9 %collective-permute-start.3 = (bf16[1024,128]{1,0:T(8,128)(2,1)S(1)}, bf16[1024,128]{1,0:T(8,128)(2,1)S(1)}, u32[]{:S(2)}, u32[]{:S(2)}) collective-permute-start(bf16[1024,128]{1,0:T(8,128)(2,1)S(1)} %copy-done.15), channel_id=1, source_target_pairs={{0,8},{1,9},{2,10},{3,11},{4,12},{5,13},{6,14},{7,15},{8,0},{9,1},... | collective-permute-start | bytes 786440 | tf_op jit(solution)/shard_map/ppermute | solution.py:352
  109.7 25.8 %collective-permute-start.4 = (bf16[1024,128]{1,0:T(8,128)(2,1)S(1)}, bf16[1024,128]{1,0:T(8,128)(2,1)S(1)}, u32[]{:S(2)}, u32[]{:S(2)}) collective-permute-start(bf16[1024,128]{1,0:T(8,128)(2,1)S(1)} %copy-done.13), channel_id=1, source_target_pairs={{0,10},{1,11},{2,8},{3,9},{4,14},{5,15},{6,12},{7,13},{8,2},{9,3},... | collective-permute-start | bytes 786440 | tf_op jit(solution)/shard_map/ppermute | solution.py:352
  141.7 1.1 collective-permute-start.15
  142.8 3.6 %collective-permute-start.16 = (f32[2,16]{1,0:T(2,128)S(1)}, f32[2,16]{1,0:T(2,128)S(1)}, u32[]{:S(2)}, u32[]{:S(2)}) collective-permute-start(f32[2,16]{1,0:T(2,128)S(1)} %add.21), channel_id=1, source_target_pairs={{0,2},{1,3},{2,0},{3,1},{4,6},{5,7},{6,4},{7,5},{8,10},{9,11},{10,... | collective-permute-start | bytes 392 | tf_op jit(solution)/shard_map/ppermute | solution.py:352
  146.4 3.6 %collective-permute-start.17 = (f32[2,16]{1,0:T(2,128)S(1)}, f32[2,16]{1,0:T(2,128)S(1)}, u32[]{:S(2)}, u32[]{:S(2)}) collective-permute-start(f32[2,16]{1,0:T(2,128)S(1)} %add.22), channel_id=1, source_target_pairs={{0,4},{1,5},{2,6},{3,7},{4,0},{5,1},{6,2},{7,3},{8,12},{9,13},{10,... | collective-permute-start | bytes 392 | tf_op jit(solution)/shard_map/ppermute | solution.py:352
  150.0 4.5 %collective-permute-start.18 = (f32[2,16]{1,0:T(2,128)S(1)}, f32[2,16]{1,0:T(2,128)S(1)}, u32[]{:S(2)}, u32[]{:S(2)}) collective-permute-start(f32[2,16]{1,0:T(2,128)S(1)} %add.23), channel_id=1, source_target_pairs={{0,8},{1,9},{2,10},{3,11},{4,12},{5,13},{6,14},{7,15},{8,0},{9,1},... | collective-permute-start | bytes 392 | tf_op jit(solution)/shard_map/ppermute | solution.py:352

commit v2 on v0

--- a/solution.py
+++ b/solution.py
@@ -1,9 +1,18 @@
+import functools
 import math
 
 import jax
 import jax.numpy as jnp
 from jax import lax
+from jax.experimental import pallas as pl
+from jax.experimental.pallas import tpu as pltpu
 from jax.sharding import PartitionSpec as P
+
+VMEM_LIMIT = 16 * 1024 * 1024
+COST_PRE = 10**11
+COST_K3 = 10**11
+F32 = jnp.float32
+BF16 = jnp.bfloat16
 
 
 def turn_rows(columns, basis_blocks):
@@ -55,7 +64,9 @@
     return summed
 
 
-def local(layer_inputs, output_grads, query_grads, eigenvalues, out_basis, in_basis, doc_lengths):
+def local_general(
+    layer_inputs, output_grads, query_grads, eigenvalues, out_basis, in_basis, doc_lengths
+):
     block_width = out_basis.shape[1]
     tok_count = layer_inputs.shape[0]
     tile_count = query_grads.shape[0]
@@ -90,6 +101,396 @@
     return lax.psum_scatter(partial_scores, "dp", scatter_dimension=0, tiled=True)
 
 
+def dot_tt(a, b):
+    return lax.dot_general(a, b, (((0,), (1,)), ((), ())), preferred_element_type=F32)
+
+
+def call(body, cost=1, **kw):
+    return pl.pallas_call(
+        body,
+        compiler_params=pltpu.CompilerParams(vmem_limit_bytes=VMEM_LIMIT),
+        cost_estimate=pl.CostEstimate(flops=cost, bytes_accessed=1, transcendentals=0),
+        **kw,
+    )
+
+
+def in_hbm(value):
+    return pltpu.with_memory_space_constraint(value, pltpu.HBM)
+
+
+def rotate_inputs(layer_inputs, in_basis):
+    tokens, features = layer_inputs.shape
+    count, width, _ = in_basis.shape
+
+    def body(x_hbm, b_hbm, o_ref, x_all, b_all, sems):
+        copies = [
+            pltpu.make_async_copy(x_hbm, x_all, sems.at[0]),
+            pltpu.make_async_copy(b_hbm, b_all, sems.at[1]),
+        ]
+        for copy in copies:
+            copy.start()
+        for copy in copies:
+            copy.wait()
+        for n in range(count):
+            span = slice(n * width, (n + 1) * width)
+            turned = jnp.dot(x_all[:, span], b_all[n], preferred_element_type=F32)
+            o_ref[span, :] = turned.astype(BF16).T
+
+    hbm = pl.BlockSpec(memory_space=pl.ANY)
+    return call(
+        body,
+        in_specs=[hbm, hbm],
+        out_specs=pl.BlockSpec(memory_space=pltpu.VMEM),
+        out_shape=jax.ShapeDtypeStruct((features, tokens), BF16),
+        scratch_shapes=[
+            pltpu.VMEM((tokens, features), BF16),
+            pltpu.VMEM((count, width, width), BF16),
+            pltpu.SemaphoreType.DMA((2,)),
+        ],
+        name="rotate_inputs",
+    )(in_hbm(layer_inputs), in_hbm(in_basis))
+
+
+def rotate_grads(output_grads, out_basis, chip, chips, layouts, sources=(), after=(), cost=1):
+    tokens, units = output_grads.shape
+    width = out_basis.shape[1]
+    part = units // chips
+    per = part // width
+    offsets = [k for layout in layouts for k in layout if isinstance(k, int)]
+    count = len(offsets)
+    heights = [sum(part if isinstance(k, int) else k[2] for k in layout) for layout in layouts]
+    extra = list(sources) + list(after)
+
+    def body(chip_ref, g_hbm, b_hbm, *refs):
+        o_refs = refs[len(extra) : len(extra) + len(layouts)]
+        g_all, b_all, g_sems, b_sems = refs[len(extra) + len(layouts) :]
+        copies = []
+        for n, k in enumerate(offsets):
+            place = chip_ref[0] ^ k
+            cols = pl.ds(pl.multiple_of(place * part, part), part)
+            blocks = pl.ds(place * per, per)
+            copies.append(
+                (
+                    pltpu.make_async_copy(g_hbm.at[:, cols], g_all.at[n], g_sems.at[n]),
+                    pltpu.make_async_copy(b_hbm.at[blocks], b_all.at[n], b_sems.at[n]),
+                )
+            )
+        for pair in copies:
+            for copy in pair:
+                copy.start()
+        n = 0
+        for o_ref, layout in zip(o_refs, layouts):
+            top = 0
+            for k in layout:
+                if not isinstance(k, int):
+                    source, first, rows = k
+                    o_ref[top : top + rows, :] = refs[source][first : first + rows, :]
+                    top += rows
+                    continue
+                for copy in copies[n]:
+                    copy.wait()
+                for i in range(per):
+                    span = slice(i * width, (i + 1) * width)
+                    turned = jnp.dot(g_all[n, :, span], b_all[n, i], preferred_element_type=F32)
+                    o_ref[top + i * width : top + (i + 1) * width, :] = turned.astype(BF16).T
+                top += part
+                n += 1
+
+    hbm = pl.BlockSpec(memory_space=pl.ANY)
+    vmem = pl.BlockSpec(memory_space=pltpu.VMEM)
+    return call(
+        body,
+        in_specs=[pl.BlockSpec(memory_space=pltpu.SMEM), hbm, hbm]
+        + [vmem] * len(sources)
+        + [hbm] * len(after),
+        out_specs=[vmem] * len(layouts),
+        out_shape=[jax.ShapeDtypeStruct((h, tokens), BF16) for h in heights],
+        scratch_shapes=[
+            pltpu.VMEM((count, tokens, part), BF16),
+            pltpu.VMEM((count, per, width, width), BF16),
+            pltpu.SemaphoreType.DMA((count,)),
+            pltpu.SemaphoreType.DMA((count,)),
+        ],
+        name="rotate_grads",
+        cost=cost,
+    )(chip[None], output_grads, out_basis, *extra)
+
+
+def sum_eigenvalues(eigenvalues):
+    tiles, rows, cols = eigenvalues.shape
+
+    def body(e_ref, o_ref):
+        @pl.when(pl.program_id(0) == 0)
+        def _():
+            o_ref[...] = jnp.zeros_like(o_ref)
+
+        part = jnp.sum(e_ref[0].reshape(rows // 8, 8, cols), axis=0)
+        total = part[:, :128]
+        for n in range(1, cols // 128):
+            total = total + part[:, n * 128 : (n + 1) * 128]
+        o_ref[...] += total
+
+    return call(
+        body,
+        grid=(tiles,),
+        in_specs=[pl.BlockSpec((1, rows, cols), lambda b: (b, 0, 0))],
+        out_specs=pl.BlockSpec((8, 128), lambda b: (0, 0)),
+        out_shape=jax.ShapeDtypeStruct((8, 128), F32),
+        name="sum_eigenvalues",
+    )(eigenvalues)
+
+
+def add_after(a, b, *after):
+    def body(a_ref, b_ref, *refs):
+        refs[-1][...] = a_ref[...] + b_ref[...]
+
+    vmem = pl.BlockSpec(memory_space=pltpu.VMEM)
+    return call(
+        body,
+        in_specs=[vmem, vmem] + [pl.BlockSpec(memory_space=pl.ANY)] * len(after),
+        out_specs=vmem,
+        out_shape=jax.ShapeDtypeStruct(a.shape, a.dtype),
+        name="add_after",
+    )(a, b, *after)
+
+
+def block_diagonal(blocks):
+    count, width = len(blocks), blocks[0].shape[0]
+    zero = jnp.zeros((width, width), blocks[0].dtype)
+    rows = [
+        jnp.concatenate([blocks[i] if i == j else zero for j in range(count)], axis=1)
+        for i in range(count)
+    ]
+    return jnp.concatenate(rows, axis=0)
+
+
+def precondition_rows(query_grads, eigenvalues, sums, out_basis, in_basis, me, entries, after):
+    tiles, queries, rows, cols = query_grads.shape
+    width = in_basis.shape[1]
+    features = in_basis.shape[0] * width
+    in_tiles = features // cols
+    groups = tiles // in_tiles
+    n_out, n_in = rows // width, cols // width
+    pair = 2 if n_out % 2 == 0 else 1
+    span = pair * width
+
+    def body(me_ref, q_ref, e_ref, s_ref, ob_ref, ib_ref, *refs):
+        o_ref, turn_ref = refs[len(after) :]
+
+        @pl.when(pl.program_id(0) % in_tiles == 0)
+        def _():
+            for n in range(n_out // pair):
+                turn_ref[n] = block_diagonal([ob_ref[n * pair + k].T for k in range(pair)])
+
+        damping = 0.1 * (jnp.sum(s_ref[...], keepdims=True) / entries)
+        scale = 1.0 / (e_ref[0] + damping)
+        half = jnp.dot(
+            q_ref[0].reshape(queries * rows, cols),
+            block_diagonal([ib_ref[n] for n in range(n_in)]),
+            preferred_element_type=F32,
+        ).astype(BF16)
+        for q in range(queries):
+            for n in range(n_out // pair):
+                start = n * span
+                turned = jnp.dot(
+                    turn_ref[n],
+                    half[q * rows + start : q * rows + start + span],
+                    preferred_element_type=F32,
+                )
+                o_ref[q, start : start + span, :] = (turned * scale[start : start + span]).astype(
+                    BF16
+                )
+
+    grid_spec = pltpu.PrefetchScalarGridSpec(
+        num_scalar_prefetch=1,
+        grid=(tiles,),
+        in_specs=[
+            pl.BlockSpec((1, queries, rows, cols), lambda b, m: (b, 0, 0, 0)),
+            pl.BlockSpec((1, rows, cols), lambda b, m: (b, 0, 0)),
+            pl.BlockSpec(sums.shape, lambda b, m: (0, 0)),
+            pl.BlockSpec((n_out, width, width), lambda b, m: (m[0] * groups + b // in_tiles, 0, 0)),
+            pl.BlockSpec((n_in, width, width), lambda b, m: (b % in_tiles, 0, 0)),
+        ]
+        + [pl.BlockSpec(memory_space=pl.ANY)] * len(after),
+        out_specs=pl.BlockSpec(
+            (queries, rows, cols), lambda b, m: (0, b // in_tiles, b % in_tiles)
+        ),
+        scratch_shapes=[pltpu.VMEM((n_out // pair, span, span), BF16)],
+    )
+    return call(
+        body,
+        grid_spec=grid_spec,
+        out_shape=jax.ShapeDtypeStruct((queries, groups * rows, features), BF16),
+        name="precondition",
+        cost=COST_PRE,
+    )(me[None], query_grads, eigenvalues, sums, out_basis, in_basis, *after)
+
+
+def join_rows(own, sibling, core, after):
+    def body(core_ref, own_ref, sib_ref, *refs):
+        o_ref, sems = refs[len(after) :]
+        copies = [
+            pltpu.make_async_copy(own_ref, o_ref.at[core_ref[0]], sems.at[0]),
+            pltpu.make_async_copy(sib_ref, o_ref.at[1 - core_ref[0]], sems.at[1]),
+        ]
+        for copy in copies:
+            copy.start()
+        for copy in copies:
+            copy.wait()
+
+    hbm = pl.BlockSpec(memory_space=pl.ANY)
+    return call(
+        body,
+        in_specs=[pl.BlockSpec(memory_space=pltpu.SMEM), hbm, hbm] + [hbm] * len(after),
+        out_specs=pl.BlockSpec(memory_space=pltpu.VMEM),
+        out_shape=jax.ShapeDtypeStruct((2,) + own.shape, own.dtype),
+        scratch_shapes=[pltpu.SemaphoreType.DMA((2,))],
+        name="join_rows",
+    )(core[None], own, sibling, *after)
+
+
+def tally(where, pieces, both, starts, ends, running):
+    count = len(pieces)
+    cores, queries, rows, features = both.shape
+    tokens = starts.shape[1]
+    block = math.gcd(rows, 512)
+    docs = starts.shape[0]
+    arrays = []
+    places = []
+    for piece in pieces:
+        for array, _ in piece:
+            if not any(array is other for other in arrays):
+                arrays.append(array)
+        places.append([next(i for i, o in enumerate(arrays) if o is a) for a, _ in piece])
+
+    def body(where_ref, *refs):
+        p_ref, st_ref, en_ref, run_ref, o_ref, x_all = refs[len(arrays) :]
+        for n in range(count):
+            first = pieces[n][0][1]
+            x_all[:, n * tokens : (n + 1) * tokens] = refs[places[n][0]][first : first + features, :]
+        scores = [[jnp.zeros((1, tokens), F32)] * queries for _ in range(count)]
+        for c in range(cores):
+            for q in range(queries):
+                for r in range(0, rows, block):
+                    turned = jnp.dot(
+                        p_ref[c, q, r : r + block, :], x_all[...], preferred_element_type=F32
+                    )
+                    for n in range(count):
+                        first = pieces[n][1][1] + c * rows + r
+                        scores[n][q] = scores[n][q] + jnp.sum(
+                            turned[:, n * tokens : (n + 1) * tokens]
+                            * refs[places[n][1]][first : first + block, :].astype(F32),
+                            axis=0,
+                            keepdims=True,
+                        )
+        for q in range(queries):
+            total = run_ref[q]
+            for n in range(count):
+                spot = where_ref[n] * tokens + lax.broadcasted_iota(jnp.int32, (docs, tokens), 1)
+                inside = (spot >= st_ref[...]) & (spot < en_ref[...])
+                total = total + jnp.where(inside, scores[n][q], 0.0)
+            o_ref[q] = total
+
+    vmem = pl.BlockSpec(memory_space=pltpu.VMEM)
+    return call(
+        body,
+        in_specs=[pl.BlockSpec(memory_space=pltpu.SMEM)] + [vmem] * (len(arrays) + 4),
+        out_specs=vmem,
+        out_shape=jax.ShapeDtypeStruct(running.shape, F32),
+        scratch_shapes=[pltpu.VMEM((features, count * tokens), BF16)],
+        name="tally",
+    )(where, *arrays, both, starts, ends, running)
+
+
+def local_rows(
+    depth, layer_inputs, output_grads, query_grads, eigenvalues, out_basis, in_basis, doc_lengths
+):
+    devices = 4 * depth
+    chips = 2 * depth
+    tokens = layer_inputs.shape[0]
+    queries = query_grads.shape[1]
+    entries = output_grads.shape[1] * layer_inputs.shape[1]
+    me = lax.axis_index("dp")
+    chip = me // 2
+    core = me % 2
+
+    def swap(value, offset):
+        return lax.ppermute(value, "dp", [(i, i ^ offset) for i in range(devices)])
+
+    features = layer_inputs.shape[1]
+    part = output_grads.shape[1] // chips
+    x = rotate_inputs(layer_inputs, in_basis)
+    rotate = functools.partial(rotate_grads, in_hbm(output_grads), in_hbm(out_basis), chip, chips)
+    side, near_side_g, g_own = rotate([[(0, 0, features), 1], [3], [0]], [x])
+    far_x = swap(x, 12)
+    near_x = swap(x, 4)
+    side = swap(side, 2)
+    near_side_g = swap(near_side_g, 6)
+    first = [far_x, near_x, side, near_side_g]
+
+    sums = sum_eigenvalues(eigenvalues)
+    for offset in (1, 2, 4, 8):
+        sums = sums + swap(sums, offset)
+
+    (middle,) = rotate([[4, 5]], [], first)
+    middle = swap(middle, 8)
+    middle_x = swap(far_x, 4)
+    near_x_side = swap(near_x, 2)
+    far_x_side = swap(far_x, 2)
+    second = [middle, middle_x, near_x_side, far_x_side]
+
+    own = precondition_rows(
+        query_grads, eigenvalues, sums, out_basis, in_basis, me, entries, first
+    )
+    both = join_rows(own, swap(own, 1), core, second)
+
+    middle_side, g_far, g_far_side, near_g = rotate(
+        [[(0, 0, features), (1, part, part)], [6], [7], [2]],
+        [middle_x, middle],
+        second + [own],
+        cost=COST_K3,
+    )
+    middle_side = swap(middle_side, 2)
+    g_far = swap(g_far, 12)
+    g_far_side = swap(g_far_side, 14)
+    near_g = swap(near_g, 4)
+
+    doc_ends = jnp.cumsum(doc_lengths)
+    doc_starts = doc_ends - doc_lengths
+    docs = doc_lengths.shape[0]
+    starts = jnp.broadcast_to(doc_starts[:, None], (docs, tokens))
+    ends = jnp.broadcast_to(doc_ends[:, None], (docs, tokens))
+    running = jnp.zeros((queries, docs, tokens), F32)
+    pieces = {
+        0: ((x, 0), (g_own, 0)),
+        1: ((side, 0), (side, features)),
+        2: ((near_x, 0), (near_g, 0)),
+        3: ((near_x_side, 0), (near_side_g, 0)),
+        4: ((middle_x, 0), (middle, 0)),
+        5: ((middle_side, 0), (middle_side, features)),
+        6: ((far_x, 0), (g_far, 0)),
+        7: ((far_x_side, 0), (g_far_side, 0)),
+    }
+    for some in ((0, 1, 3, 4), (2, 6), (5, 7)):
+        where = jnp.stack([me ^ (2 * k) for k in some]).astype(jnp.int32)
+        running = tally(where, [pieces[k] for k in some], both, starts, ends, running)
+    shares = jnp.sum(running, axis=2)
+    for offset in (1, 2, 4, 8):
+        shares = shares + swap(shares, offset)
+    each = docs // devices
+    mine = lax.dynamic_slice_in_dim(shares, me * each, each, 1)
+    return mine.T
+
+
+def local(layer_inputs, output_grads, query_grads, eigenvalues, out_basis, in_basis, doc_lengths, devices):
+    args = (layer_inputs, output_grads, query_grads, eigenvalues, out_basis, in_basis, doc_lengths)
+    in_tiles = layer_inputs.shape[1] // query_grads.shape[3]
+    tile_count = query_grads.shape[0]
+    if devices == 16 and tile_count % in_tiles == 0:
+        return local_rows(devices // 4, *args)
+    return local_general(*args)
+
+
 def solution(mesh):
     in_specs = (
         P(("groups", "dp"), None),
@@ -101,4 +502,5 @@
         P("groups"),
     )
     out_specs = P(("groups", "dp"), None)
-    return jax.shard_map(local, mesh=mesh, in_specs=in_specs, out_specs=out_specs, check_vma=False)
+    body = functools.partial(local, devices=mesh.shape["dp"])
+    return jax.shard_map(body, mesh=mesh, in_specs=in_specs, out_specs=out_specs, check_vma=False)

time: 885 us -> 116 us (0.13)
  blocking collectives: 403 us -> 0 us
  local copies, waits for them, and re-layouts: 195 us -> 3.09 us
  waiting for transfers between devices: 142 us -> 51.9 us
  matrix products: 51.9 us -> 0 us
  other arithmetic: 42.3 us -> 0.5 us
  Pallas kernels: 0 us -> 31.5 us
  starting transfers between devices: 44 us -> 28.9 us
    psum x1 -> x0, blocking collectives: 320 us -> none  [local(): eigen_sum = lax.psum(jnp.sum(eigenvalues), 'dp')]
    all_to_all x2 -> x0, waiting for transfers between devices: 142 us -> none  [the longest x1 142 us: local(): lax.all_to_all(inputs_tiles, 'dp', split_axis=0, concat_axis=1, tiled=True)]
    mul x4 -> x0, local copies, waits for them, and re-layouts: 121 us -> none  [one_piece(): projected * grads_piece[:, :, None, :].astype(jnp.float32)]
    unnamed x1 -> x0, blocking collectives: 82.7 us -> none
    dot_general x8 -> x0, matrix products: 51.9 us -> none  [the longest x2 34.7 us: one_piece(): jnp.einsum('bti,bpi->btp', inputs_piece, flat_pre, preferred_element_type...]
    ppermute x0 -> x21, waiting for transfers between devices: none -> 51.9 us  [swap(): return lax.ppermute(value, 'dp', [(i, i ^ offset) for i in range(devices)])]
    all_to_all x2 -> x0, starting transfers between devices: 44 us -> none  [the longest x1 36.5 us: local(): lax.all_to_all(grads_tiles, 'dp', split_axis=0, concat_axis=1, tiled=True)]
    pallas_call x0 -> x10, Pallas kernels: none -> 31.5 us  [the longest x3 12.5 us: tally(): call(body, in_specs=[pl.BlockSpec(memory_space=pltpu.SMEM)] + [vmem] * (l...]
  transfers between devices with their start and end apart: 2 -> 21, of which waited for: 1 -> 13; matrix products, arithmetic and copies ran while one was open for 7% -> 1% of each run, Pallas kernels for 0% -> 21%
where the time goes in v2:
time: 116 us
  waiting for transfers between devices  51.9 us (45%)
  Pallas kernels  31.5 us (27%)
  starting transfers between devices  28.9 us (25%)
  local copies, waits for them, and re-layouts  3.09 us (3%)
    ppermute x21, waiting for transfers between devices, swap(): return lax.ppermute(value, 'dp', [(i, i ^ offset) for i in range(devices)])  51.9 us
    ppermute x21, starting transfers between devices, swap(): return lax.ppermute(value, 'dp', [(i, i ^ offset) for i in range(devices)])  28.9 us
    pallas_call x3, Pallas kernels, tally(): call(body, in_specs=[pl.BlockSpec(memory_space=pltpu.SMEM)] + [vmem] * (l...  12.5 us
    pallas_call x1, Pallas kernels, precondition_rows(): call(body, grid_spec=grid_spec, out_shape=jax.ShapeDtypeStruct((queries,...  6.63 us
    pallas_call x3, Pallas kernels, rotate_grads(): call(body, in_specs=[pl.BlockSpec(memory_space=pltpu.SMEM), hbm, hbm] + [...  6.47 us
    pallas_call x1, Pallas kernels, join_rows(): call(body, in_specs=[pl.BlockSpec(memory_space=pltpu.SMEM), hbm, hbm] + [...  3.56 us
  transfers between devices with their start and end apart: 21, of which 13 were waited for; matrix products, arithmetic and copies ran while one was open for 1% of the time, Pallas kernels for 21%

profile of v2, /device:TPU:0, one launch (start us, length us, event | category | flops | bytes accessed | tf_op | source)
XLA Modules:
  0.0 116.1 jit_solution(12884495956135600927)
XLA Ops:
  0.0 1.7 %rotate_inputs.1.refs_0_ = bf16[2048,128]{1,0:T(8,128)(2,1)S(1)} custom-call(bf16[128,2048]{1,0:T(8,128)(2,1)} %x_hbm.1, bf16[16,128,128]{2,1,0:T(8,128)(2,1)} %ib_ref.1), custom_call_target="tpu_custom_call" | custom-call | flops 1 | bytes 1 | tf_op jit(solution)/shard_map/rotate_inputs/pallas_call | solution.py:140
  1.7 2.1 %rotate_grads.3 = (bf16[3072,128]{1,0:T(8,128)(2,1)S(1)}, bf16[1024,128]{1,0:T(8,128)(2,1)S(1)}, bf16[1024,128]{1,0:T(8,128)(2,1)S(1)}) custom-call(s32[1]{0:T(128)} %bitcast.2.chip_ref, bf16[128,8192]{1,0:T(8,128)(2,1)} %g_hbm.5, bf16[64,128,128]{2,1,0:T(8,128)(2,1)} %b_hbm.7, bf16[2048,128]{1,0:T(8,128)(2,1)S(1)} %rotate_inputs.1.refs_0_), custom_call_target="tpu_custom_call" | custom-call | flops 1 | bytes 1 | tf_op jit(solution)/shard_map/rotate_grads/pallas_call | solution.py:201
  3.9 3.0 %collective-permute-start.3 = (bf16[3072,128]{1,0:T(8,128)(2,1)S(1)}, bf16[3072,128]{1,0:T(8,128)(2,1)S(1)}, u32[]{:S(2)}, u32[]{:S(2)}) collective-permute-start(bf16[3072,128]{1,0:T(8,128)(2,1)S(1)} %get-tuple-element.12), channel_id=1, source_target_pairs={{0,2},{1,3},{2,0},{3,1},{4,6},{5,7},{6,4},{7,5},{8,10},{9,11},{10,... | collective-permute-start | bytes 2359304 | tf_op jit(solution)/shard_map/ppermute | solution.py:418
  6.9 3.6 %collective-permute-start = (bf16[2048,128]{1,0:T(8,128)(2,1)S(1)}, bf16[2048,128]{1,0:T(8,128)(2,1)S(1)}, u32[]{:S(2)}, u32[]{:S(2)}) collective-permute-start(bf16[2048,128]{1,0:T(8,128)(2,1)S(1)} %rotate_inputs.1.refs_0_), channel_id=1, source_target_pairs={{0,12},{1,13},{2,14},{3,15},{4,8},{5,9},{6,10},{7,11},{8,4},{9,5},... | collective-permute-start | bytes 1572872 | tf_op jit(solution)/shard_map/ppermute | solution.py:418
  10.5 2.0 %collective-permute-start.4 = (bf16[1024,128]{1,0:T(8,128)(2,1)S(1)}, bf16[1024,128]{1,0:T(8,128)(2,1)S(1)}, u32[]{:S(2)}, u32[]{:S(2)}) collective-permute-start(bf16[1024,128]{1,0:T(8,128)(2,1)S(1)} %get-tuple-element.13), channel_id=1, source_target_pairs={{0,6},{1,7},{2,4},{3,5},{4,2},{5,3},{6,0},{7,1},{8,14},{9,15},{10,... | collective-permute-start | bytes 786440 | tf_op jit(solution)/shard_map/ppermute | solution.py:418
  12.5 0.7 sum_eigenvalues.1
  13.3 1.2 collective-permute-done.8
  14.4 1.5 %collective-permute-start.9 = (f32[8,128]{1,0:T(8,128)S(1)}, f32[8,128]{1,0:T(8,128)S(1)}, u32[]{:S(2)}, u32[]{:S(2)}) collective-permute-start(f32[8,128]{1,0:T(8,128)S(1)} %add.32), channel_id=1, source_target_pairs={{0,2},{1,3},{2,0},{3,1},{4,6},{5,7},{6,4},{7,5},{8,10},{9,11},{10,... | collective-permute-start | bytes 12296 | tf_op jit(solution)/shard_map/ppermute | solution.py:418
  15.9 8.6 %collective-permute-done.9 = f32[8,128]{1,0:T(8,128)S(1)} collective-permute-done((f32[8,128]{1,0:T(8,128)S(1)}, f32[8,128]{1,0:T(8,128)S(1)}, u32[]{:S(2)}, u32[]{:S(2)}) %collective-permute-start.9) | collective-permute-done | bytes 4128 | tf_op jit(solution)/shard_map/ppermute | solution.py:418
  24.5 1.8 %collective-permute-start.10 = (f32[8,128]{1,0:T(8,128)S(1)}, f32[8,128]{1,0:T(8,128)S(1)}, u32[]{:S(2)}, u32[]{:S(2)}) collective-permute-start(f32[8,128]{1,0:T(8,128)S(1)} %add.33), channel_id=1, source_target_pairs={{0,4},{1,5},{2,6},{3,7},{4,0},{5,1},{6,2},{7,3},{8,12},{9,13},{10,... | collective-permute-start | bytes 12296 | tf_op jit(solution)/shard_map/ppermute | solution.py:418
  26.3 12.9 %collective-permute-done.10 = f32[8,128]{1,0:T(8,128)S(1)} collective-permute-done((f32[8,128]{1,0:T(8,128)S(1)}, f32[8,128]{1,0:T(8,128)S(1)}, u32[]{:S(2)}, u32[]{:S(2)}) %collective-permute-start.10) | collective-permute-done | bytes 4128 | tf_op jit(solution)/shard_map/ppermute | solution.py:418
  39.2 0.6 collective-permute-start.11
  39.7 4.0 %collective-permute-done.11 = f32[8,128]{1,0:T(8,128)S(1)} collective-permute-done((f32[8,128]{1,0:T(8,128)S(1)}, f32[8,128]{1,0:T(8,128)S(1)}, u32[]{:S(2)}, u32[]{:S(2)}) %collective-permute-start.11) | collective-permute-done | bytes 4128 | tf_op jit(solution)/shard_map/ppermute | solution.py:418
  43.7 1.7 %collective-permute-start.1 = (bf16[2048,128]{1,0:T(8,128)(2,1)S(1)}, bf16[2048,128]{1,0:T(8,128)(2,1)S(1)}, u32[]{:S(2)}, u32[]{:S(2)}) collective-permute-start(bf16[2048,128]{1,0:T(8,128)(2,1)S(1)} %collective-permute-done.refs_0_.refs_2_), channel_id=1, source_target_pairs={{0,4},{1,5},{2,6},{3,7},{4,0},{5,1},{6,2},{7,3},{8,12},{9,13},{10,... | collective-permute-start | bytes 1572872 | tf_op jit(solution)/shard_map/ppermute | solution.py:418
  45.4 0.5 collective-permute-start.7
  45.9 1.5 %collective-permute-start.6 = (bf16[2048,128]{1,0:T(8,128)(2,1)S(1)}, bf16[2048,128]{1,0:T(8,128)(2,1)S(1)}, u32[]{:S(2)}, u32[]{:S(2)}) collective-permute-start(bf16[2048,128]{1,0:T(8,128)(2,1)S(1)} %collective-permute-done.2.refs_1_.refs_0_), channel_id=1, source_target_pairs={{0,2},{1,3},{2,0},{3,1},{4,6},{5,7},{6,4},{7,5},{8,10},{9,11},{10,... | collective-permute-start | bytes 1572872 | tf_op jit(solution)/shard_map/ppermute | solution.py:418
  47.4 1.7 %rotate_grads.4 = bf16[2048,128]{1,0:T(8,128)(2,1)S(1)} custom-call(s32[1]{0:T(128)} %bitcast.2.chip_ref, bf16[128,8192]{1,0:T(8,128)(2,1)} %g_hbm.5, bf16[64,128,128]{2,1,0:T(8,128)(2,1)} %b_hbm.7, bf16[2048,128]{1,0:T(8,128)(2,1)S(1)} %collective-permute-done.refs_0_.refs_2_, bf16[2048,128]{1,0:T(8,128)(2,1)S(1)} %collective-permute-done.2.refs_1_.refs_0_, ...), custom_call_target="tpu_custom_call" | custom-call | flops 1 | bytes 1 | tf_op jit(solution)/shard_map/rotate_grads/pallas_call | solution.py:201
  49.2 0.7 collective-permute-start.5
  49.9 6.6 %precondition.1.refs_6_.own_ref = bf16[2,512,2048]{2,1,0:T(8,128)(2,1)} custom-call(s32[1]{0:T(128)} %bitcast.3.me_ref, bf16[8,2,512,256]{3,2,1,0:T(8,128)(2,1)S(1)} %copy-done.11, f32[8,512,256]{2,1,0:T(8,128)S(1)} %copy-done.3, f32[8,128]{1,0:T(8,128)S(1)} %add.35.s_ref, bf16[64,128,128]{2,1,0:T(8,128)(2,1)S(1)} %copy-done, ...), custom_call_target="tpu_custom_call" | custom-call | flops 99999997952 | bytes 1 | tf_op jit(solution)/shard_map/precondition/pallas_call | solution.py:320
  56.6 6.6 %collective-permute-done.1.refs_0_.refs_3_.refs_1_.refs_5_ = bf16[2048,128]{1,0:T(8,128)(2,1)S(1)} collective-permute-done((bf16[2048,128]{1,0:T(8,128)(2,1)S(1)}, bf16[2048,128]{1,0:T(8,128)(2,1)S(1)}, u32[]{:S(2)}, u32[]{:S(2)}) %collective-permute-start.1) | collective-permute-done | bytes 524320 | tf_op jit(solution)/shard_map/ppermute | solution.py:418
  63.2 4.6 %collective-permute-done.6.refs_4_.refs_2_.refs_3_ = bf16[2048,128]{1,0:T(8,128)(2,1)S(1)} collective-permute-done((bf16[2048,128]{1,0:T(8,128)(2,1)S(1)}, bf16[2048,128]{1,0:T(8,128)(2,1)S(1)}, u32[]{:S(2)}, u32[]{:S(2)}) %collective-permute-start.6) | collective-permute-done | bytes 524320 | tf_op jit(solution)/shard_map/ppermute | solution.py:418
  67.7 4.2 %collective-permute-done.5.refs_1_.refs_2_.refs_0_.refs_6_ = bf16[2048,128]{1,0:T(8,128)(2,1)S(1)} collective-permute-done((bf16[2048,128]{1,0:T(8,128)(2,1)S(1)}, bf16[2048,128]{1,0:T(8,128)(2,1)S(1)}, u32[]{:S(2)}, u32[]{:S(2)}) %collective-permute-start.5) | collective-permute-done | bytes 524320 | tf_op jit(solution)/shard_map/ppermute | solution.py:418
  72.0 2.6 %rotate_grads.5 = (bf16[3072,128]{1,0:T(8,128)(2,1)}, bf16[1024,128]{1,0:T(8,128)(2,1)S(1)}, bf16[1024,128]{1,0:T(8,128)(2,1)S(1)}, bf16[1024,128]{1,0:T(8,128)(2,1)S(1)}) custom-call(s32[1]{0:T(128)} %bitcast.2.chip_ref, bf16[128,8192]{1,0:T(8,128)(2,1)} %g_hbm.5, bf16[64,128,128]{2,1,0:T(8,128)(2,1)} %b_hbm.7, ...), custom_call_target="tpu_custom_call" | custom-call | flops 99999997952 | bytes 1 | tf_op jit(solution)/shard_map/rotate_grads/pallas_call | solution.py:201
  74.6 0.7 copy-done.12
  75.3 0.7 copy-done.13
  76.0 0.7 copy-done.14
  76.7 0.5 collective-permute-start.12
  77.2 1.4 %collective-permute-start.16 = (bf16[1024,128]{1,0:T(8,128)(2,1)}, bf16[1024,128]{1,0:T(8,128)(2,1)}, u32[]{:S(2)}, u32[]{:S(2)}) collective-permute-start(bf16[1024,128]{1,0:T(8,128)(2,1)} %copy-done.13), channel_id=1, source_target_pairs={{0,12},{1,13},{2,14},{3,15},{4,8},{5,9},{6,10},{7,11},{8,4},{9,5},... | collective-permute-start | bytes 786440 | tf_op jit(solution)/shard_map/ppermute | solution.py:418
  78.6 3.4 %collective-permute-start.13 = (bf16[1024,128]{1,0:T(8,128)(2,1)}, bf16[1024,128]{1,0:T(8,128)(2,1)}, u32[]{:S(2)}, u32[]{:S(2)}) collective-permute-start(bf16[1024,128]{1,0:T(8,128)(2,1)} %copy-done.12), channel_id=1, source_target_pairs={{0,14},{1,15},{2,12},{3,13},{4,10},{5,11},{6,8},{7,9},{8,6},{9,7},... | collective-permute-start | bytes 786440 | tf_op jit(solution)/shard_map/ppermute | solution.py:418
  82.1 0.1 copy.11
  82.2 0.1 reduce
  82.3 0.1 pad_add_fusion.where_ref
  82.4 0.1 pad_add_fusion.2.where_ref
  82.5 3.6 %join_rows.1.refs_7_.refs_4_.refs_3_ = bf16[2,2,512,2048]{3,2,1,0:T(8,128)(2,1)S(1)} custom-call(s32[1]{0:T(128)} %bitcast.4.core_ref, bf16[2,512,2048]{2,1,0:T(8,128)(2,1)} %precondition.1.refs_6_.own_ref, bf16[2,512,2048]{2,1,0:T(8,128)(2,1)} %collective-permute-done.14.sib_ref, ...), custom_call_target="tpu_custom_call" | custom-call | flops 1 | bytes 1 | tf_op jit(solution)/shard_map/join_rows/pallas_call | solution.py:342
  86.2 5.3 %tally.3.refs_7_ = f32[2,16,128]{2,1,0:T(8,128)S(1)} custom-call(s32[4]{0:T(128)S(1)} %pad_add_fusion.2.where_ref, bf16[2048,128]{1,0:T(8,128)(2,1)S(1)} %copy-done.2, bf16[1024,128]{1,0:T(8,128)(2,1)S(1)} %copy-done.10, bf16[3072,128]{1,0:T(8,128)(2,1)S(1)} %collective-permute-done.3.refs_2_, ...), custom_call_target="tpu_custom_call" | custom-call | flops 1 | bytes 1 | tf_op jit(solution)/shard_map/tally/pallas_call | solution.py:395
  91.5 2.0 %collective-permute-done.15.refs_1_ = bf16[1024,128]{1,0:T(8,128)(2,1)} collective-permute-done((bf16[1024,128]{1,0:T(8,128)(2,1)}, bf16[1024,128]{1,0:T(8,128)(2,1)}, u32[]{:S(2)}, u32[]{:S(2)}) %collective-permute-start.15) | collective-permute-done | bytes 262176 | tf_op jit(solution)/shard_map/ppermute | solution.py:418
  93.6 3.5 %tally.4.refs_6_ = f32[2,16,128]{2,1,0:T(8,128)S(1)} custom-call(s32[2]{0:T(128)S(1)} %pad_add_fusion.1.where_ref, bf16[2048,128]{1,0:T(8,128)(2,1)S(1)} %copy-done.5, bf16[1024,128]{1,0:T(8,128)(2,1)} %collective-permute-done.15.refs_1_, bf16[2048,128]{1,0:T(8,128)(2,1)S(1)} %collective-permute-done.refs_0_.refs_2_, ...), custom_call_target="tpu_custom_call" | custom-call | flops 1 | bytes 1 | tf_op jit(solution)/shard_map/tally/pallas_call | solution.py:395
  97.1 0.8 collective-permute-done.12.refs_0_
  97.9 3.7 %tally.5 = f32[2,16,128]{2,1,0:T(8,128)S(1)} custom-call(s32[2]{0:T(128)S(1)} %pad_add_fusion.where_ref, bf16[3072,128]{1,0:T(8,128)(2,1)} %collective-permute-done.12.refs_0_, bf16[2048,128]{1,0:T(8,128)(2,1)S(1)} %collective-permute-done.7.refs_5_.refs_3_.refs_1_, bf16[1024,128]{1,0:T(8,128)(2,1)} %collective-permute-done.13.refs_2_, ...), custom_call_target="tpu_custom_call" | custom-call | flops 1 | bytes 1 | tf_op jit(solution)/shard_map/tally/pallas_call | solution.py:395
  101.6 0.1 reduce_sum.9
  101.7 1.1 collective-permute-done.17
  102.8 0.7 collective-permute-start.18
  103.5 2.9 %collective-permute-done.18 = f32[2,16]{1,0:T(2,128)S(1)} collective-permute-done((f32[2,16]{1,0:T(2,128)S(1)}, f32[2,16]{1,0:T(2,128)S(1)}, u32[]{:S(2)}, u32[]{:S(2)}) %collective-permute-start.18) | collective-permute-done | bytes 160 | tf_op jit(solution)/shard_map/ppermute | solution.py:418
  106.4 2.9 %collective-permute-start.19 = (f32[2,16]{1,0:T(2,128)S(1)}, f32[2,16]{1,0:T(2,128)S(1)}, u32[]{:S(2)}, u32[]{:S(2)}) collective-permute-start(f32[2,16]{1,0:T(2,128)S(1)} %add.38), channel_id=1, source_target_pairs={{0,4},{1,5},{2,6},{3,7},{4,0},{5,1},{6,2},{7,3},{8,12},{9,13},{10,... | collective-permute-start | bytes 392 | tf_op jit(solution)/shard_map/ppermute | solution.py:418
  109.3 1.5 %collective-permute-done.19 = f32[2,16]{1,0:T(2,128)S(1)} collective-permute-done((f32[2,16]{1,0:T(2,128)S(1)}, f32[2,16]{1,0:T(2,128)S(1)}, u32[]{:S(2)}, u32[]{:S(2)}) %collective-permute-start.19) | collective-permute-done | bytes 160 | tf_op jit(solution)/shard_map/ppermute | solution.py:418
  110.9 3.0 %collective-permute-start.20 = (f32[2,16]{1,0:T(2,128)S(1)}, f32[2,16]{1,0:T(2,128)S(1)}, u32[]{:S(2)}, u32[]{:S(2)}) collective-permute-start(f32[2,16]{1,0:T(2,128)S(1)} %add.39), channel_id=1, source_target_pairs={{0,8},{1,9},{2,10},{3,11},{4,12},{5,13},{6,14},{7,15},{8,0},{9,1},... | collective-permute-start | bytes 392 | tf_op jit(solution)/shard_map/ppermute | solution.py:418
  113.9 1.5 %collective-permute-done.20 = f32[2,16]{1,0:T(2,128)S(1)} collective-permute-done((f32[2,16]{1,0:T(2,128)S(1)}, f32[2,16]{1,0:T(2,128)S(1)}, u32[]{:S(2)}, u32[]{:S(2)}) %collective-permute-start.20) | collective-permute-done | bytes 160 | tf_op jit(solution)/shard_map/ppermute | solution.py:418
  115.4 0.7 dynamic-slice_reduce_fusion
  (56 shorter events, 0.5 us)
Async XLA Ops:
  0.0 12.5 %copy-start.3 = (f32[8,512,256]{2,1,0:T(8,128)S(1)}, f32[8,512,256]{2,1,0:T(8,128)}, u32[]{:S(2)}) copy-start(f32[8,512,256]{2,1,0:T(8,128)} %e_ref.3) | copy-start | bytes 12582916
  1.7 11.4 %copy-start.1 = (bf16[2048,128]{1,0:T(8,128)(2,1)}, bf16[2048,128]{1,0:T(8,128)(2,1)S(1)}, u32[]{:S(2)}) copy-start(bf16[2048,128]{1,0:T(8,128)(2,1)S(1)} %rotate_inputs.1.refs_0_) | copy-start | bytes 1572868
  3.9 43.6 %copy-start.9 = (bf16[1024,128]{1,0:T(8,128)(2,1)}, bf16[1024,128]{1,0:T(8,128)(2,1)S(1)}, u32[]{:S(2)}) copy-start(bf16[1024,128]{1,0:T(8,128)(2,1)S(1)} %get-tuple-element.18.refs_1_) | copy-start | bytes 786436
  3.9 43.6 %collective-permute-start.3 = (bf16[3072,128]{1,0:T(8,128)(2,1)S(1)}, bf16[3072,128]{1,0:T(8,128)(2,1)S(1)}, u32[]{:S(2)}, u32[]{:S(2)}) collective-permute-start(bf16[3072,128]{1,0:T(8,128)(2,1)S(1)} %get-tuple-element.12), channel_id=1, source_target_pairs={{0,2},{1,3},{2,0},{3,1},{4,6},{5,7},{6,4},{7,5},{8,10},{9,11},{10,... | collective-permute-start | bytes 2359304 | tf_op jit(solution)/shard_map/ppermute | solution.py:418
  6.9 36.8 %collective-permute-start = (bf16[2048,128]{1,0:T(8,128)(2,1)S(1)}, bf16[2048,128]{1,0:T(8,128)(2,1)S(1)}, u32[]{:S(2)}, u32[]{:S(2)}) collective-permute-start(bf16[2048,128]{1,0:T(8,128)(2,1)S(1)} %rotate_inputs.1.refs_0_), channel_id=1, source_target_pairs={{0,12},{1,13},{2,14},{3,15},{4,8},{5,9},{6,10},{7,11},{8,4},{9,5},... | collective-permute-start | bytes 1572872 | tf_op jit(solution)/shard_map/ppermute | solution.py:418
  10.5 35.4 %collective-permute-start.2 = (bf16[2048,128]{1,0:T(8,128)(2,1)S(1)}, bf16[2048,128]{1,0:T(8,128)(2,1)S(1)}, u32[]{:S(2)}, u32[]{:S(2)}) collective-permute-start(bf16[2048,128]{1,0:T(8,128)(2,1)S(1)} %rotate_inputs.1.refs_0_), channel_id=1, source_target_pairs={{0,4},{1,5},{2,6},{3,7},{4,0},{5,1},{6,2},{7,3},{8,12},{9,13},{10,... | collective-permute-start | bytes 1572872 | tf_op jit(solution)/shard_map/ppermute | solution.py:418
  10.5 36.9 %collective-permute-start.4 = (bf16[1024,128]{1,0:T(8,128)(2,1)S(1)}, bf16[1024,128]{1,0:T(8,128)(2,1)S(1)}, u32[]{:S(2)}, u32[]{:S(2)}) collective-permute-start(bf16[1024,128]{1,0:T(8,128)(2,1)S(1)} %get-tuple-element.13), channel_id=1, source_target_pairs={{0,6},{1,7},{2,4},{3,5},{4,2},{5,3},{6,0},{7,1},{8,14},{9,15},{10,... | collective-permute-start | bytes 786440 | tf_op jit(solution)/shard_map/ppermute | solution.py:418
  13.2 36.7 %copy-start = (bf16[64,128,128]{2,1,0:T(8,128)(2,1)S(1)}, bf16[64,128,128]{2,1,0:T(8,128)(2,1)}, u32[]{:S(2)}) copy-start(bf16[64,128,128]{2,1,0:T(8,128)(2,1)} %b_hbm.7) | copy-start | bytes 6291460
  13.2 36.7 %copy-start.8 = (bf16[16,128,128]{2,1,0:T(8,128)(2,1)S(1)}, bf16[16,128,128]{2,1,0:T(8,128)(2,1)}, u32[]{:S(2)}) copy-start(bf16[16,128,128]{2,1,0:T(8,128)(2,1)} %ib_ref.1) | copy-start | bytes 1572868
  13.2 36.7 %copy-start.11 = (bf16[8,2,512,256]{3,2,1,0:T(8,128)(2,1)S(1)}, bf16[8,2,512,256]{3,2,1,0:T(8,128)(2,1)}, u32[]{:S(2)}) copy-start(bf16[8,2,512,256]{3,2,1,0:T(8,128)(2,1)} %q_ref.1) | copy-start | bytes 12582916
  13.2 1.2 %collective-permute-start.8 = (f32[8,128]{1,0:T(8,128)S(1)}, f32[8,128]{1,0:T(8,128)S(1)}, u32[]{:S(2)}, u32[]{:S(2)}) collective-permute-start(f32[8,128]{1,0:T(8,128)S(1)} %sum_eigenvalues.1), channel_id=1, source_target_pairs={{0,1},{1,0},{2,3},{3,2},{4,5},{5,4},{6,7},{7,6},{8,9},{9,8},{10,11... | collective-permute-start | bytes 12296 | tf_op jit(solution)/shard_map/ppermute | solution.py:418
  14.4 10.1 %collective-permute-start.9 = (f32[8,128]{1,0:T(8,128)S(1)}, f32[8,128]{1,0:T(8,128)S(1)}, u32[]{:S(2)}, u32[]{:S(2)}) collective-permute-start(f32[8,128]{1,0:T(8,128)S(1)} %add.32), channel_id=1, source_target_pairs={{0,2},{1,3},{2,0},{3,1},{4,6},{5,7},{6,4},{7,5},{8,10},{9,11},{10,... | collective-permute-start | bytes 12296 | tf_op jit(solution)/shard_map/ppermute | solution.py:418
  24.5 14.6 %collective-permute-start.10 = (f32[8,128]{1,0:T(8,128)S(1)}, f32[8,128]{1,0:T(8,128)S(1)}, u32[]{:S(2)}, u32[]{:S(2)}) collective-permute-start(f32[8,128]{1,0:T(8,128)S(1)} %add.33), channel_id=1, source_target_pairs={{0,4},{1,5},{2,6},{3,7},{4,0},{5,1},{6,2},{7,3},{8,12},{9,13},{10,... | collective-permute-start | bytes 12296 | tf_op jit(solution)/shard_map/ppermute | solution.py:418
  39.2 4.5 %collective-permute-start.11 = (f32[8,128]{1,0:T(8,128)S(1)}, f32[8,128]{1,0:T(8,128)S(1)}, u32[]{:S(2)}, u32[]{:S(2)}) collective-permute-start(f32[8,128]{1,0:T(8,128)S(1)} %add.34), channel_id=1, source_target_pairs={{0,8},{1,9},{2,10},{3,11},{4,12},{5,13},{6,14},{7,15},{8,0},{9,1},... | collective-permute-start | bytes 12296 | tf_op jit(solution)/shard_map/ppermute | solution.py:418
  43.7 19.4 %collective-permute-start.1 = (bf16[2048,128]{1,0:T(8,128)(2,1)S(1)}, bf16[2048,128]{1,0:T(8,128)(2,1)S(1)}, u32[]{:S(2)}, u32[]{:S(2)}) collective-permute-start(bf16[2048,128]{1,0:T(8,128)(2,1)S(1)} %collective-permute-done.refs_0_.refs_2_), channel_id=1, source_target_pairs={{0,4},{1,5},{2,6},{3,7},{4,0},{5,1},{6,2},{7,3},{8,12},{9,13},{10,... | collective-permute-start | bytes 1572872 | tf_op jit(solution)/shard_map/ppermute | solution.py:418
  45.4 17.8 %collective-permute-start.7 = (bf16[2048,128]{1,0:T(8,128)(2,1)S(1)}, bf16[2048,128]{1,0:T(8,128)(2,1)S(1)}, u32[]{:S(2)}, u32[]{:S(2)}) collective-permute-start(bf16[2048,128]{1,0:T(8,128)(2,1)S(1)} %collective-permute-done.refs_0_.refs_2_), channel_id=1, source_target_pairs={{0,2},{1,3},{2,0},{3,1},{4,6},{5,7},{6,4},{7,5},{8,10},{9,11},{10,... | collective-permute-start | bytes 1572872 | tf_op jit(solution)/shard_map/ppermute | solution.py:418
  45.9 10.6 %copy-start.4 = (bf16[2048,128]{1,0:T(8,128)(2,1)}, bf16[2048,128]{1,0:T(8,128)(2,1)S(1)}, u32[]{:S(2)}) copy-start(bf16[2048,128]{1,0:T(8,128)(2,1)S(1)} %collective-permute-done.2.refs_1_.refs_0_) | copy-start | bytes 1572868
  45.9 21.8 %collective-permute-start.6 = (bf16[2048,128]{1,0:T(8,128)(2,1)S(1)}, bf16[2048,128]{1,0:T(8,128)(2,1)S(1)}, u32[]{:S(2)}, u32[]{:S(2)}) collective-permute-start(bf16[2048,128]{1,0:T(8,128)(2,1)S(1)} %collective-permute-done.2.refs_1_.refs_0_), channel_id=1, source_target_pairs={{0,2},{1,3},{2,0},{3,1},{4,6},{5,7},{6,4},{7,5},{8,10},{9,11},{10,... | collective-permute-start | bytes 1572872 | tf_op jit(solution)/shard_map/ppermute | solution.py:418
  47.4 9.1 %copy-start.6 = (bf16[1024,128]{1,0:T(8,128)(2,1)}, bf16[1024,128]{1,0:T(8,128)(2,1)S(1)}, u32[]{:S(2)}) copy-start(bf16[1024,128]{1,0:T(8,128)(2,1)S(1)} %collective-permute-done.4.refs_3_.refs_4_) | copy-start | bytes 786436
  49.2 22.8 %collective-permute-start.5 = (bf16[2048,128]{1,0:T(8,128)(2,1)S(1)}, bf16[2048,128]{1,0:T(8,128)(2,1)S(1)}, u32[]{:S(2)}, u32[]{:S(2)}) collective-permute-start(bf16[2048,128]{1,0:T(8,128)(2,1)S(1)} %rotate_grads.4), channel_id=1, source_target_pairs={{0,8},{1,9},{2,10},{3,11},{4,12},{5,13},{6,14},{7,15},{8,0},{9,1},... | collective-permute-start | bytes 1572872 | tf_op jit(solution)/shard_map/ppermute | solution.py:418
  56.5 25.6 %copy-start.15 = (s32[16]{0:T(128)S(1)}, s32[16]{0:T(128)}, u32[]{:S(2)}) copy-start(s32[16]{0:T(128)} %param.13) | copy-start | bytes 196
  56.5 26.0 %collective-permute-start.14 = (bf16[2,512,2048]{2,1,0:T(8,128)(2,1)}, bf16[2,512,2048]{2,1,0:T(8,128)(2,1)}, u32[]{:S(2)}, u32[]{:S(2)}) collective-permute-start(bf16[2,512,2048]{2,1,0:T(8,128)(2,1)} %precondition.1.refs_6_.own_ref), channel_id=1, source_target_pairs={{0,1},{1,0},{2,3},{3,2},{4,5},{5,4},{6,7},{7,6},{8,9},{9,8},{10,11... | collective-permute-start | bytes 12582920 | tf_op jit(solution)/shard_map/ppermute | solution.py:418
  74.6 0.7 copy-start.12
  75.3 0.7 copy-start.13
  76.0 0.7 copy-start.14
  76.7 21.2 %collective-permute-start.12 = (bf16[3072,128]{1,0:T(8,128)(2,1)}, bf16[3072,128]{1,0:T(8,128)(2,1)}, u32[]{:S(2)}, u32[]{:S(2)}) collective-permute-start(bf16[3072,128]{1,0:T(8,128)(2,1)} %get-tuple-element.14), channel_id=1, source_target_pairs={{0,2},{1,3},{2,0},{3,1},{4,6},{5,7},{6,4},{7,5},{8,10},{9,11},{10,... | collective-permute-start | bytes 2359304 | tf_op jit(solution)/shard_map/ppermute | solution.py:418
  77.2 16.3 %collective-permute-start.15 = (bf16[1024,128]{1,0:T(8,128)(2,1)}, bf16[1024,128]{1,0:T(8,128)(2,1)}, u32[]{:S(2)}, u32[]{:S(2)}) collective-permute-start(bf16[1024,128]{1,0:T(8,128)(2,1)} %copy-done.14), channel_id=1, source_target_pairs={{0,4},{1,5},{2,6},{3,7},{4,0},{5,1},{6,2},{7,3},{8,12},{9,13},{10,... | collective-permute-start | bytes 786440 | tf_op jit(solution)/shard_map/ppermute | solution.py:418
  77.2 16.3 %collective-permute-start.16 = (bf16[1024,128]{1,0:T(8,128)(2,1)}, bf16[1024,128]{1,0:T(8,128)(2,1)}, u32[]{:S(2)}, u32[]{:S(2)}) collective-permute-start(bf16[1024,128]{1,0:T(8,128)(2,1)} %copy-done.13), channel_id=1, source_target_pairs={{0,12},{1,13},{2,14},{3,15},{4,8},{5,9},{6,10},{7,11},{8,4},{9,5},... | collective-permute-start | bytes 786440 | tf_op jit(solution)/shard_map/ppermute | solution.py:418
  78.6 18.5 %collective-permute-start.13 = (bf16[1024,128]{1,0:T(8,128)(2,1)}, bf16[1024,128]{1,0:T(8,128)(2,1)}, u32[]{:S(2)}, u32[]{:S(2)}) collective-permute-start(bf16[1024,128]{1,0:T(8,128)(2,1)} %copy-done.12), channel_id=1, source_target_pairs={{0,14},{1,15},{2,12},{3,13},{4,10},{5,11},{6,8},{7,9},{8,6},{9,7},... | collective-permute-start | bytes 786440 | tf_op jit(solution)/shard_map/ppermute | solution.py:418
  82.5 3.7 %copy-start.2 = (bf16[2048,128]{1,0:T(8,128)(2,1)S(1)}, bf16[2048,128]{1,0:T(8,128)(2,1)}, u32[]{:S(2)}) copy-start(bf16[2048,128]{1,0:T(8,128)(2,1)} %copy-done.1) | copy-start | bytes 1572868
  82.5 3.7 %copy-start.7 = (bf16[1024,128]{1,0:T(8,128)(2,1)S(1)}, bf16[1024,128]{1,0:T(8,128)(2,1)}, u32[]{:S(2)}) copy-start(bf16[1024,128]{1,0:T(8,128)(2,1)} %copy-done.6) | copy-start | bytes 786436
  82.5 3.7 %copy-start.10 = (bf16[1024,128]{1,0:T(8,128)(2,1)S(1)}, bf16[1024,128]{1,0:T(8,128)(2,1)}, u32[]{:S(2)}) copy-start(bf16[1024,128]{1,0:T(8,128)(2,1)} %copy-done.9) | copy-start | bytes 786436
  86.2 7.3 %copy-start.5 = (bf16[2048,128]{1,0:T(8,128)(2,1)S(1)}, bf16[2048,128]{1,0:T(8,128)(2,1)}, u32[]{:S(2)}) copy-start(bf16[2048,128]{1,0:T(8,128)(2,1)} %copy-done.4) | copy-start | bytes 1572868
  101.7 1.1 collective-permute-start.17
  102.8 3.6 %collective-permute-start.18 = (f32[2,16]{1,0:T(2,128)S(1)}, f32[2,16]{1,0:T(2,128)S(1)}, u32[]{:S(2)}, u32[]{:S(2)}) collective-permute-start(f32[2,16]{1,0:T(2,128)S(1)} %add.37), channel_id=1, source_target_pairs={{0,2},{1,3},{2,0},{3,1},{4,6},{5,7},{6,4},{7,5},{8,10},{9,11},{10,... | collective-permute-start | bytes 392 | tf_op jit(solution)/shard_map/ppermute | solution.py:418
  106.4 4.5 %collective-permute-start.19 = (f32[2,16]{1,0:T(2,128)S(1)}, f32[2,16]{1,0:T(2,128)S(1)}, u32[]{:S(2)}, u32[]{:S(2)}) collective-permute-start(f32[2,16]{1,0:T(2,128)S(1)} %add.38), channel_id=1, source_target_pairs={{0,4},{1,5},{2,6},{3,7},{4,0},{5,1},{6,2},{7,3},{8,12},{9,13},{10,... | collective-permute-start | bytes 392 | tf_op jit(solution)/shard_map/ppermute | solution.py:418
  110.9 4.5 %collective-permute-start.20 = (f32[2,16]{1,0:T(2,128)S(1)}, f32[2,16]{1,0:T(2,128)S(1)}, u32[]{:S(2)}, u32[]{:S(2)}) collective-permute-start(f32[2,16]{1,0:T(2,128)S(1)} %add.39), channel_id=1, source_target_pairs={{0,8},{1,9},{2,10},{3,11},{4,12},{5,13},{6,14},{7,15},{8,0},{9,1},... | collective-permute-start | bytes 392 | tf_op jit(solution)/shard_map/ppermute | solution.py:418

commit v3 on v2

--- a/solution.py
+++ b/solution.py
@@ -118,74 +118,63 @@
     return pltpu.with_memory_space_constraint(value, pltpu.HBM)
 
 
-def rotate_inputs(layer_inputs, in_basis):
-    tokens, features = layer_inputs.shape
-    count, width, _ = in_basis.shape
-
-    def body(x_hbm, b_hbm, o_ref, x_all, b_all, sems):
-        copies = [
-            pltpu.make_async_copy(x_hbm, x_all, sems.at[0]),
-            pltpu.make_async_copy(b_hbm, b_all, sems.at[1]),
-        ]
-        for copy in copies:
-            copy.start()
-        for copy in copies:
-            copy.wait()
-        for n in range(count):
-            span = slice(n * width, (n + 1) * width)
-            turned = jnp.dot(x_all[:, span], b_all[n], preferred_element_type=F32)
-            o_ref[span, :] = turned.astype(BF16).T
-
-    hbm = pl.BlockSpec(memory_space=pl.ANY)
-    return call(
-        body,
-        in_specs=[hbm, hbm],
-        out_specs=pl.BlockSpec(memory_space=pltpu.VMEM),
-        out_shape=jax.ShapeDtypeStruct((features, tokens), BF16),
-        scratch_shapes=[
-            pltpu.VMEM((tokens, features), BF16),
-            pltpu.VMEM((count, width, width), BF16),
-            pltpu.SemaphoreType.DMA((2,)),
-        ],
-        name="rotate_inputs",
-    )(in_hbm(layer_inputs), in_hbm(in_basis))
-
-
-def rotate_grads(output_grads, out_basis, chip, chips, layouts, sources=(), after=(), cost=1):
+def rotate(output_grads, out_basis, chip, chips, layouts, layer_inputs=None, in_basis=None):
     tokens, units = output_grads.shape
     width = out_basis.shape[1]
     part = units // chips
     per = part // width
-    offsets = [k for layout in layouts for k in layout if isinstance(k, int)]
+    offsets = [k for layout in layouts for k in layout if k is not None]
     count = len(offsets)
-    heights = [sum(part if isinstance(k, int) else k[2] for k in layout) for layout in layouts]
-    extra = list(sources) + list(after)
-
-    def body(chip_ref, g_hbm, b_hbm, *refs):
-        o_refs = refs[len(extra) : len(extra) + len(layouts)]
-        g_all, b_all, g_sems, b_sems = refs[len(extra) + len(layouts) :]
+    features = 0 if layer_inputs is None else layer_inputs.shape[1]
+    heights = [sum(features if k is None else part for k in layout) for layout in layouts]
+    operands = [output_grads, out_basis]
+    if features:
+        operands += [layer_inputs, in_basis]
+
+    def body(chip_ref, *refs):
+        hbm_refs = refs[: len(operands)]
+        o_refs = refs[len(operands) : len(operands) + len(layouts)]
+        scratch = refs[len(operands) + len(layouts) :]
+        g_all, b_all, g_sems, b_sems = scratch[:4]
         copies = []
+        if features:
+            x_all, xb_all, x_sems = scratch[4:]
+            x_copies = [
+                pltpu.make_async_copy(hbm_refs[2], x_all, x_sems.at[0]),
+                pltpu.make_async_copy(hbm_refs[3], xb_all, x_sems.at[1]),
+            ]
+            for copy in x_copies:
+                copy.start()
         for n, k in enumerate(offsets):
             place = chip_ref[0] ^ k
             cols = pl.ds(pl.multiple_of(place * part, part), part)
             blocks = pl.ds(place * per, per)
             copies.append(
                 (
-                    pltpu.make_async_copy(g_hbm.at[:, cols], g_all.at[n], g_sems.at[n]),
-                    pltpu.make_async_copy(b_hbm.at[blocks], b_all.at[n], b_sems.at[n]),
+                    pltpu.make_async_copy(hbm_refs[0].at[:, cols], g_all.at[n], g_sems.at[n]),
+                    pltpu.make_async_copy(hbm_refs[1].at[blocks], b_all.at[n], b_sems.at[n]),
                 )
             )
         for pair in copies:
             for copy in pair:
                 copy.start()
+        if features:
+            for copy in x_copies:
+                copy.wait()
+            for i in range(features // width):
+                span = slice(i * width, (i + 1) * width)
+                turned = jnp.dot(x_all[:, span], xb_all[i], preferred_element_type=F32)
+                turned = turned.astype(BF16).T
+                for o_ref, layout in zip(o_refs, layouts):
+                    if None in layout:
+                        top = part * layout.index(None)
+                        o_ref[top + i * width : top + (i + 1) * width, :] = turned
         n = 0
         for o_ref, layout in zip(o_refs, layouts):
             top = 0
             for k in layout:
-                if not isinstance(k, int):
-                    source, first, rows = k
-                    o_ref[top : top + rows, :] = refs[source][first : first + rows, :]
-                    top += rows
+                if k is None:
+                    top += features
                     continue
                 for copy in copies[n]:
                     copy.wait()
@@ -198,22 +187,61 @@
 
     hbm = pl.BlockSpec(memory_space=pl.ANY)
     vmem = pl.BlockSpec(memory_space=pltpu.VMEM)
-    return call(
-        body,
-        in_specs=[pl.BlockSpec(memory_space=pltpu.SMEM), hbm, hbm]
-        + [vmem] * len(sources)
-        + [hbm] * len(after),
+    scratch_shapes = [
+        pltpu.VMEM((count, tokens, part), BF16),
+        pltpu.VMEM((count, per, width, width), BF16),
+        pltpu.SemaphoreType.DMA((count,)),
+        pltpu.SemaphoreType.DMA((count,)),
+    ]
+    if features:
+        scratch_shapes += [
+            pltpu.VMEM((tokens, features), BF16),
+            pltpu.VMEM(in_basis.shape, BF16),
+            pltpu.SemaphoreType.DMA((2,)),
+        ]
+    return call(
+        body,
+        in_specs=[pl.BlockSpec(memory_space=pltpu.SMEM)] + [hbm] * len(operands),
         out_specs=[vmem] * len(layouts),
         out_shape=[jax.ShapeDtypeStruct((h, tokens), BF16) for h in heights],
-        scratch_shapes=[
-            pltpu.VMEM((count, tokens, part), BF16),
-            pltpu.VMEM((count, per, width, width), BF16),
-            pltpu.SemaphoreType.DMA((count,)),
-            pltpu.SemaphoreType.DMA((count,)),
-        ],
-        name="rotate_grads",
+        scratch_shapes=scratch_shapes,
+        name="rotate",
+    )(chip[None], *[in_hbm(value) for value in operands])
+
+
+def pack(layouts, held, after, cost=1):
+    arrays = []
+    places = []
+    for layout in layouts:
+        for array, _, _ in layout:
+            if not any(array is other for other in arrays):
+                arrays.append(array)
+        places.append([next(i for i, o in enumerate(arrays) if o is a) for a, _, _ in layout])
+    operands = arrays + list(held) + list(after)
+
+    def body(*refs):
+        o_refs = refs[len(operands) : len(operands) + len(layouts)]
+        for o_ref, layout, place in zip(o_refs, layouts, places):
+            top = 0
+            for (_, first, rows), i in zip(layout, place):
+                o_ref[top : top + rows, :] = refs[i][first : first + rows, :]
+                top += rows
+
+    anywhere = pl.BlockSpec(memory_space=pl.ANY)
+    vmem = pl.BlockSpec(memory_space=pltpu.VMEM)
+    shapes = [
+        jax.ShapeDtypeStruct((sum(rows for _, _, rows in layout), layout[0][0].shape[1]), BF16)
+        for layout in layouts
+    ]
+    return call(
+        body,
         cost=cost,
-    )(chip[None], output_grads, out_basis, *extra)
+        in_specs=[vmem] * len(arrays) + [anywhere] * (len(held) + len(after)),
+        out_specs=[vmem] * len(layouts) + [anywhere] * len(held),
+        out_shape=shapes + [jax.ShapeDtypeStruct(h.shape, h.dtype) for h in held],
+        input_output_aliases={len(arrays) + n: len(layouts) + n for n in range(len(held))},
+        name="pack",
+    )(*operands)
 
 
 def sum_eigenvalues(eigenvalues):
@@ -240,18 +268,18 @@
     )(eigenvalues)
 
 
-def add_after(a, b, *after):
-    def body(a_ref, b_ref, *refs):
-        refs[-1][...] = a_ref[...] + b_ref[...]
+def hold(value, *after):
+    def body(v_ref, *refs):
+        refs[-1][...] = v_ref[...]
 
     vmem = pl.BlockSpec(memory_space=pltpu.VMEM)
     return call(
         body,
-        in_specs=[vmem, vmem] + [pl.BlockSpec(memory_space=pl.ANY)] * len(after),
+        in_specs=[vmem] + [pl.BlockSpec(memory_space=pl.ANY)] * len(after),
         out_specs=vmem,
-        out_shape=jax.ShapeDtypeStruct(a.shape, a.dtype),
-        name="add_after",
-    )(a, b, *after)
+        out_shape=jax.ShapeDtypeStruct(value.shape, value.dtype),
+        name="hold",
+    )(value, *after)
 
 
 def block_diagonal(blocks):
@@ -349,55 +377,97 @@
     )(core[None], own, sibling, *after)
 
 
-def tally(where, pieces, both, starts, ends, running):
-    count = len(pieces)
+def project(inputs, both, tokens, after):
+    cores, queries, rows, features = both.shape
+    block = math.gcd(rows, 512)
+
+    def body(*refs):
+        p_ref = refs[len(inputs)]
+        for c in range(cores):
+            for q in range(queries):
+                for r in range(0, rows, block):
+                    for n, (_, first) in enumerate(inputs):
+                        refs[len(inputs) + 1 + len(after) + n][c, q, r : r + block, :] = jnp.dot(
+                            p_ref[c, q, r : r + block, :],
+                            refs[n][first : first + features, :],
+                            preferred_element_type=F32,
+                        )
+
+    vmem = pl.BlockSpec(memory_space=pltpu.VMEM)
+    return call(
+        body,
+        in_specs=[vmem] * (len(inputs) + 1) + [pl.BlockSpec(memory_space=pl.ANY)] * len(after),
+        out_specs=[vmem] * len(inputs),
+        out_shape=[jax.ShapeDtypeStruct((cores, queries, rows, tokens), F32)] * len(inputs),
+        name="project",
+    )(*[x for x, _ in inputs], both, *after)
+
+
+def tally(where, projected, pieces, early, both, starts, ends, running):
     cores, queries, rows, features = both.shape
     tokens = starts.shape[1]
     block = math.gcd(rows, 512)
     docs = starts.shape[0]
     arrays = []
-    places = []
-    for piece in pieces:
-        for array, _ in piece:
-            if not any(array is other for other in arrays):
-                arrays.append(array)
-        places.append([next(i for i, o in enumerate(arrays) if o is a) for a, _ in piece])
+
+    def place(array):
+        if not any(array is other for other in arrays):
+            arrays.append(array)
+        return next(i for i, o in enumerate(arrays) if o is array)
+
+    fresh = [(place(x), first) for (x, first), _ in pieces] + [(place(x), f) for x, f in early]
+    ready = [place(p) for p, _ in projected]
+    grads = [(place(g), f) for _, (g, f) in projected] + [(place(g), f) for _, (g, f) in pieces]
+    held, count = len(ready), len(pieces)
 
     def body(where_ref, *refs):
-        p_ref, st_ref, en_ref, run_ref, o_ref, x_all = refs[len(arrays) :]
-        for n in range(count):
-            first = pieces[n][0][1]
-            x_all[:, n * tokens : (n + 1) * tokens] = refs[places[n][0]][first : first + features, :]
-        scores = [[jnp.zeros((1, tokens), F32)] * queries for _ in range(count)]
+        p_ref, st_ref, en_ref, run_ref, o_ref = refs[len(arrays) : len(arrays) + 5]
+        t_refs = refs[len(arrays) + 5 : len(arrays) + 5 + len(early)]
+        x_all = refs[-1]
+        for n, (i, first) in enumerate(fresh):
+            x_all[:, n * tokens : (n + 1) * tokens] = refs[i][first : first + features, :]
+        scores = [[jnp.zeros((1, tokens), F32)] * queries for _ in grads]
         for c in range(cores):
             for q in range(queries):
                 for r in range(0, rows, block):
-                    turned = jnp.dot(
-                        p_ref[c, q, r : r + block, :], x_all[...], preferred_element_type=F32
-                    )
-                    for n in range(count):
-                        first = pieces[n][1][1] + c * rows + r
+                    if fresh:
+                        turned = jnp.dot(
+                            p_ref[c, q, r : r + block, :], x_all[...], preferred_element_type=F32
+                        )
+                    for n, t_ref in enumerate(t_refs):
+                        t_ref[c, q, r : r + block, :] = turned[
+                            :, (count + n) * tokens : (count + n + 1) * tokens
+                        ]
+                    for n, (i, first) in enumerate(grads):
+                        if n < held:
+                            mine = refs[ready[n]][c, q, r : r + block, :]
+                        else:
+                            mine = turned[:, (n - held) * tokens : (n - held + 1) * tokens]
+                        first = first + c * rows + r
                         scores[n][q] = scores[n][q] + jnp.sum(
-                            turned[:, n * tokens : (n + 1) * tokens]
-                            * refs[places[n][1]][first : first + block, :].astype(F32),
+                            mine * refs[i][first : first + block, :].astype(F32),
                             axis=0,
                             keepdims=True,
                         )
         for q in range(queries):
             total = run_ref[q]
-            for n in range(count):
+            for n in range(len(grads)):
                 spot = where_ref[n] * tokens + lax.broadcasted_iota(jnp.int32, (docs, tokens), 1)
                 inside = (spot >= st_ref[...]) & (spot < en_ref[...])
                 total = total + jnp.where(inside, scores[n][q], 0.0)
             o_ref[q] = total
 
     vmem = pl.BlockSpec(memory_space=pltpu.VMEM)
-    return call(
-        body,
-        in_specs=[pl.BlockSpec(memory_space=pltpu.SMEM)] + [vmem] * (len(arrays) + 4),
-        out_specs=vmem,
-        out_shape=jax.ShapeDtypeStruct(running.shape, F32),
-        scratch_shapes=[pltpu.VMEM((features, count * tokens), BF16)],
+    kept = jax.ShapeDtypeStruct((cores, queries, rows, tokens), F32)
+    return call(
+        body,
+        in_specs=[pl.BlockSpec(memory_space=pltpu.SMEM)]
+        + [vmem] * len(arrays)
+        + [vmem if fresh else pl.BlockSpec(memory_space=pl.ANY)]
+        + [vmem] * 3,
+        out_specs=[vmem] * (1 + len(early)),
+        out_shape=[jax.ShapeDtypeStruct(running.shape, F32)] + [kept] * len(early),
+        scratch_shapes=[pltpu.VMEM((features, len(fresh) * tokens), BF16)] if fresh else [],
         name="tally",
     )(where, *arrays, both, starts, ends, running)
 
@@ -419,36 +489,41 @@
 
     features = layer_inputs.shape[1]
     part = output_grads.shape[1] // chips
-    x = rotate_inputs(layer_inputs, in_basis)
-    rotate = functools.partial(rotate_grads, in_hbm(output_grads), in_hbm(out_basis), chip, chips)
-    side, near_side_g, g_own = rotate([[(0, 0, features), 1], [3], [0]], [x])
+    turn = functools.partial(rotate, output_grads, out_basis, chip, chips)
+    x, side, g_own = turn([[None], [None, 1, 3], [0]], layer_inputs, in_basis)
     far_x = swap(x, 12)
     near_x = swap(x, 4)
     side = swap(side, 2)
-    near_side_g = swap(near_side_g, 6)
-    first = [far_x, near_x, side, near_side_g]
-
+    first = [far_x, near_x, side]
+
+    middle, g_far, g_far_side, near_g = turn([[4, 5], [6], [7], [2]])
     sums = sum_eigenvalues(eigenvalues)
-    for offset in (1, 2, 4, 8):
+    sums = sums + swap(sums, 1)
+    sums = hold(sums, middle)
+    for offset in (2, 4):
         sums = sums + swap(sums, offset)
 
-    (middle,) = rotate([[4, 5]], [], first)
+    sides_sent, middle = pack([[(near_x, 0, features), (far_x, 0, features)]], [middle], first)
     middle = swap(middle, 8)
     middle_x = swap(far_x, 4)
-    near_x_side = swap(near_x, 2)
-    far_x_side = swap(far_x, 2)
-    second = [middle, middle_x, near_x_side, far_x_side]
-
+    sides = swap(sides_sent, 2)
+    second = [middle, middle_x, sides]
+
+    sums = hold(sums, sides_sent)
+    sums = sums + swap(sums, 8)
     own = precondition_rows(
         query_grads, eigenvalues, sums, out_basis, in_basis, me, entries, first
     )
-    both = join_rows(own, swap(own, 1), core, second)
-
-    middle_side, g_far, g_far_side, near_g = rotate(
-        [[(0, 0, features), (1, part, part)], [6], [7], [2]],
-        [middle_x, middle],
+    both = join_rows(own, swap(own, 1), core, [])
+
+    middle_side, near_g, g_far, g_far_side = pack(
+        [
+            [(middle_x, 0, features), (middle, part, part)],
+            [(near_g, 0, part), (side, features + part, part)],
+        ],
+        [g_far, g_far_side],
         second + [own],
-        cost=COST_K3,
+        COST_K3,
     )
     middle_side = swap(middle_side, 2)
     g_far = swap(g_far, 12)
@@ -461,19 +536,41 @@
     starts = jnp.broadcast_to(doc_starts[:, None], (docs, tokens))
     ends = jnp.broadcast_to(doc_ends[:, None], (docs, tokens))
     running = jnp.zeros((queries, docs, tokens), F32)
-    pieces = {
-        0: ((x, 0), (g_own, 0)),
-        1: ((side, 0), (side, features)),
-        2: ((near_x, 0), (near_g, 0)),
-        3: ((near_x_side, 0), (near_side_g, 0)),
-        4: ((middle_x, 0), (middle, 0)),
-        5: ((middle_side, 0), (middle_side, features)),
-        6: ((far_x, 0), (g_far, 0)),
-        7: ((far_x_side, 0), (g_far_side, 0)),
-    }
-    for some in ((0, 1, 3, 4), (2, 6), (5, 7)):
-        where = jnp.stack([me ^ (2 * k) for k in some]).astype(jnp.int32)
-        running = tally(where, [pieces[k] for k in some], both, starts, ends, running)
+
+    def where(*offsets):
+        return jnp.stack([me ^ (2 * k) for k in offsets]).astype(jnp.int32)
+
+    running, *kept = tally(
+        where(0, 1, 4),
+        [],
+        [
+            ((x, 0), (g_own, 0)),
+            ((side, 0), (side, features)),
+            ((middle_x, 0), (middle, 0)),
+        ],
+        [(near_x, 0), (sides, 0), (far_x, 0), (sides, features)],
+        both,
+        starts,
+        ends,
+        running,
+    )
+    projected = project([(middle_side, 0)], both, tokens, [running])
+    (running,) = tally(
+        where(2, 3, 6, 7, 5),
+        [
+            (kept[0], (near_g, 0)),
+            (kept[1], (near_g, part)),
+            (kept[2], (g_far, 0)),
+            (kept[3], (g_far_side, 0)),
+            (projected[0], (middle_side, features)),
+        ],
+        [],
+        [],
+        both,
+        starts,
+        ends,
+        running,
+    )
     shares = jnp.sum(running, axis=2)
     for offset in (1, 2, 4, 8):
         shares = shares + swap(shares, offset)

time: 116 us -> 102 us (0.88)
  waiting for transfers between devices: 51.9 us -> 43.2 us
  starting transfers between devices: 28.9 us -> 23.9 us
  local copies, waits for them, and re-layouts: 3.09 us -> 1.8 us
    ppermute x21 -> x19, waiting for transfers between devices: 51.9 us -> 43.2 us  [swap(): return lax.ppermute(value, 'dp', [(i, i ^ offset) for i in range(devices)])]
    ppermute x21 -> x19, starting transfers between devices: 28.9 us -> 23.9 us  [swap(): return lax.ppermute(value, 'dp', [(i, i ^ offset) for i in range(devices)])]
    unnamed x32 -> x30, local copies, waits for them, and re-layouts: 2.16 us -> 0.78 us
    pallas_call x7 -> x9, Pallas kernels: 20.7 us -> 21.2 us  [the longest x2 11.5 us: tally(): call(body, in_specs=[pl.BlockSpec(memory_space=pltpu.SMEM)] + [vmem] * le...]
  transfers between devices with their start and end apart: 21 -> 19, of which waited for: 13 -> 9; matrix products, arithmetic and copies ran while one was open for 1% -> 1% of each run, Pallas kernels for 21% -> 27%
where the time goes in v3:
time: 102 us
  waiting for transfers between devices  43.2 us (42%)
  Pallas kernels  32.1 us (31%)
  starting transfers between devices  23.9 us (23%)
  local copies, waits for them, and re-layouts  1.8 us (2%)
    ppermute x19, waiting for transfers between devices, swap(): return lax.ppermute(value, 'dp', [(i, i ^ offset) for i in range(devices)])  43.2 us
    ppermute x19, starting transfers between devices, swap(): return lax.ppermute(value, 'dp', [(i, i ^ offset) for i in range(devices)])  23.9 us
    pallas_call x2, Pallas kernels, tally(): call(body, in_specs=[pl.BlockSpec(memory_space=pltpu.SMEM)] + [vmem] * le...  11.5 us
    pallas_call x1, Pallas kernels, precondition_rows(): call(body, grid_spec=grid_spec, out_shape=jax.ShapeDtypeStruct((queries,...  6.64 us
    pallas_call x2, Pallas kernels, rotate(): call(body, in_specs=[pl.BlockSpec(memory_space=pltpu.SMEM)] + [hbm] * len...  6.13 us
    pallas_call x1, Pallas kernels, join_rows(): call(body, in_specs=[pl.BlockSpec(memory_space=pltpu.SMEM), hbm, hbm] + [...  3.62 us
    pallas_call x1, Pallas kernels, project(): call(body, in_specs=[vmem] * (len(inputs) + 1) + [pl.BlockSpec(memory_spa...  2.32 us
  transfers between devices with their start and end apart: 19, of which 9 were waited for; matrix products, arithmetic and copies ran while one was open for 1% of the time, Pallas kernels for 27%

profile of v3, /device:TPU:0, one launch (start us, length us, event | category | flops | bytes accessed | tf_op | source)
XLA Modules:
  0.0 101.7 jit_solution(10566436318469964557)
XLA Ops:
  0.0 2.9 %rotate.2 = (bf16[2048,128]{1,0:T(8,128)(2,1)S(1)}, bf16[4096,128]{1,0:T(8,128)(2,1)S(1)}, bf16[1024,128]{1,0:T(8,128)(2,1)S(1)}) custom-call(s32[1]{0:T(128)} %bitcast.8.chip_ref, bf16[128,8192]{1,0:T(8,128)(2,1)} %refs_0_.3, bf16[64,128,128]{2,1,0:T(8,128)(2,1)} %ob_ref.1, bf16[128,2048]{1,0:T(8,128)(2,1)} %refs_2_.1, bf16[16,128,128]{2,1,0:T(8,128)(2,1)} %ib_ref.1), custom_call_target="tpu_custom_call" | custom-call | flops 1 | bytes 1 | tf_op jit(solution)/shard_map/rotate/pallas_call | solution.py:202
  3.0 3.0 %collective-permute-start = (bf16[4096,128]{1,0:T(8,128)(2,1)S(1)}, bf16[4096,128]{1,0:T(8,128)(2,1)S(1)}, u32[]{:S(2)}, u32[]{:S(2)}) collective-permute-start(bf16[4096,128]{1,0:T(8,128)(2,1)S(1)} %get-tuple-element.24), channel_id=1, source_target_pairs={{0,2},{1,3},{2,0},{3,1},{4,6},{5,7},{6,4},{7,5},{8,10},{9,11},{10,... | collective-permute-start | bytes 3145736 | tf_op jit(solution)/shard_map/ppermute | solution.py:488
  6.0 3.6 %collective-permute-start.1 = (bf16[2048,128]{1,0:T(8,128)(2,1)S(1)}, bf16[2048,128]{1,0:T(8,128)(2,1)S(1)}, u32[]{:S(2)}, u32[]{:S(2)}) collective-permute-start(bf16[2048,128]{1,0:T(8,128)(2,1)S(1)} %get-tuple-element.23.refs_0_), channel_id=1, source_target_pairs={{0,12},{1,13},{2,14},{3,15},{4,8},{5,9},{6,10},{7,11},{8,4},{9,5},... | collective-permute-start | bytes 1572872 | tf_op jit(solution)/shard_map/ppermute | solution.py:488
  9.6 0.7 sum_eigenvalues.1
  10.3 0.0 copy-start
  10.3 0.0 copy-start.4
  10.3 0.1 collective-permute-start.6
  10.4 3.2 %rotate.3 = (bf16[2048,128]{1,0:T(8,128)(2,1)S(1)}, bf16[1024,128]{1,0:T(8,128)(2,1)}, bf16[1024,128]{1,0:T(8,128)(2,1)}, bf16[1024,128]{1,0:T(8,128)(2,1)S(1)}) custom-call(s32[1]{0:T(128)} %bitcast.8.chip_ref, bf16[128,8192]{1,0:T(8,128)(2,1)} %refs_0_.3, bf16[64,128,128]{2,1,0:T(8,128)(2,1)} %ob_ref.1), custom_call_target="tpu_custom_call" | custom-call | flops 1 | bytes 1 | tf_op jit(solution)/shard_map/rotate/pallas_call | solution.py:202
  13.6 0.6 collective-permute-start.7
  14.2 15.0 %collective-permute-done.7 = f32[8,128]{1,0:T(8,128)S(1)} collective-permute-done((f32[8,128]{1,0:T(8,128)S(1)}, f32[8,128]{1,0:T(8,128)S(1)}, u32[]{:S(2)}, u32[]{:S(2)}) %collective-permute-start.7) | collective-permute-done | bytes 4128 | tf_op jit(solution)/shard_map/ppermute | solution.py:488
  29.2 1.8 %collective-permute-start.8 = (f32[8,128]{1,0:T(8,128)S(1)}, f32[8,128]{1,0:T(8,128)S(1)}, u32[]{:S(2)}, u32[]{:S(2)}) collective-permute-start(f32[8,128]{1,0:T(8,128)S(1)} %add.34), channel_id=1, source_target_pairs={{0,4},{1,5},{2,6},{3,7},{4,0},{5,1},{6,2},{7,3},{8,12},{9,13},{10,... | collective-permute-start | bytes 12296 | tf_op jit(solution)/shard_map/ppermute | solution.py:488
  31.0 1.8 %collective-permute-done.8 = f32[8,128]{1,0:T(8,128)S(1)} collective-permute-done((f32[8,128]{1,0:T(8,128)S(1)}, f32[8,128]{1,0:T(8,128)S(1)}, u32[]{:S(2)}, u32[]{:S(2)}) %collective-permute-start.8) | collective-permute-done | bytes 4128 | tf_op jit(solution)/shard_map/ppermute | solution.py:488
  32.9 0.1 pack.2
  33.0 2.9 %collective-permute-start.9 = (f32[8,128]{1,0:T(8,128)S(1)}, f32[8,128]{1,0:T(8,128)S(1)}, u32[]{:S(2)}, u32[]{:S(2)}) collective-permute-start(f32[8,128]{1,0:T(8,128)S(1)} %hold.3), channel_id=1, source_target_pairs={{0,8},{1,9},{2,10},{3,11},{4,12},{5,13},{6,14},{7,15},{8,0},{9,1},... | collective-permute-start | bytes 12296 | tf_op jit(solution)/shard_map/ppermute | solution.py:488
  35.8 1.6 %collective-permute-start.2 = (bf16[2048,128]{1,0:T(8,128)(2,1)S(1)}, bf16[2048,128]{1,0:T(8,128)(2,1)S(1)}, u32[]{:S(2)}, u32[]{:S(2)}) collective-permute-start(bf16[2048,128]{1,0:T(8,128)(2,1)S(1)} %collective-permute-done.1.refs_1_.refs_3_.refs_0_.refs_5_), channel_id=1, source_target_pairs={{0,4},{1,5},{2,6},{3,7},{4,0},{5,1},{6,2},{7,3},{8,12},{9,13},{10,... | collective-permute-start | bytes 1572872 | tf_op jit(solution)/shard_map/ppermute | solution.py:488
  37.4 1.5 %collective-permute-start.4 = (bf16[4096,128]{1,0:T(8,128)(2,1)S(1)}, bf16[4096,128]{1,0:T(8,128)(2,1)S(1)}, u32[]{:S(2)}, u32[]{:S(2)}) collective-permute-start(bf16[4096,128]{1,0:T(8,128)(2,1)S(1)} %get-tuple-element.26.refs_0_), channel_id=1, source_target_pairs={{0,2},{1,3},{2,0},{3,1},{4,6},{5,7},{6,4},{7,5},{8,10},{9,11},{10,... | collective-permute-start | bytes 3145736 | tf_op jit(solution)/shard_map/ppermute | solution.py:488
  38.9 0.3 collective-permute-start.5
  39.3 6.6 %precondition.1.own_ref.refs_9_ = bf16[2,512,2048]{2,1,0:T(8,128)(2,1)} custom-call(s32[1]{0:T(128)} %bitcast.5.me_ref, bf16[8,2,512,256]{3,2,1,0:T(8,128)(2,1)S(1)} %copy-done.13, f32[8,512,256]{2,1,0:T(8,128)S(1)} %copy-done.1, f32[8,128]{1,0:T(8,128)S(1)} %add.36.s_ref, bf16[64,128,128]{2,1,0:T(8,128)(2,1)S(1)} %copy-done, ...), custom_call_target="tpu_custom_call" | custom-call | flops 99999997952 | bytes 1 | tf_op jit(solution)/shard_map/precondition/pallas_call | solution.py:348
  45.9 10.8 %collective-permute-done.2.refs_2_.refs_0_.refs_7_ = bf16[2048,128]{1,0:T(8,128)(2,1)S(1)} collective-permute-done((bf16[2048,128]{1,0:T(8,128)(2,1)S(1)}, bf16[2048,128]{1,0:T(8,128)(2,1)S(1)}, u32[]{:S(2)}, u32[]{:S(2)}) %collective-permute-start.2) | collective-permute-done | bytes 524320 | tf_op jit(solution)/shard_map/ppermute | solution.py:488
  56.8 5.2 %collective-permute-done.5.refs_7_.refs_1_.refs_6_ = bf16[2048,128]{1,0:T(8,128)(2,1)S(1)} collective-permute-done((bf16[2048,128]{1,0:T(8,128)(2,1)S(1)}, bf16[2048,128]{1,0:T(8,128)(2,1)S(1)}, u32[]{:S(2)}, u32[]{:S(2)}) %collective-permute-start.5) | collective-permute-done | bytes 524320 | tf_op jit(solution)/shard_map/ppermute | solution.py:488
  61.9 1.2 %pack.3 = (bf16[3072,128]{1,0:T(8,128)(2,1)}, bf16[2048,128]{1,0:T(8,128)(2,1)}, bf16[1024,128]{1,0:T(8,128)(2,1)}, bf16[1024,128]{1,0:T(8,128)(2,1)}) custom-call(bf16[2048,128]{1,0:T(8,128)(2,1)S(1)} %collective-permute-done.2.refs_2_.refs_0_.refs_7_, ...), custom_call_target="tpu_custom_call", output_to_operand_aliasing={{2}: (4, {}), {3}: (5, {})} | custom-call | flops 99999997952 | bytes 1 | tf_op jit(solution)/shard_map/pack/pallas_call | solution.py:236
  63.2 0.4 copy-done.2
  63.5 0.5 collective-permute-start.11
  64.0 2.1 %collective-permute-start.13 = (bf16[1024,128]{1,0:T(8,128)(2,1)}, bf16[1024,128]{1,0:T(8,128)(2,1)}, u32[]{:S(2)}, u32[]{:S(2)}) collective-permute-start(bf16[1024,128]{1,0:T(8,128)(2,1)} %get-tuple-element.39), channel_id=1, source_target_pairs={{0,12},{1,13},{2,14},{3,15},{4,8},{5,9},{6,10},{7,11},{8,4},{9,5},... | collective-permute-start | bytes 786440 | tf_op jit(solution)/shard_map/ppermute | solution.py:488
  66.1 2.7 %collective-permute-start.14 = (bf16[1024,128]{1,0:T(8,128)(2,1)}, bf16[1024,128]{1,0:T(8,128)(2,1)}, u32[]{:S(2)}, u32[]{:S(2)}) collective-permute-start(bf16[1024,128]{1,0:T(8,128)(2,1)} %get-tuple-element.40), channel_id=1, source_target_pairs={{0,14},{1,15},{2,12},{3,13},{4,10},{5,11},{6,8},{7,9},{8,6},{9,7},... | collective-permute-start | bytes 786440 | tf_op jit(solution)/shard_map/ppermute | solution.py:488
  68.8 0.1 copy.14
  68.9 0.1 reduce
  69.1 0.1 stack.35.where_ref
  69.2 0.1 pad_add_fusion.where_ref
  69.3 3.6 %join_rows.1.refs_8_.refs_1_.refs_9_ = bf16[2,2,512,2048]{3,2,1,0:T(8,128)(2,1)S(1)} custom-call(s32[1]{0:T(128)} %bitcast.9.core_ref, bf16[2,512,2048]{2,1,0:T(8,128)(2,1)} %precondition.1.own_ref.refs_9_, bf16[2,512,2048]{2,1,0:T(8,128)(2,1)} %collective-permute-done.10.sib_ref), custom_call_target="tpu_custom_call" | custom-call | flops 1 | bytes 1 | tf_op jit(solution)/shard_map/join_rows/pallas_call | solution.py:370
  72.9 0.1 broadcast_in_dim.12.refs_9_.refs_10_
  73.0 0.1 broadcast_in_dim.26.refs_10_.refs_11_
  73.1 0.2 copy-done.8
  73.2 0.2 copy-done.10
  73.4 0.1 copy-done.12
  73.4 9.8 %tally.2 = (f32[2,16,128]{2,1,0:T(8,128)S(1)}, f32[2,2,512,128]{3,2,1,0:T(8,128)S(1)}, f32[2,2,512,128]{3,2,1,0:T(8,128)S(1)}, f32[2,2,512,128]{3,2,1,0:T(8,128)S(1)}, f32[2,2,512,128]{3,2,1,0:T(8,128)S(1)}) custom-call(s32[3]{0:T(128)S(1)} %pad_add_fusion.where_ref, bf16[2048,128]{1,0:T(8,128)(2,1)S(1)} %copy-done.6, ...), custom_call_target="tpu_custom_call" | custom-call | flops 1 | bytes 1 | tf_op jit(solution)/shard_map/tally/pallas_call | solution.py:462
  83.2 2.3 %project.1.refs_4_ = f32[2,2,512,128]{3,2,1,0:T(8,128)S(1)} custom-call(bf16[3072,128]{1,0:T(8,128)(2,1)S(1)} %collective-permute-done.11.refs_0_.refs_8_, bf16[2,2,512,2048]{3,2,1,0:T(8,128)(2,1)S(1)} %join_rows.1.refs_8_.refs_1_.refs_9_, f32[2,16,128]{2,1,0:T(8,128)S(1)} %get-tuple-element.37.refs_2_.refs_12_), custom_call_target="tpu_custom_call" | custom-call | flops 1 | bytes 1 | tf_op jit(solution)/shard_map/project/pallas_call | solution.py:397
  85.5 0.9 collective-permute-done.14.refs_7_
  86.4 1.7 %tally.3 = f32[2,16,128]{2,1,0:T(8,128)S(1)} custom-call(s32[5]{0:T(128)S(1)} %stack.35.where_ref, f32[2,2,512,128]{3,2,1,0:T(8,128)S(1)} %get-tuple-element.29.refs_0_, f32[2,2,512,128]{3,2,1,0:T(8,128)S(1)} %get-tuple-element.30.refs_1_, f32[2,2,512,128]{3,2,1,0:T(8,128)S(1)} %get-tuple-element.31.refs_2_, ...), custom_call_target="tpu_custom_call" | custom-call | flops 1 | bytes 1 | tf_op jit(solution)/shard_map/tally/pallas_call | solution.py:462
  88.1 0.1 reduce_sum.9
  88.2 1.1 %collective-permute-done.15 = f32[2,16]{1,0:T(2,128)S(1)} collective-permute-done((f32[2,16]{1,0:T(2,128)S(1)}, f32[2,16]{1,0:T(2,128)S(1)}, u32[]{:S(2)}, u32[]{:S(2)}) %collective-permute-start.15) | collective-permute-done | bytes 160 | tf_op jit(solution)/shard_map/ppermute | solution.py:488
  89.4 0.4 collective-permute-start.16
  89.8 3.1 %collective-permute-done.16 = f32[2,16]{1,0:T(2,128)S(1)} collective-permute-done((f32[2,16]{1,0:T(2,128)S(1)}, f32[2,16]{1,0:T(2,128)S(1)}, u32[]{:S(2)}, u32[]{:S(2)}) %collective-permute-start.16) | collective-permute-done | bytes 160 | tf_op jit(solution)/shard_map/ppermute | solution.py:488
  92.9 1.4 %collective-permute-start.17 = (f32[2,16]{1,0:T(2,128)S(1)}, f32[2,16]{1,0:T(2,128)S(1)}, u32[]{:S(2)}, u32[]{:S(2)}) collective-permute-start(f32[2,16]{1,0:T(2,128)S(1)} %add.38), channel_id=1, source_target_pairs={{0,4},{1,5},{2,6},{3,7},{4,0},{5,1},{6,2},{7,3},{8,12},{9,13},{10,... | collective-permute-start | bytes 392 | tf_op jit(solution)/shard_map/ppermute | solution.py:488
  94.3 2.2 %collective-permute-done.17 = f32[2,16]{1,0:T(2,128)S(1)} collective-permute-done((f32[2,16]{1,0:T(2,128)S(1)}, f32[2,16]{1,0:T(2,128)S(1)}, u32[]{:S(2)}, u32[]{:S(2)}) %collective-permute-start.17) | collective-permute-done | bytes 160 | tf_op jit(solution)/shard_map/ppermute | solution.py:488
  96.5 1.4 %collective-permute-start.18 = (f32[2,16]{1,0:T(2,128)S(1)}, f32[2,16]{1,0:T(2,128)S(1)}, u32[]{:S(2)}, u32[]{:S(2)}) collective-permute-start(f32[2,16]{1,0:T(2,128)S(1)} %add.39), channel_id=1, source_target_pairs={{0,8},{1,9},{2,10},{3,11},{4,12},{5,13},{6,14},{7,15},{8,0},{9,1},... | collective-permute-start | bytes 392 | tf_op jit(solution)/shard_map/ppermute | solution.py:488
  97.9 3.1 %collective-permute-done.18 = f32[2,16]{1,0:T(2,128)S(1)} collective-permute-done((f32[2,16]{1,0:T(2,128)S(1)}, f32[2,16]{1,0:T(2,128)S(1)}, u32[]{:S(2)}, u32[]{:S(2)}) %collective-permute-start.18) | collective-permute-done | bytes 160 | tf_op jit(solution)/shard_map/ppermute | solution.py:488
  101.0 0.7 dynamic-slice_reduce_fusion
  (51 shorter events, 0.2 us)
Async XLA Ops:
  0.0 9.6 %copy-start.1 = (f32[8,512,256]{2,1,0:T(8,128)S(1)}, f32[8,512,256]{2,1,0:T(8,128)}, u32[]{:S(2)}) copy-start(f32[8,512,256]{2,1,0:T(8,128)} %e_ref.3) | copy-start | bytes 12582916
  2.9 10.6 %copy-start.5 = (bf16[2048,128]{1,0:T(8,128)(2,1)}, bf16[2048,128]{1,0:T(8,128)(2,1)S(1)}, u32[]{:S(2)}) copy-start(bf16[2048,128]{1,0:T(8,128)(2,1)S(1)} %get-tuple-element.23.refs_0_) | copy-start | bytes 1572868
  3.0 10.6 %copy-start.11 = (bf16[1024,128]{1,0:T(8,128)(2,1)}, bf16[1024,128]{1,0:T(8,128)(2,1)S(1)}, u32[]{:S(2)}) copy-start(bf16[1024,128]{1,0:T(8,128)(2,1)S(1)} %get-tuple-element.27.refs_6_) | copy-start | bytes 786436
  3.0 29.9 %collective-permute-start = (bf16[4096,128]{1,0:T(8,128)(2,1)S(1)}, bf16[4096,128]{1,0:T(8,128)(2,1)S(1)}, u32[]{:S(2)}, u32[]{:S(2)}) collective-permute-start(bf16[4096,128]{1,0:T(8,128)(2,1)S(1)} %get-tuple-element.24), channel_id=1, source_target_pairs={{0,2},{1,3},{2,0},{3,1},{4,6},{5,7},{6,4},{7,5},{8,10},{9,11},{10,... | collective-permute-start | bytes 3145736 | tf_op jit(solution)/shard_map/ppermute | solution.py:488
  6.0 26.9 %collective-permute-start.1 = (bf16[2048,128]{1,0:T(8,128)(2,1)S(1)}, bf16[2048,128]{1,0:T(8,128)(2,1)S(1)}, u32[]{:S(2)}, u32[]{:S(2)}) collective-permute-start(bf16[2048,128]{1,0:T(8,128)(2,1)S(1)} %get-tuple-element.23.refs_0_), channel_id=1, source_target_pairs={{0,12},{1,13},{2,14},{3,15},{4,8},{5,9},{6,10},{7,11},{8,4},{9,5},... | collective-permute-start | bytes 1572872 | tf_op jit(solution)/shard_map/ppermute | solution.py:488
  9.6 23.3 %collective-permute-start.3 = (bf16[2048,128]{1,0:T(8,128)(2,1)S(1)}, bf16[2048,128]{1,0:T(8,128)(2,1)S(1)}, u32[]{:S(2)}, u32[]{:S(2)}) collective-permute-start(bf16[2048,128]{1,0:T(8,128)(2,1)S(1)} %get-tuple-element.23.refs_0_), channel_id=1, source_target_pairs={{0,4},{1,5},{2,6},{3,7},{4,0},{5,1},{6,2},{7,3},{8,12},{9,13},{10,... | collective-permute-start | bytes 1572872 | tf_op jit(solution)/shard_map/ppermute | solution.py:488
  10.3 29.0 %copy-start = (bf16[64,128,128]{2,1,0:T(8,128)(2,1)S(1)}, bf16[64,128,128]{2,1,0:T(8,128)(2,1)}, u32[]{:S(2)}) copy-start(bf16[64,128,128]{2,1,0:T(8,128)(2,1)} %ob_ref.1) | copy-start | bytes 6291460
  10.3 29.0 %copy-start.4 = (bf16[16,128,128]{2,1,0:T(8,128)(2,1)S(1)}, bf16[16,128,128]{2,1,0:T(8,128)(2,1)}, u32[]{:S(2)}) copy-start(bf16[16,128,128]{2,1,0:T(8,128)(2,1)} %ib_ref.1) | copy-start | bytes 1572868
  10.3 29.0 %copy-start.13 = (bf16[8,2,512,256]{3,2,1,0:T(8,128)(2,1)S(1)}, bf16[8,2,512,256]{3,2,1,0:T(8,128)(2,1)}, u32[]{:S(2)}) copy-start(bf16[8,2,512,256]{3,2,1,0:T(8,128)(2,1)} %q_ref.1) | copy-start | bytes 12582916
  10.3 3.3 %collective-permute-start.6 = (f32[8,128]{1,0:T(8,128)S(1)}, f32[8,128]{1,0:T(8,128)S(1)}, u32[]{:S(2)}, u32[]{:S(2)}) collective-permute-start(f32[8,128]{1,0:T(8,128)S(1)} %sum_eigenvalues.1), channel_id=1, source_target_pairs={{0,1},{1,0},{2,3},{3,2},{4,5},{5,4},{6,7},{7,6},{8,9},{9,8},{10,11... | collective-permute-start | bytes 12296 | tf_op jit(solution)/shard_map/ppermute | solution.py:488
  13.6 15.6 %collective-permute-start.7 = (f32[8,128]{1,0:T(8,128)S(1)}, f32[8,128]{1,0:T(8,128)S(1)}, u32[]{:S(2)}, u32[]{:S(2)}) collective-permute-start(f32[8,128]{1,0:T(8,128)S(1)} %hold.2), channel_id=1, source_target_pairs={{0,2},{1,3},{2,0},{3,1},{4,6},{5,7},{6,4},{7,5},{8,10},{9,11},{10,... | collective-permute-start | bytes 12296 | tf_op jit(solution)/shard_map/ppermute | solution.py:488
  29.2 3.6 %collective-permute-start.8 = (f32[8,128]{1,0:T(8,128)S(1)}, f32[8,128]{1,0:T(8,128)S(1)}, u32[]{:S(2)}, u32[]{:S(2)}) collective-permute-start(f32[8,128]{1,0:T(8,128)S(1)} %add.34), channel_id=1, source_target_pairs={{0,4},{1,5},{2,6},{3,7},{4,0},{5,1},{6,2},{7,3},{8,12},{9,13},{10,... | collective-permute-start | bytes 12296 | tf_op jit(solution)/shard_map/ppermute | solution.py:488
  33.0 6.3 %collective-permute-start.9 = (f32[8,128]{1,0:T(8,128)S(1)}, f32[8,128]{1,0:T(8,128)S(1)}, u32[]{:S(2)}, u32[]{:S(2)}) collective-permute-start(f32[8,128]{1,0:T(8,128)S(1)} %hold.3), channel_id=1, source_target_pairs={{0,8},{1,9},{2,10},{3,11},{4,12},{5,13},{6,14},{7,15},{8,0},{9,1},... | collective-permute-start | bytes 12296 | tf_op jit(solution)/shard_map/ppermute | solution.py:488
  35.8 20.9 %collective-permute-start.2 = (bf16[2048,128]{1,0:T(8,128)(2,1)S(1)}, bf16[2048,128]{1,0:T(8,128)(2,1)S(1)}, u32[]{:S(2)}, u32[]{:S(2)}) collective-permute-start(bf16[2048,128]{1,0:T(8,128)(2,1)S(1)} %collective-permute-done.1.refs_1_.refs_3_.refs_0_.refs_5_), channel_id=1, source_target_pairs={{0,4},{1,5},{2,6},{3,7},{4,0},{5,1},{6,2},{7,3},{8,12},{9,13},{10,... | collective-permute-start | bytes 1572872 | tf_op jit(solution)/shard_map/ppermute | solution.py:488
  37.4 24.5 %collective-permute-start.4 = (bf16[4096,128]{1,0:T(8,128)(2,1)S(1)}, bf16[4096,128]{1,0:T(8,128)(2,1)S(1)}, u32[]{:S(2)}, u32[]{:S(2)}) collective-permute-start(bf16[4096,128]{1,0:T(8,128)(2,1)S(1)} %get-tuple-element.26.refs_0_), channel_id=1, source_target_pairs={{0,2},{1,3},{2,0},{3,1},{4,6},{5,7},{6,4},{7,5},{8,10},{9,11},{10,... | collective-permute-start | bytes 3145736 | tf_op jit(solution)/shard_map/ppermute | solution.py:488
  38.9 23.0 %collective-permute-start.5 = (bf16[2048,128]{1,0:T(8,128)(2,1)S(1)}, bf16[2048,128]{1,0:T(8,128)(2,1)S(1)}, u32[]{:S(2)}, u32[]{:S(2)}) collective-permute-start(bf16[2048,128]{1,0:T(8,128)(2,1)S(1)} %get-tuple-element.28), channel_id=1, source_target_pairs={{0,8},{1,9},{2,10},{3,11},{4,12},{5,13},{6,14},{7,15},{8,0},{9,1},... | collective-permute-start | bytes 1572872 | tf_op jit(solution)/shard_map/ppermute | solution.py:488
  45.9 23.3 %collective-permute-start.10 = (bf16[2,512,2048]{2,1,0:T(8,128)(2,1)}, bf16[2,512,2048]{2,1,0:T(8,128)(2,1)}, u32[]{:S(2)}, u32[]{:S(2)}) collective-permute-start(bf16[2,512,2048]{2,1,0:T(8,128)(2,1)} %precondition.1.own_ref.refs_9_), channel_id=1, source_target_pairs={{0,1},{1,0},{2,3},{3,2},{4,5},{5,4},{6,7},{7,6},{8,9},{9,8},{10,11... | collective-permute-start | bytes 12582920 | tf_op jit(solution)/shard_map/ppermute | solution.py:488
  56.8 6.4 %copy-start.7 = (bf16[2048,128]{1,0:T(8,128)(2,1)}, bf16[2048,128]{1,0:T(8,128)(2,1)S(1)}, u32[]{:S(2)}) copy-start(bf16[2048,128]{1,0:T(8,128)(2,1)S(1)} %collective-permute-done.2.refs_2_.refs_0_.refs_7_) | copy-start | bytes 1572868
  61.9 1.2 %copy-start.9 = (bf16[2048,128]{1,0:T(8,128)(2,1)}, bf16[2048,128]{1,0:T(8,128)(2,1)S(1)}, u32[]{:S(2)}) copy-start(bf16[2048,128]{1,0:T(8,128)(2,1)S(1)} %collective-permute-done.5.refs_7_.refs_1_.refs_6_) | copy-start | bytes 1572868
  61.9 1.6 %copy-start.2 = (bf16[4096,128]{1,0:T(8,128)(2,1)}, bf16[4096,128]{1,0:T(8,128)(2,1)S(1)}, u32[]{:S(2)}) copy-start(bf16[4096,128]{1,0:T(8,128)(2,1)S(1)} %collective-permute-done.4.refs_4_.refs_8_) | copy-start | bytes 3145732
  61.9 6.9 %copy-start.14 = (s32[16]{0:T(128)S(1)}, s32[16]{0:T(128)}, u32[]{:S(2)}) copy-start(s32[16]{0:T(128)} %param.13) | copy-start | bytes 196
  63.5 19.7 %collective-permute-start.11 = (bf16[3072,128]{1,0:T(8,128)(2,1)}, bf16[3072,128]{1,0:T(8,128)(2,1)S(1)}, u32[]{:S(2)}, u32[]{:S(2)}) collective-permute-start(bf16[3072,128]{1,0:T(8,128)(2,1)} %get-tuple-element.36), channel_id=1, source_target_pairs={{0,2},{1,3},{2,0},{3,1},{4,6},{5,7},{6,4},{7,5},{8,10},{9,11},{10,... | collective-permute-start | bytes 2359304 | tf_op jit(solution)/shard_map/ppermute | solution.py:488
  64.0 22.4 %collective-permute-start.12 = (bf16[2048,128]{1,0:T(8,128)(2,1)}, bf16[2048,128]{1,0:T(8,128)(2,1)S(1)}, u32[]{:S(2)}, u32[]{:S(2)}) collective-permute-start(bf16[2048,128]{1,0:T(8,128)(2,1)} %get-tuple-element.38), channel_id=1, source_target_pairs={{0,4},{1,5},{2,6},{3,7},{4,0},{5,1},{6,2},{7,3},{8,12},{9,13},{10,... | collective-permute-start | bytes 1572872 | tf_op jit(solution)/shard_map/ppermute | solution.py:488
  64.0 21.5 %collective-permute-start.13 = (bf16[1024,128]{1,0:T(8,128)(2,1)}, bf16[1024,128]{1,0:T(8,128)(2,1)}, u32[]{:S(2)}, u32[]{:S(2)}) collective-permute-start(bf16[1024,128]{1,0:T(8,128)(2,1)} %get-tuple-element.39), channel_id=1, source_target_pairs={{0,12},{1,13},{2,14},{3,15},{4,8},{5,9},{6,10},{7,11},{8,4},{9,5},... | collective-permute-start | bytes 786440 | tf_op jit(solution)/shard_map/ppermute | solution.py:488
  66.1 20.3 %collective-permute-start.14 = (bf16[1024,128]{1,0:T(8,128)(2,1)}, bf16[1024,128]{1,0:T(8,128)(2,1)}, u32[]{:S(2)}, u32[]{:S(2)}) collective-permute-start(bf16[1024,128]{1,0:T(8,128)(2,1)} %get-tuple-element.40), channel_id=1, source_target_pairs={{0,14},{1,15},{2,12},{3,13},{4,10},{5,11},{6,8},{7,9},{8,6},{9,7},... | collective-permute-start | bytes 786440 | tf_op jit(solution)/shard_map/ppermute | solution.py:488
  69.2 3.8 %copy-start.3 = (bf16[4096,128]{1,0:T(8,128)(2,1)S(1)}, bf16[4096,128]{1,0:T(8,128)(2,1)}, u32[]{:S(2)}) copy-start(bf16[4096,128]{1,0:T(8,128)(2,1)} %copy-done.2) | copy-start | bytes 3145732
  69.2 3.8 %copy-start.6 = (bf16[2048,128]{1,0:T(8,128)(2,1)S(1)}, bf16[2048,128]{1,0:T(8,128)(2,1)}, u32[]{:S(2)}) copy-start(bf16[2048,128]{1,0:T(8,128)(2,1)} %copy-done.5) | copy-start | bytes 1572868
  69.2 4.0 %copy-start.8 = (bf16[2048,128]{1,0:T(8,128)(2,1)S(1)}, bf16[2048,128]{1,0:T(8,128)(2,1)}, u32[]{:S(2)}) copy-start(bf16[2048,128]{1,0:T(8,128)(2,1)} %copy-done.7) | copy-start | bytes 1572868
  69.3 4.1 %copy-start.10 = (bf16[2048,128]{1,0:T(8,128)(2,1)S(1)}, bf16[2048,128]{1,0:T(8,128)(2,1)}, u32[]{:S(2)}) copy-start(bf16[2048,128]{1,0:T(8,128)(2,1)} %copy-done.9) | copy-start | bytes 1572868
  69.3 4.2 %copy-start.12 = (bf16[1024,128]{1,0:T(8,128)(2,1)S(1)}, bf16[1024,128]{1,0:T(8,128)(2,1)}, u32[]{:S(2)}) copy-start(bf16[1024,128]{1,0:T(8,128)(2,1)} %copy-done.11) | copy-start | bytes 786436
  88.2 1.1 %collective-permute-start.15 = (f32[2,16]{1,0:T(2,128)S(1)}, f32[2,16]{1,0:T(2,128)S(1)}, u32[]{:S(2)}, u32[]{:S(2)}) collective-permute-start(f32[2,16]{1,0:T(2,128)S(1)} %reduce_sum.9), channel_id=1, source_target_pairs={{0,1},{1,0},{2,3},{3,2},{4,5},{5,4},{6,7},{7,6},{8,9},{9,8},{10,11... | collective-permute-start | bytes 392 | tf_op jit(solution)/shard_map/ppermute | solution.py:488
  89.4 3.6 %collective-permute-start.16 = (f32[2,16]{1,0:T(2,128)S(1)}, f32[2,16]{1,0:T(2,128)S(1)}, u32[]{:S(2)}, u32[]{:S(2)}) collective-permute-start(f32[2,16]{1,0:T(2,128)S(1)} %add.37), channel_id=1, source_target_pairs={{0,2},{1,3},{2,0},{3,1},{4,6},{5,7},{6,4},{7,5},{8,10},{9,11},{10,... | collective-permute-start | bytes 392 | tf_op jit(solution)/shard_map/ppermute | solution.py:488
  92.9 3.6 %collective-permute-start.17 = (f32[2,16]{1,0:T(2,128)S(1)}, f32[2,16]{1,0:T(2,128)S(1)}, u32[]{:S(2)}, u32[]{:S(2)}) collective-permute-start(f32[2,16]{1,0:T(2,128)S(1)} %add.38), channel_id=1, source_target_pairs={{0,4},{1,5},{2,6},{3,7},{4,0},{5,1},{6,2},{7,3},{8,12},{9,13},{10,... | collective-permute-start | bytes 392 | tf_op jit(solution)/shard_map/ppermute | solution.py:488
  96.5 4.5 %collective-permute-start.18 = (f32[2,16]{1,0:T(2,128)S(1)}, f32[2,16]{1,0:T(2,128)S(1)}, u32[]{:S(2)}, u32[]{:S(2)}) collective-permute-start(f32[2,16]{1,0:T(2,128)S(1)} %add.39), channel_id=1, source_target_pairs={{0,8},{1,9},{2,10},{3,11},{4,12},{5,13},{6,14},{7,15},{8,0},{9,1},... | collective-permute-start | bytes 392 | tf_op jit(solution)/shard_map/ppermute | solution.py:488

commit v4 on v2

--- a/solution.py
+++ b/solution.py
@@ -10,6 +10,8 @@
 
 VMEM_LIMIT = 16 * 1024 * 1024
 COST_PRE = 10**11
+COST_K1 = 1
+COST_KG = 10**11
 COST_K3 = 10**11
 F32 = jnp.float32
 BF16 = jnp.bfloat16
@@ -118,52 +120,17 @@
     return pltpu.with_memory_space_constraint(value, pltpu.HBM)
 
 
-def rotate_inputs(layer_inputs, in_basis):
-    tokens, features = layer_inputs.shape
-    count, width, _ = in_basis.shape
-
-    def body(x_hbm, b_hbm, o_ref, x_all, b_all, sems):
-        copies = [
-            pltpu.make_async_copy(x_hbm, x_all, sems.at[0]),
-            pltpu.make_async_copy(b_hbm, b_all, sems.at[1]),
-        ]
-        for copy in copies:
-            copy.start()
-        for copy in copies:
-            copy.wait()
-        for n in range(count):
-            span = slice(n * width, (n + 1) * width)
-            turned = jnp.dot(x_all[:, span], b_all[n], preferred_element_type=F32)
-            o_ref[span, :] = turned.astype(BF16).T
-
-    hbm = pl.BlockSpec(memory_space=pl.ANY)
-    return call(
-        body,
-        in_specs=[hbm, hbm],
-        out_specs=pl.BlockSpec(memory_space=pltpu.VMEM),
-        out_shape=jax.ShapeDtypeStruct((features, tokens), BF16),
-        scratch_shapes=[
-            pltpu.VMEM((tokens, features), BF16),
-            pltpu.VMEM((count, width, width), BF16),
-            pltpu.SemaphoreType.DMA((2,)),
-        ],
-        name="rotate_inputs",
-    )(in_hbm(layer_inputs), in_hbm(in_basis))
-
-
-def rotate_grads(output_grads, out_basis, chip, chips, layouts, sources=(), after=(), cost=1):
+def rotate(output_grads, out_basis, chip, chips, layouts, after=(), cost=1):
     tokens, units = output_grads.shape
     width = out_basis.shape[1]
     part = units // chips
     per = part // width
-    offsets = [k for layout in layouts for k in layout if isinstance(k, int)]
+    offsets = [k for layout in layouts for k in layout]
     count = len(offsets)
-    heights = [sum(part if isinstance(k, int) else k[2] for k in layout) for layout in layouts]
-    extra = list(sources) + list(after)
 
     def body(chip_ref, g_hbm, b_hbm, *refs):
-        o_refs = refs[len(extra) : len(extra) + len(layouts)]
-        g_all, b_all, g_sems, b_sems = refs[len(extra) + len(layouts) :]
+        o_refs = refs[len(after) : len(after) + len(layouts)]
+        g_all, b_all, g_sems, b_sems = refs[len(after) + len(layouts) :]
         copies = []
         for n, k in enumerate(offsets):
             place = chip_ref[0] ^ k
@@ -180,40 +147,126 @@
                 copy.start()
         n = 0
         for o_ref, layout in zip(o_refs, layouts):
-            top = 0
-            for k in layout:
-                if not isinstance(k, int):
-                    source, first, rows = k
-                    o_ref[top : top + rows, :] = refs[source][first : first + rows, :]
-                    top += rows
-                    continue
+            for top in range(len(layout)):
                 for copy in copies[n]:
                     copy.wait()
                 for i in range(per):
                     span = slice(i * width, (i + 1) * width)
+                    first = top * part + i * width
                     turned = jnp.dot(g_all[n, :, span], b_all[n, i], preferred_element_type=F32)
-                    o_ref[top + i * width : top + (i + 1) * width, :] = turned.astype(BF16).T
-                top += part
+                    o_ref[first : first + width, :] = turned.astype(BF16).T
                 n += 1
 
     hbm = pl.BlockSpec(memory_space=pl.ANY)
     vmem = pl.BlockSpec(memory_space=pltpu.VMEM)
     return call(
         body,
-        in_specs=[pl.BlockSpec(memory_space=pltpu.SMEM), hbm, hbm]
-        + [vmem] * len(sources)
-        + [hbm] * len(after),
+        cost=cost,
+        in_specs=[pl.BlockSpec(memory_space=pltpu.SMEM), hbm, hbm] + [hbm] * len(after),
         out_specs=[vmem] * len(layouts),
-        out_shape=[jax.ShapeDtypeStruct((h, tokens), BF16) for h in heights],
+        out_shape=[jax.ShapeDtypeStruct((part * len(l), tokens), BF16) for l in layouts],
         scratch_shapes=[
             pltpu.VMEM((count, tokens, part), BF16),
             pltpu.VMEM((count, per, width, width), BF16),
             pltpu.SemaphoreType.DMA((count,)),
             pltpu.SemaphoreType.DMA((count,)),
         ],
-        name="rotate_grads",
-        cost=cost,
-    )(chip[None], output_grads, out_basis, *extra)
+        name="rotate",
+    )(chip[None], in_hbm(output_grads), in_hbm(out_basis), *after)
+
+
+def turn(x_ref, first, tokens, basis_ref, o_ref, left=0, cut=None, rest_ref=None):
+    count, width, _ = basis_ref.shape
+    for i in range(count):
+        span = slice(i * width, (i + 1) * width)
+        turned = jnp.dot(
+            x_ref[first : first + tokens, span], basis_ref[i], preferred_element_type=F32
+        )
+        turned = turned.astype(BF16).T
+        if cut is None or i * width < cut:
+            o_ref[span, left : left + tokens] = turned
+        else:
+            rest_ref[i * width - cut : (i + 1) * width - cut, :] = turned
+
+
+def pair_up(a, b, held, after):
+    def body(a_ref, b_ref, *refs):
+        o_ref = refs[1 + len(after)]
+        o_ref[: a.shape[0], :] = a_ref[...]
+        o_ref[a.shape[0] :, :] = b_ref[...]
+
+    anywhere = pl.BlockSpec(memory_space=pl.ANY)
+    vmem = pl.BlockSpec(memory_space=pltpu.VMEM)
+    return call(
+        body,
+        in_specs=[vmem, vmem] + [anywhere] * (1 + len(after)),
+        out_specs=[vmem, anywhere],
+        out_shape=[
+            jax.ShapeDtypeStruct((a.shape[0] + b.shape[0], a.shape[1]), a.dtype),
+            jax.ShapeDtypeStruct(held.shape, held.dtype),
+        ],
+        input_output_aliases={2: 1},
+        name="pair_up",
+    )(a, b, held, *after)
+
+
+def pack_grads(near, far, across):
+    part, tokens = near.shape
+
+    def body(n_ref, f_ref, a_ref, near_ref, far_ref, sems):
+        top, low = pl.ds(0, part), pl.ds(part, part)
+        copies = [
+            pltpu.make_async_copy(n_ref, near_ref.at[top], sems.at[0]),
+            pltpu.make_async_copy(a_ref.at[low], near_ref.at[low], sems.at[1]),
+            pltpu.make_async_copy(f_ref, far_ref.at[top], sems.at[2]),
+            pltpu.make_async_copy(a_ref.at[pl.ds(2 * part, part)], far_ref.at[low], sems.at[3]),
+        ]
+        for copy in copies:
+            copy.start()
+        for copy in copies:
+            copy.wait()
+
+    anywhere = pl.BlockSpec(memory_space=pl.ANY)
+    vmem = pl.BlockSpec(memory_space=pltpu.VMEM)
+    return call(
+        body,
+        in_specs=[anywhere] * 3,
+        out_specs=[vmem] * 2,
+        out_shape=[jax.ShapeDtypeStruct((2 * part, tokens), BF16)] * 2,
+        scratch_shapes=[pltpu.SemaphoreType.DMA((4,))],
+        name="pack_grads",
+    )(near, far, across)
+
+
+def last_round(x, middle, in_basis, cut, after):
+    tokens = x.shape[0]
+    count, width, _ = in_basis.shape
+    features = count * width
+    part = middle.shape[0] // 2
+
+    def body(x_ref, m_ref, b_ref, *refs):
+        high_ref, low_ref, sem = refs[len(after) :]
+        copy = pltpu.make_async_copy(
+            m_ref.at[pl.ds(part, part)], low_ref.at[pl.ds(features - cut, part)], sem
+        )
+        copy.start()
+        turn(x_ref, 0, tokens, b_ref, high_ref, 0, cut, low_ref)
+        copy.wait()
+
+    anywhere = pl.BlockSpec(memory_space=pl.ANY)
+    vmem = pl.BlockSpec(memory_space=pltpu.VMEM)
+    return call(
+        body,
+        cost=COST_K3,
+        in_specs=[vmem, anywhere, vmem] + [anywhere] * len(after),
+        out_specs=[vmem] * 2,
+        out_shape=[
+            jax.ShapeDtypeStruct((cut, tokens), BF16),
+            jax.ShapeDtypeStruct((features - cut + part, tokens), BF16),
+        ],
+        scratch_shapes=[pltpu.SemaphoreType.DMA],
+        name="last_round",
+    )(x, middle, in_basis, *after)
 
 
 def sum_eigenvalues(eigenvalues):
@@ -240,18 +293,18 @@
     )(eigenvalues)
 
 
-def add_after(a, b, *after):
-    def body(a_ref, b_ref, *refs):
-        refs[-1][...] = a_ref[...] + b_ref[...]
-
-    vmem = pl.BlockSpec(memory_space=pltpu.VMEM)
-    return call(
-        body,
-        in_specs=[vmem, vmem] + [pl.BlockSpec(memory_space=pl.ANY)] * len(after),
+def hold(value, *after):
+    def body(v_ref, *refs):
+        refs[-1][...] = v_ref[...]
+
+    vmem = pl.BlockSpec(memory_space=pltpu.VMEM)
+    return call(
+        body,
+        in_specs=[vmem] + [pl.BlockSpec(memory_space=pl.ANY)] * len(after),
         out_specs=vmem,
-        out_shape=jax.ShapeDtypeStruct(a.shape, a.dtype),
-        name="add_after",
-    )(a, b, *after)
+        out_shape=jax.ShapeDtypeStruct(value.shape, value.dtype),
+        name="hold",
+    )(value, *after)
 
 
 def block_diagonal(blocks):
@@ -326,80 +379,198 @@
     )(me[None], query_grads, eigenvalues, sums, out_basis, in_basis, *after)
 
 
-def join_rows(own, sibling, core, after):
-    def body(core_ref, own_ref, sib_ref, *refs):
-        o_ref, sems = refs[len(after) :]
+def join_and_tally(where, turned_piece, pieces, early, in_basis, own, sibling, starts, ends, order):
+    queries, rows, features = own.shape
+    docs, tokens = starts.shape
+    width = in_basis.shape[1]
+    block = math.gcd(rows, 512)
+    all_pieces = [turned_piece] + list(pieces)
+    count = len(all_pieces)
+    raw = [x for x, _ in pieces] + list(early)
+    cut = turned_piece[0][0].shape[0]
+    raw_place = [next(i for i, o in enumerate(order) if o is x) for x, _ in raw]
+    heights = [array.shape[0] for array in order]
+    tops = [sum(heights[:i]) for i in range(len(heights))]
+    grads = [g for _, (g, _) in all_pieces]
+    operands = list(order) + [in_hbm(in_basis), *turned_piece[0]]
+    operands += [in_hbm(g) for g in grads] + [own, sibling, starts, ends]
+
+    def body(where_ref, *refs):
+        raw_refs = refs[: len(order)]
+        basis_hbm, high_hbm, low_hbm = refs[len(order) : len(order) + 3]
+        g_hbm = refs[len(order) + 3 : len(order) + 3 + count]
+        own_ref, sib_ref, st_ref, en_ref, o_ref, both_ref = refs[
+            len(order) + 3 + count : len(operands) + 2
+        ]
+        t_refs = refs[len(operands) + 2 : -7]
+        raw_all, basis_ref, x_all, g_all, x_sems, g_sems, p_sems = refs[-7:]
+        x_copies = [pltpu.make_async_copy(basis_hbm, basis_ref, x_sems.at[len(order)])]
+        x_copies += [
+            pltpu.make_async_copy(
+                raw_refs[i], raw_all.at[pl.ds(tops[i], heights[i])], x_sems.at[i]
+            )
+            for i in range(len(order))
+        ]
         copies = [
-            pltpu.make_async_copy(own_ref, o_ref.at[core_ref[0]], sems.at[0]),
-            pltpu.make_async_copy(sib_ref, o_ref.at[1 - core_ref[0]], sems.at[1]),
-        ]
-        for copy in copies:
+            [
+                pltpu.make_async_copy(p_ref.at[q], both_ref.at[c, q], p_sems.at[c, q])
+                for q in range(queries)
+            ]
+            for c, p_ref in enumerate((own_ref, sib_ref))
+        ]
+        x_copies += [
+            pltpu.make_async_copy(
+                high_hbm, x_all.at[pl.ds(0, cut), pl.ds(0, tokens)], x_sems.at[len(order) + 1]
+            ),
+            pltpu.make_async_copy(
+                low_hbm.at[pl.ds(0, features - cut)],
+                x_all.at[pl.ds(cut, features - cut), pl.ds(0, tokens)],
+                x_sems.at[len(order) + 2],
+            ),
+        ]
+        g_copies = [
+            pltpu.make_async_copy(
+                g_hbm[n].at[pl.ds(all_pieces[n][1][1], 2 * rows)], g_all.at[n], g_sems.at[n]
+            )
+            for n in range(count)
+        ]
+        for copy in x_copies:
             copy.start()
-        for copy in copies:
+        copies[0][0].start()
+        for copy in g_copies:
+            copy.start()
+        for c in range(2):
+            for q in range(queries):
+                if c or q:
+                    copies[c][q].start()
+        for copy in x_copies:
             copy.wait()
+        for n, (_, first) in enumerate(raw):
+            turn(raw_all, tops[raw_place[n]] + first, tokens, basis_ref, x_all, (n + 1) * tokens)
+        scores = [[jnp.zeros((1, tokens), F32)] * queries for _ in all_pieces]
+        for c in range(2):
+            core = where_ref[0] if c == 0 else 1 - where_ref[0]
+            for q in range(queries):
+                copies[c][q].wait()
+                if c == 0 and q == 0:
+                    for copy in g_copies:
+                        copy.wait()
+                for r in range(0, rows, block):
+                    turned = jnp.dot(
+                        both_ref[c, q, r : r + block, :], x_all[...], preferred_element_type=F32
+                    )
+                    for n, t_ref in enumerate(t_refs):
+                        left = (count + n) * tokens
+                        t_ref[c, q, r : r + block, :] = turned[:, left : left + tokens]
+                    for n in range(count):
+                        spot = pl.ds(pl.multiple_of(core * rows + r, block), block)
+                        scores[n][q] = scores[n][q] + jnp.sum(
+                            turned[:, n * tokens : (n + 1) * tokens]
+                            * g_all[n, spot, :].astype(F32),
+                            axis=0,
+                            keepdims=True,
+                        )
+        add_shares(where_ref, scores, None, st_ref, en_ref, o_ref)
 
     hbm = pl.BlockSpec(memory_space=pl.ANY)
-    return call(
-        body,
-        in_specs=[pl.BlockSpec(memory_space=pltpu.SMEM), hbm, hbm] + [hbm] * len(after),
-        out_specs=pl.BlockSpec(memory_space=pltpu.VMEM),
-        out_shape=jax.ShapeDtypeStruct((2,) + own.shape, own.dtype),
-        scratch_shapes=[pltpu.SemaphoreType.DMA((2,))],
-        name="join_rows",
-    )(core[None], own, sibling, *after)
-
-
-def tally(where, pieces, both, starts, ends, running):
-    count = len(pieces)
+    vmem = pl.BlockSpec(memory_space=pltpu.VMEM)
+    kept = jax.ShapeDtypeStruct((2, queries, rows, tokens), F32)
+    return call(
+        body,
+        in_specs=[pl.BlockSpec(memory_space=pltpu.SMEM)]
+        + [hbm] * (len(order) + 3 + count)
+        + [hbm, hbm, vmem, vmem],
+        out_specs=[vmem] * (2 + len(early)),
+        out_shape=[
+            jax.ShapeDtypeStruct((queries, docs, tokens), F32),
+            jax.ShapeDtypeStruct((2,) + own.shape, own.dtype),
+        ]
+        + [kept] * len(early),
+        scratch_shapes=[
+            pltpu.VMEM((sum(heights), features), BF16),
+            pltpu.VMEM(in_basis.shape, BF16),
+            pltpu.VMEM((features, (count + len(early)) * tokens), BF16),
+            pltpu.VMEM((count, 2 * rows, tokens), BF16),
+            pltpu.SemaphoreType.DMA((len(order) + 3,)),
+            pltpu.SemaphoreType.DMA((count,)),
+            pltpu.SemaphoreType.DMA((2, queries)),
+        ],
+        name="join_and_tally",
+    )(where, *operands)
+
+
+def add_shares(where_ref, scores, run_ref, st_ref, en_ref, o_ref):
+    docs, tokens = st_ref.shape
+    for q in range(len(scores[0])):
+        total = jnp.zeros((docs, tokens), F32) if run_ref is None else run_ref[q]
+        for n in range(len(scores)):
+            spot = where_ref[1 + n] * tokens + lax.broadcasted_iota(jnp.int32, (docs, tokens), 1)
+            inside = (spot >= st_ref[...]) & (spot < en_ref[...])
+            total = total + jnp.where(inside, scores[n][q], 0.0)
+        o_ref[q] = total
+
+
+def project(high, low, both, after):
     cores, queries, rows, features = both.shape
-    tokens = starts.shape[1]
+    cut, tokens = high.shape
     block = math.gcd(rows, 512)
-    docs = starts.shape[0]
-    arrays = []
-    places = []
-    for piece in pieces:
-        for array, _ in piece:
-            if not any(array is other for other in arrays):
-                arrays.append(array)
-        places.append([next(i for i, o in enumerate(arrays) if o is a) for a, _ in piece])
-
-    def body(where_ref, *refs):
-        p_ref, st_ref, en_ref, run_ref, o_ref, x_all = refs[len(arrays) :]
-        for n in range(count):
-            first = pieces[n][0][1]
-            x_all[:, n * tokens : (n + 1) * tokens] = refs[places[n][0]][first : first + features, :]
-        scores = [[jnp.zeros((1, tokens), F32)] * queries for _ in range(count)]
+
+    def body(h_ref, l_ref, p_ref, *refs):
+        x_all = refs[-1]
+        x_all[:cut, :] = h_ref[...]
+        x_all[cut:, :] = l_ref[: features - cut, :]
         for c in range(cores):
             for q in range(queries):
                 for r in range(0, rows, block):
-                    turned = jnp.dot(
-                        p_ref[c, q, r : r + block, :], x_all[...], preferred_element_type=F32
+                    span = slice(r, r + block)
+                    refs[-2][c, q, span, :] = jnp.dot(
+                        p_ref[c, q, span, :], x_all[...], preferred_element_type=F32
                     )
-                    for n in range(count):
-                        first = pieces[n][1][1] + c * rows + r
+
+    vmem = pl.BlockSpec(memory_space=pltpu.VMEM)
+    return call(
+        body,
+        in_specs=[vmem] * 3 + [pl.BlockSpec(memory_space=pl.ANY)] * len(after),
+        out_specs=vmem,
+        out_shape=jax.ShapeDtypeStruct((cores, queries, rows, tokens), F32),
+        scratch_shapes=[pltpu.VMEM((features, tokens), BF16)],
+        name="project",
+    )(high, low, both, *after)
+
+
+def tally(where, projected, grads, starts, ends, running, order):
+    cores, queries, rows, tokens = projected[0].shape
+    block = math.gcd(rows, 512)
+    arrays = list(order)
+    places = [next(i for i, o in enumerate(arrays) if o is array) for array, _ in grads]
+    held = len(projected)
+
+    def body(where_ref, *refs):
+        g_refs = refs[held : held + len(arrays)]
+        st_ref, en_ref, run_ref, o_ref = refs[held + len(arrays) :]
+        scores = [[jnp.zeros((1, tokens), F32)] * queries for _ in grads]
+        for c in range(cores):
+            core = where_ref[0] if c == 0 else 1 - where_ref[0]
+            for q in range(queries):
+                for r in range(0, rows, block):
+                    for n, (_, first) in enumerate(grads):
+                        spot = pl.ds(pl.multiple_of(core * rows + first + r, block), block)
                         scores[n][q] = scores[n][q] + jnp.sum(
-                            turned[:, n * tokens : (n + 1) * tokens]
-                            * refs[places[n][1]][first : first + block, :].astype(F32),
+                            refs[n][c, q, r : r + block, :]
+                            * g_refs[places[n]][spot, :].astype(F32),
                             axis=0,
                             keepdims=True,
                         )
-        for q in range(queries):
-            total = run_ref[q]
-            for n in range(count):
-                spot = where_ref[n] * tokens + lax.broadcasted_iota(jnp.int32, (docs, tokens), 1)
-                inside = (spot >= st_ref[...]) & (spot < en_ref[...])
-                total = total + jnp.where(inside, scores[n][q], 0.0)
-            o_ref[q] = total
-
-    vmem = pl.BlockSpec(memory_space=pltpu.VMEM)
-    return call(
-        body,
-        in_specs=[pl.BlockSpec(memory_space=pltpu.SMEM)] + [vmem] * (len(arrays) + 4),
+        add_shares(where_ref, scores, run_ref, st_ref, en_ref, o_ref)
+
+    vmem = pl.BlockSpec(memory_space=pltpu.VMEM)
+    return call(
+        body,
+        in_specs=[pl.BlockSpec(memory_space=pltpu.SMEM)] + [vmem] * (held + len(arrays) + 3),
         out_specs=vmem,
         out_shape=jax.ShapeDtypeStruct(running.shape, F32),
-        scratch_shapes=[pltpu.VMEM((features, count * tokens), BF16)],
         name="tally",
-    )(where, *arrays, both, starts, ends, running)
+    )(where, *projected, *arrays, starts, ends, running)
 
 
 def local_rows(
@@ -419,61 +590,71 @@
 
     features = layer_inputs.shape[1]
     part = output_grads.shape[1] // chips
-    x = rotate_inputs(layer_inputs, in_basis)
-    rotate = functools.partial(rotate_grads, in_hbm(output_grads), in_hbm(out_basis), chip, chips)
-    side, near_side_g, g_own = rotate([[(0, 0, features), 1], [3], [0]], [x])
-    far_x = swap(x, 12)
-    near_x = swap(x, 4)
-    side = swap(side, 2)
-    near_side_g = swap(near_side_g, 6)
-    first = [far_x, near_x, side, near_side_g]
-
+    spin = functools.partial(rotate, output_grads, out_basis, chip, chips)
+    far_x = swap(layer_inputs, 12)
+    near_x = swap(layer_inputs, 4)
+    side_x = swap(layer_inputs, 2)
     sums = sum_eigenvalues(eigenvalues)
-    for offset in (1, 2, 4, 8):
+    (side_g,) = spin([[1, 3, 7]], [sums], cost=COST_K1)
+    side_g = swap(side_g, 2)
+
+    g_own, middle, g_far, near_g = spin([[0], [4, 5], [6], [2]], cost=COST_KG)
+    sums = sums + swap(sums, 2)
+    sums = hold(sums, middle)
+    for offset in (1, 4):
         sums = sums + swap(sums, offset)
 
-    (middle,) = rotate([[4, 5]], [], first)
+    sides_sent, middle = pair_up(near_x, far_x, middle, [side_x])
     middle = swap(middle, 8)
     middle_x = swap(far_x, 4)
-    near_x_side = swap(near_x, 2)
-    far_x_side = swap(far_x, 2)
-    second = [middle, middle_x, near_x_side, far_x_side]
-
+    sides = swap(sides_sent, 2)
+
+    sums = hold(sums, sides_sent)
+    sums = sums + swap(sums, 8)
     own = precondition_rows(
-        query_grads, eigenvalues, sums, out_basis, in_basis, me, entries, first
-    )
-    both = join_rows(own, swap(own, 1), core, second)
-
-    middle_side, g_far, g_far_side, near_g = rotate(
-        [[(0, 0, features), (1, part, part)], [6], [7], [2]],
-        [middle_x, middle],
-        second + [own],
-        cost=COST_K3,
-    )
-    middle_side = swap(middle_side, 2)
+        query_grads, eigenvalues, sums, out_basis, in_basis, me, entries, [near_x, far_x, side_x, side_g]
+    )
+    sibling = swap(own, 1)
+
+    near_g, g_far = pack_grads(near_g, g_far, side_g)
+    near_g = swap(near_g, 4)
     g_far = swap(g_far, 12)
-    g_far_side = swap(g_far_side, 14)
-    near_g = swap(near_g, 4)
+    cut = features * 3 // 4
+    turned = last_round(middle_x, middle, in_basis, cut, [sides, own])
+    high, low = [swap(value, 2) for value in turned]
 
     doc_ends = jnp.cumsum(doc_lengths)
     doc_starts = doc_ends - doc_lengths
     docs = doc_lengths.shape[0]
     starts = jnp.broadcast_to(doc_starts[:, None], (docs, tokens))
     ends = jnp.broadcast_to(doc_ends[:, None], (docs, tokens))
-    running = jnp.zeros((queries, docs, tokens), F32)
-    pieces = {
-        0: ((x, 0), (g_own, 0)),
-        1: ((side, 0), (side, features)),
-        2: ((near_x, 0), (near_g, 0)),
-        3: ((near_x_side, 0), (near_side_g, 0)),
-        4: ((middle_x, 0), (middle, 0)),
-        5: ((middle_side, 0), (middle_side, features)),
-        6: ((far_x, 0), (g_far, 0)),
-        7: ((far_x_side, 0), (g_far_side, 0)),
-    }
-    for some in ((0, 1, 3, 4), (2, 6), (5, 7)):
-        where = jnp.stack([me ^ (2 * k) for k in some]).astype(jnp.int32)
-        running = tally(where, [pieces[k] for k in some], both, starts, ends, running)
+
+    def where(*offsets):
+        return jnp.stack([core] + [me ^ (2 * k) for k in offsets]).astype(jnp.int32)
+
+    layer_inputs = in_hbm(layer_inputs)
+    running, both, *kept = join_and_tally(
+        where(4, 0, 1),
+        (turned, (middle, 0)),
+        [((layer_inputs, 0), (g_own, 0)), ((side_x, 0), (side_g, 0))],
+        [(near_x, 0), (sides, 0), (far_x, 0), (sides, tokens)],
+        in_basis,
+        own,
+        sibling,
+        starts,
+        ends,
+        [layer_inputs, side_x, near_x, far_x, sides],
+    )
+    kept.append(project(high, low, both, [running]))
+    running = tally(
+        where(2, 3, 6, 7, 5),
+        kept,
+        [(near_g, 0), (near_g, part), (g_far, 0), (g_far, part), (low, features - cut)],
+        starts,
+        ends,
+        running,
+        [near_g, g_far, low],
+    )
     shares = jnp.sum(running, axis=2)
     for offset in (1, 2, 4, 8):
         shares = shares + swap(shares, offset)

time: 116 us -> 97.7 us (0.84)
  waiting for transfers between devices: 51.9 us -> 39.7 us
  starting transfers between devices: 28.9 us -> 20.4 us
  Pallas kernels: 31.5 us -> 33.6 us
    ppermute x21 -> x20, waiting for transfers between devices: 51.9 us -> 39.7 us  [swap(): return lax.ppermute(value, 'dp', [(i, i ^ offset) for i in range(devices)])]
    ppermute x21 -> x20, starting transfers between devices: 28.9 us -> 20.4 us  [swap(): return lax.ppermute(value, 'dp', [(i, i ^ offset) for i in range(devices)])]
    pallas_call x8 -> x10, Pallas kernels: 24.2 us -> 26.3 us  [the longest x1 13.6 us: join_and_tally(): call(body, in_specs=[pl.BlockSpec(memory_space=pltpu.SMEM)] + [hbm] * (le...]
  transfers between devices with their start and end apart: 21 -> 20, of which waited for: 13 -> 10; matrix products, arithmetic and copies ran while one was open for 1% -> 1% of each run, Pallas kernels for 21% -> 33%
where the time goes in v4:
time: 97.7 us; the launch traced here: 97.5 us
  waiting for transfers between devices  39.7 us (41%)
  Pallas kernels  33.6 us (34%)
  starting transfers between devices  20.4 us (21%)
  local copies, waits for them, and re-layouts  3.23 us (3%)
    ppermute x20, waiting for transfers between devices, swap(): return lax.ppermute(value, 'dp', [(i, i ^ offset) for i in range(devices)])  39.7 us
    ppermute x20, starting transfers between devices, swap(): return lax.ppermute(value, 'dp', [(i, i ^ offset) for i in range(devices)])  20.4 us
    pallas_call x1, Pallas kernels, join_and_tally(): call(body, in_specs=[pl.BlockSpec(memory_space=pltpu.SMEM)] + [hbm] * (le...  13.6 us
    pallas_call x1, Pallas kernels, precondition_rows(): call(body, grid_spec=grid_spec, out_shape=jax.ShapeDtypeStruct((queries,...  6.61 us
    pallas_call x2, Pallas kernels, rotate(): call(body, cost=cost, in_specs=[pl.BlockSpec(memory_space=pltpu.SMEM), hb...  5.18 us
    pallas_call x1, Pallas kernels, project(): call(body, in_specs=[vmem] * 3 + [pl.BlockSpec(memory_space=pl.ANY)] * le...  3.38 us
    unnamed x18, local copies, waits for them, and re-layouts  2.23 us
  transfers between devices with their start and end apart: 20, of which 10 were waited for; matrix products, arithmetic and copies ran while one was open for 1% of the time, Pallas kernels for 33%

profile of v4, /device:TPU:0, one launch (start us, length us, event | category | flops | bytes accessed | tf_op | source)
XLA Modules:
  0.0 97.5 jit_solution(7866691273423448546)
XLA Ops:
  0.0 5.0 %collective-permute-start.2 = (bf16[128,2048]{1,0:T(8,128)(2,1)}, bf16[128,2048]{1,0:T(8,128)(2,1)S(1)}, u32[]{:S(2)}, u32[]{:S(2)}) collective-permute-start(bf16[128,2048]{1,0:T(8,128)(2,1)} %refs_0_.1), channel_id=1, source_target_pairs={{0,12},{1,13},{2,14},{3,15},{4,8},{5,9},{6,10},{7,11},{8,4},{9,5},... | collective-permute-start | bytes 1572872 | tf_op jit(solution)/shard_map/ppermute | solution.py:589
  5.0 1.5 %collective-permute-start = (bf16[128,2048]{1,0:T(8,128)(2,1)}, bf16[128,2048]{1,0:T(8,128)(2,1)S(1)}, u32[]{:S(2)}, u32[]{:S(2)}) collective-permute-start(bf16[128,2048]{1,0:T(8,128)(2,1)} %refs_0_.1), channel_id=1, source_target_pairs={{0,2},{1,3},{2,0},{3,1},{4,6},{5,7},{6,4},{7,5},{8,10},{9,11},{10,... | collective-permute-start | bytes 1572872 | tf_op jit(solution)/shard_map/ppermute | solution.py:589
  6.6 2.2 %copy-done = f32[8,512,256]{2,1,0:T(8,128)S(1)} copy-done((f32[8,512,256]{2,1,0:T(8,128)S(1)}, f32[8,512,256]{2,1,0:T(8,128)}, u32[]{:S(2)}) %copy-start) | copy-done | bytes 4194328
  8.8 0.7 sum_eigenvalues.1.refs_0_
  9.4 0.6 collective-permute-start.6
  10.0 1.9 %rotate.3 = bf16[3072,128]{1,0:T(8,128)(2,1)S(1)} custom-call(s32[1]{0:T(128)} %bitcast.9.chip_ref, bf16[128,8192]{1,0:T(8,128)(2,1)} %g_hbm.3, bf16[64,128,128]{2,1,0:T(8,128)(2,1)} %ob_ref.1, f32[8,128]{1,0:T(8,128)S(1)} %sum_eigenvalues.1.refs_0_), custom_call_target="tpu_custom_call" | custom-call | flops 1 | bytes 1 | tf_op jit(solution)/shard_map/rotate/pallas_call | solution.py:162
  11.9 0.0 copy-start.1
  11.9 0.0 copy-start.3
  11.9 0.0 copy-start.4
  12.0 0.0 copy-start.7
  12.0 1.6 %collective-permute-start.10 = (bf16[3072,128]{1,0:T(8,128)(2,1)S(1)}, bf16[3072,128]{1,0:T(8,128)(2,1)S(1)}, u32[]{:S(2)}, u32[]{:S(2)}) collective-permute-start(bf16[3072,128]{1,0:T(8,128)(2,1)S(1)} %rotate.3), channel_id=1, source_target_pairs={{0,2},{1,3},{2,0},{3,1},{4,6},{5,7},{6,4},{7,5},{8,10},{9,11},{10,... | collective-permute-start | bytes 2359304 | tf_op jit(solution)/shard_map/ppermute | solution.py:589
  13.6 3.3 %rotate.2 = (bf16[1024,128]{1,0:T(8,128)(2,1)S(1)}, bf16[2048,128]{1,0:T(8,128)(2,1)S(1)}, bf16[1024,128]{1,0:T(8,128)(2,1)S(1)}, bf16[1024,128]{1,0:T(8,128)(2,1)S(1)}) custom-call(s32[1]{0:T(128)} %bitcast.9.chip_ref, bf16[128,8192]{1,0:T(8,128)(2,1)} %g_hbm.3, bf16[64,128,128]{2,1,0:T(8,128)(2,1)} %ob_ref.1), custom_call_target="tpu_custom_call" | custom-call | flops 99999997952 | bytes 1 | tf_op jit(solution)/shard_map/rotate/pallas_call | solution.py:162
  16.8 3.4 %collective-permute-done.6 = f32[8,128]{1,0:T(8,128)S(1)} collective-permute-done((f32[8,128]{1,0:T(8,128)S(1)}, f32[8,128]{1,0:T(8,128)S(1)}, u32[]{:S(2)}, u32[]{:S(2)}) %collective-permute-start.6) | collective-permute-done | bytes 4128 | tf_op jit(solution)/shard_map/ppermute | solution.py:589
  20.2 1.2 %collective-permute-done.7 = f32[8,128]{1,0:T(8,128)S(1)} collective-permute-done((f32[8,128]{1,0:T(8,128)S(1)}, f32[8,128]{1,0:T(8,128)S(1)}, u32[]{:S(2)}, u32[]{:S(2)}) %collective-permute-start.7) | collective-permute-done | bytes 4128 | tf_op jit(solution)/shard_map/ppermute | solution.py:589
  21.4 0.0 collective-permute-start.8
  21.4 7.2 %collective-permute-done.8 = f32[8,128]{1,0:T(8,128)S(1)} collective-permute-done((f32[8,128]{1,0:T(8,128)S(1)}, f32[8,128]{1,0:T(8,128)S(1)}, u32[]{:S(2)}, u32[]{:S(2)}) %collective-permute-start.8) | collective-permute-done | bytes 4128 | tf_op jit(solution)/shard_map/ppermute | solution.py:589
  28.6 0.0 collective-permute-done.2.b_ref.refs_1_.refs_3_
  28.6 0.1 pair_up.1
  28.7 1.1 %collective-permute-start.9 = (f32[8,128]{1,0:T(8,128)S(1)}, f32[8,128]{1,0:T(8,128)S(1)}, u32[]{:S(2)}, u32[]{:S(2)}) collective-permute-start(f32[8,128]{1,0:T(8,128)S(1)} %hold.3), channel_id=1, source_target_pairs={{0,8},{1,9},{2,10},{3,11},{4,12},{5,13},{6,14},{7,15},{8,0},{9,1},... | collective-permute-start | bytes 12296 | tf_op jit(solution)/shard_map/ppermute | solution.py:589
  29.8 1.0 %collective-permute-start.3 = (bf16[256,2048]{1,0:T(8,128)(2,1)S(1)}, bf16[256,2048]{1,0:T(8,128)(2,1)S(1)}, u32[]{:S(2)}, u32[]{:S(2)}) collective-permute-start(bf16[256,2048]{1,0:T(8,128)(2,1)S(1)} %get-tuple-element.22.refs_0_), channel_id=1, source_target_pairs={{0,2},{1,3},{2,0},{3,1},{4,6},{5,7},{6,4},{7,5},{8,10},{9,11},{10,... | collective-permute-start | bytes 3145736 | tf_op jit(solution)/shard_map/ppermute | solution.py:589
  30.9 2.4 %collective-permute-start.5 = (bf16[2048,128]{1,0:T(8,128)(2,1)S(1)}, bf16[2048,128]{1,0:T(8,128)(2,1)S(1)}, u32[]{:S(2)}, u32[]{:S(2)}) collective-permute-start(bf16[2048,128]{1,0:T(8,128)(2,1)S(1)} %get-tuple-element.23), channel_id=1, source_target_pairs={{0,8},{1,9},{2,10},{3,11},{4,12},{5,13},{6,14},{7,15},{8,0},{9,1},... | collective-permute-start | bytes 1572872 | tf_op jit(solution)/shard_map/ppermute | solution.py:589
  33.2 1.7 %collective-permute-start.4 = (bf16[128,2048]{1,0:T(8,128)(2,1)S(1)}, bf16[128,2048]{1,0:T(8,128)(2,1)S(1)}, u32[]{:S(2)}, u32[]{:S(2)}) collective-permute-start(bf16[128,2048]{1,0:T(8,128)(2,1)S(1)} %collective-permute-done.2.b_ref.refs_1_.refs_3_), channel_id=1, source_target_pairs={{0,4},{1,5},{2,6},{3,7},{4,0},{5,1},{6,2},{7,3},{8,12},{9,13},{10,... | collective-permute-start | bytes 1572872 | tf_op jit(solution)/shard_map/ppermute | solution.py:589
  34.9 2.1 %collective-permute-done.10.refs_3_.refs_10_.a_ref = bf16[3072,128]{1,0:T(8,128)(2,1)S(1)} collective-permute-done((bf16[3072,128]{1,0:T(8,128)(2,1)S(1)}, bf16[3072,128]{1,0:T(8,128)(2,1)S(1)}, u32[]{:S(2)}, u32[]{:S(2)}) %collective-permute-start.10) | collective-permute-done | bytes 786464 | tf_op jit(solution)/shard_map/ppermute | solution.py:589
  37.1 6.6 %precondition.1.refs_1_.refs_11_ = bf16[2,512,2048]{2,1,0:T(8,128)(2,1)} custom-call(s32[1]{0:T(128)} %bitcast.7.me_ref, bf16[8,2,512,256]{3,2,1,0:T(8,128)(2,1)S(1)} %copy-done.7, f32[8,512,256]{2,1,0:T(8,128)S(1)} %copy-done.1, f32[8,128]{1,0:T(8,128)S(1)} %add.36.s_ref, bf16[64,128,128]{2,1,0:T(8,128)(2,1)S(1)} %copy-done.3, ...), custom_call_target="tpu_custom_call" | custom-call | flops 99999997952 | bytes 1 | tf_op jit(solution)/shard_map/precondition/pallas_call | solution.py:373
  43.7 1.1 %pack_grads.1 = (bf16[2048,128]{1,0:T(8,128)(2,1)}, bf16[2048,128]{1,0:T(8,128)(2,1)}) custom-call(bf16[1024,128]{1,0:T(8,128)(2,1)S(1)} %get-tuple-element.33.n_ref, bf16[1024,128]{1,0:T(8,128)(2,1)S(1)} %get-tuple-element.34.f_ref, bf16[3072,128]{1,0:T(8,128)(2,1)S(1)} %collective-permute-done.10.refs_3_.refs_10_.a_ref), custom_call_target="tpu_custom_call" | custom-call | flops 1 | bytes 1 | tf_op jit(solution)/shard_map/pack_grads/pallas_call | solution.py:231
  44.8 0.1 collective-permute-start.14
  44.9 11.4 %collective-permute-done.5.m_ref.refs_8_ = bf16[2048,128]{1,0:T(8,128)(2,1)S(1)} collective-permute-done((bf16[2048,128]{1,0:T(8,128)(2,1)S(1)}, bf16[2048,128]{1,0:T(8,128)(2,1)S(1)}, u32[]{:S(2)}, u32[]{:S(2)}) %collective-permute-start.5) | collective-permute-done | bytes 524320 | tf_op jit(solution)/shard_map/ppermute | solution.py:589
  56.2 2.6 %collective-permute-start.15 = (bf16[2048,128]{1,0:T(8,128)(2,1)}, bf16[2048,128]{1,0:T(8,128)(2,1)}, u32[]{:S(2)}, u32[]{:S(2)}) collective-permute-start(bf16[2048,128]{1,0:T(8,128)(2,1)} %get-tuple-element.36), channel_id=1, source_target_pairs={{0,12},{1,13},{2,14},{3,15},{4,8},{5,9},{6,10},{7,11},{8,4},{9,5},... | collective-permute-start | bytes 1572872 | tf_op jit(solution)/shard_map/ppermute | solution.py:589
  58.9 1.1 %last_round.1 = (bf16[1536,128]{1,0:T(8,128)(2,1)}, bf16[1536,128]{1,0:T(8,128)(2,1)S(1)}) custom-call(bf16[128,2048]{1,0:T(8,128)(2,1)S(1)} %collective-permute-done.4.x_ref, bf16[2048,128]{1,0:T(8,128)(2,1)S(1)} %collective-permute-done.5.m_ref.refs_8_, bf16[16,128,128]{2,1,0:T(8,128)(2,1)S(1)} %copy-done.4, ...), custom_call_target="tpu_custom_call" | custom-call | flops 99999997952 | bytes 1 | tf_op jit(solution)/shard_map/last_round/pallas_call | solution.py:258
  60.0 0.8 collective-permute-start.12
  60.8 1.3 %collective-permute-start.13 = (bf16[1536,128]{1,0:T(8,128)(2,1)S(1)}, bf16[1536,128]{1,0:T(8,128)(2,1)S(1)}, u32[]{:S(2)}, u32[]{:S(2)}) collective-permute-start(bf16[1536,128]{1,0:T(8,128)(2,1)S(1)} %get-tuple-element.25.refs_7_), channel_id=1, source_target_pairs={{0,2},{1,3},{2,0},{3,1},{4,6},{5,7},{6,4},{7,5},{8,10},{9,11},{10,... | collective-permute-start | bytes 1179656 | tf_op jit(solution)/shard_map/ppermute | solution.py:589
  62.1 0.1 copy.12
  62.3 0.1 reduce
  62.4 0.1 stack.40.where_ref
  62.5 0.1 pad_add_fusion.where_ref
  62.6 0.1 broadcast_in_dim.7.refs_13_.refs_8_
  62.6 0.1 broadcast_in_dim.8.refs_14_.refs_9_
  62.7 13.6 %join_and_tally.1 = (f32[2,16,128]{2,1,0:T(8,128)S(1)}, bf16[2,2,512,2048]{3,2,1,0:T(8,128)(2,1)S(1)}, f32[2,2,512,128]{3,2,1,0:T(8,128)S(1)}, f32[2,2,512,128]{...) custom-call(s32[4]{0:T(128)S(1)} %pad_add_fusion.where_ref, ...), custom_call_target="tpu_custom_call" | custom-call | flops 1 | bytes 1 | tf_op jit(solution)/shard_map/join_and_tally/pallas_call | solution.py:478
  76.3 2.3 %collective-permute-done.13.l_ref.refs_7_ = bf16[1536,128]{1,0:T(8,128)(2,1)S(1)} collective-permute-done((bf16[1536,128]{1,0:T(8,128)(2,1)S(1)}, bf16[1536,128]{1,0:T(8,128)(2,1)S(1)}, u32[]{:S(2)}, u32[]{:S(2)}) %collective-permute-start.13) | collective-permute-done | bytes 393248 | tf_op jit(solution)/shard_map/ppermute | solution.py:589
  78.6 3.4 %project.1.refs_4_ = f32[2,2,512,128]{3,2,1,0:T(8,128)S(1)} custom-call(bf16[1536,128]{1,0:T(8,128)(2,1)} %collective-permute-done.12.h_ref, bf16[1536,128]{1,0:T(8,128)(2,1)S(1)} %collective-permute-done.13.l_ref.refs_7_, bf16[2,2,512,2048]{3,2,1,0:T(8,128)(2,1)S(1)} %get-tuple-element.31.p_ref, f32[2,16,128]{2,1,0:T(8,128)S(1)} %get-tuple-element.32.refs_0_.refs_10_), custom_call_target="tpu_custom_call" | custom-call | flops 1 | bytes 1 | tf_op jit(solution)/shard_map/project/pallas_call | solution.py:531
  82.0 1.9 %tally.1 = f32[2,16,128]{2,1,0:T(8,128)S(1)} custom-call(s32[6]{0:T(128)S(1)} %stack.40.where_ref, f32[2,2,512,128]{3,2,1,0:T(8,128)S(1)} %get-tuple-element.27.refs_0_, f32[2,2,512,128]{3,2,1,0:T(8,128)S(1)} %get-tuple-element.28.refs_1_, f32[2,2,512,128]{3,2,1,0:T(8,128)S(1)} %get-tuple-element.29.refs_2_, ...), custom_call_target="tpu_custom_call" | custom-call | flops 1 | bytes 1 | tf_op jit(solution)/shard_map/tally/pallas_call | solution.py:567
  83.9 0.1 reduce_sum.9
  84.0 1.1 %collective-permute-done.16 = f32[2,16]{1,0:T(2,128)S(1)} collective-permute-done((f32[2,16]{1,0:T(2,128)S(1)}, f32[2,16]{1,0:T(2,128)S(1)}, u32[]{:S(2)}, u32[]{:S(2)}) %collective-permute-start.16) | collective-permute-done | bytes 160 | tf_op jit(solution)/shard_map/ppermute | solution.py:589
  85.1 0.6 collective-permute-start.17
  85.8 3.0 %collective-permute-done.17 = f32[2,16]{1,0:T(2,128)S(1)} collective-permute-done((f32[2,16]{1,0:T(2,128)S(1)}, f32[2,16]{1,0:T(2,128)S(1)}, u32[]{:S(2)}, u32[]{:S(2)}) %collective-permute-start.17) | collective-permute-done | bytes 160 | tf_op jit(solution)/shard_map/ppermute | solution.py:589
  88.7 3.6 %collective-permute-done.18 = f32[2,16]{1,0:T(2,128)S(1)} collective-permute-done((f32[2,16]{1,0:T(2,128)S(1)}, f32[2,16]{1,0:T(2,128)S(1)}, u32[]{:S(2)}, u32[]{:S(2)}) %collective-permute-start.18) | collective-permute-done | bytes 160 | tf_op jit(solution)/shard_map/ppermute | solution.py:589
  92.3 4.5 %collective-permute-done.19 = f32[2,16]{1,0:T(2,128)S(1)} collective-permute-done((f32[2,16]{1,0:T(2,128)S(1)}, f32[2,16]{1,0:T(2,128)S(1)}, u32[]{:S(2)}, u32[]{:S(2)}) %collective-permute-start.19) | collective-permute-done | bytes 160 | tf_op jit(solution)/shard_map/ppermute | solution.py:589
  96.8 0.7 dynamic-slice_reduce_fusion
  (40 shorter events, 0.1 us)
Async XLA Ops:
  0.0 28.6 %collective-permute-start.2 = (bf16[128,2048]{1,0:T(8,128)(2,1)}, bf16[128,2048]{1,0:T(8,128)(2,1)S(1)}, u32[]{:S(2)}, u32[]{:S(2)}) collective-permute-start(bf16[128,2048]{1,0:T(8,128)(2,1)} %refs_0_.1), channel_id=1, source_target_pairs={{0,12},{1,13},{2,14},{3,15},{4,8},{5,9},{6,10},{7,11},{8,4},{9,5},... | collective-permute-start | bytes 1572872 | tf_op jit(solution)/shard_map/ppermute | solution.py:589
  5.0 23.6 %collective-permute-start = (bf16[128,2048]{1,0:T(8,128)(2,1)}, bf16[128,2048]{1,0:T(8,128)(2,1)S(1)}, u32[]{:S(2)}, u32[]{:S(2)}) collective-permute-start(bf16[128,2048]{1,0:T(8,128)(2,1)} %refs_0_.1), channel_id=1, source_target_pairs={{0,2},{1,3},{2,0},{3,1},{4,6},{5,7},{6,4},{7,5},{8,10},{9,11},{10,... | collective-permute-start | bytes 1572872 | tf_op jit(solution)/shard_map/ppermute | solution.py:589
  6.6 22.1 %collective-permute-start.1 = (bf16[128,2048]{1,0:T(8,128)(2,1)}, bf16[128,2048]{1,0:T(8,128)(2,1)S(1)}, u32[]{:S(2)}, u32[]{:S(2)}) collective-permute-start(bf16[128,2048]{1,0:T(8,128)(2,1)} %refs_0_.1), channel_id=1, source_target_pairs={{0,4},{1,5},{2,6},{3,7},{4,0},{5,1},{6,2},{7,3},{8,12},{9,13},{10,... | collective-permute-start | bytes 1572872 | tf_op jit(solution)/shard_map/ppermute | solution.py:589
  6.6 2.2 %copy-start = (f32[8,512,256]{2,1,0:T(8,128)S(1)}, f32[8,512,256]{2,1,0:T(8,128)}, u32[]{:S(2)}) copy-start(f32[8,512,256]{2,1,0:T(8,128)} %e_ref.3) | copy-start | bytes 12582916
  9.4 10.8 %collective-permute-start.6 = (f32[8,128]{1,0:T(8,128)S(1)}, f32[8,128]{1,0:T(8,128)S(1)}, u32[]{:S(2)}, u32[]{:S(2)}) collective-permute-start(f32[8,128]{1,0:T(8,128)S(1)} %sum_eigenvalues.1.refs_0_), channel_id=1, source_target_pairs={{0,2},{1,3},{2,0},{3,1},{4,6},{5,7},{6,4},{7,5},{8,10},{9,11},{10,... | collective-permute-start | bytes 12296 | tf_op jit(solution)/shard_map/ppermute | solution.py:589
  11.9 25.1 %copy-start.1 = (f32[8,512,256]{2,1,0:T(8,128)S(1)}, f32[8,512,256]{2,1,0:T(8,128)}, u32[]{:S(2)}) copy-start(f32[8,512,256]{2,1,0:T(8,128)} %e_ref.3) | copy-start | bytes 12582916
  11.9 25.1 %copy-start.3 = (bf16[64,128,128]{2,1,0:T(8,128)(2,1)S(1)}, bf16[64,128,128]{2,1,0:T(8,128)(2,1)}, u32[]{:S(2)}) copy-start(bf16[64,128,128]{2,1,0:T(8,128)(2,1)} %ob_ref.1) | copy-start | bytes 6291460
  11.9 25.1 %copy-start.4 = (bf16[16,128,128]{2,1,0:T(8,128)(2,1)S(1)}, bf16[16,128,128]{2,1,0:T(8,128)(2,1)}, u32[]{:S(2)}) copy-start(bf16[16,128,128]{2,1,0:T(8,128)(2,1)} %refs_5_.1) | copy-start | bytes 1572868
  12.0 25.1 %copy-start.7 = (bf16[8,2,512,256]{3,2,1,0:T(8,128)(2,1)S(1)}, bf16[8,2,512,256]{3,2,1,0:T(8,128)(2,1)}, u32[]{:S(2)}) copy-start(bf16[8,2,512,256]{3,2,1,0:T(8,128)(2,1)} %q_ref.1) | copy-start | bytes 12582916
  12.0 25.1 %collective-permute-start.10 = (bf16[3072,128]{1,0:T(8,128)(2,1)S(1)}, bf16[3072,128]{1,0:T(8,128)(2,1)S(1)}, u32[]{:S(2)}, u32[]{:S(2)}) collective-permute-start(bf16[3072,128]{1,0:T(8,128)(2,1)S(1)} %rotate.3), channel_id=1, source_target_pairs={{0,2},{1,3},{2,0},{3,1},{4,6},{5,7},{6,4},{7,5},{8,10},{9,11},{10,... | collective-permute-start | bytes 2359304 | tf_op jit(solution)/shard_map/ppermute | solution.py:589
  16.8 26.9 %copy-start.6 = (bf16[1024,128]{1,0:T(8,128)(2,1)}, bf16[1024,128]{1,0:T(8,128)(2,1)S(1)}, u32[]{:S(2)}) copy-start(bf16[1024,128]{1,0:T(8,128)(2,1)S(1)} %get-tuple-element.26.refs_9_) | copy-start | bytes 786436
  20.2 1.2 %collective-permute-start.7 = (f32[8,128]{1,0:T(8,128)S(1)}, f32[8,128]{1,0:T(8,128)S(1)}, u32[]{:S(2)}, u32[]{:S(2)}) collective-permute-start(f32[8,128]{1,0:T(8,128)S(1)} %hold.2), channel_id=1, source_target_pairs={{0,1},{1,0},{2,3},{3,2},{4,5},{5,4},{6,7},{7,6},{8,9},{9,8},{10,11... | collective-permute-start | bytes 12296 | tf_op jit(solution)/shard_map/ppermute | solution.py:589
  21.4 7.2 %collective-permute-start.8 = (f32[8,128]{1,0:T(8,128)S(1)}, f32[8,128]{1,0:T(8,128)S(1)}, u32[]{:S(2)}, u32[]{:S(2)}) collective-permute-start(f32[8,128]{1,0:T(8,128)S(1)} %add.34), channel_id=1, source_target_pairs={{0,4},{1,5},{2,6},{3,7},{4,0},{5,1},{6,2},{7,3},{8,12},{9,13},{10,... | collective-permute-start | bytes 12296 | tf_op jit(solution)/shard_map/ppermute | solution.py:589
  28.7 6.2 %collective-permute-start.9 = (f32[8,128]{1,0:T(8,128)S(1)}, f32[8,128]{1,0:T(8,128)S(1)}, u32[]{:S(2)}, u32[]{:S(2)}) collective-permute-start(f32[8,128]{1,0:T(8,128)S(1)} %hold.3), channel_id=1, source_target_pairs={{0,8},{1,9},{2,10},{3,11},{4,12},{5,13},{6,14},{7,15},{8,0},{9,1},... | collective-permute-start | bytes 12296 | tf_op jit(solution)/shard_map/ppermute | solution.py:589
  29.8 29.1 %collective-permute-start.3 = (bf16[256,2048]{1,0:T(8,128)(2,1)S(1)}, bf16[256,2048]{1,0:T(8,128)(2,1)S(1)}, u32[]{:S(2)}, u32[]{:S(2)}) collective-permute-start(bf16[256,2048]{1,0:T(8,128)(2,1)S(1)} %get-tuple-element.22.refs_0_), channel_id=1, source_target_pairs={{0,2},{1,3},{2,0},{3,1},{4,6},{5,7},{6,4},{7,5},{8,10},{9,11},{10,... | collective-permute-start | bytes 3145736 | tf_op jit(solution)/shard_map/ppermute | solution.py:589
  30.9 25.4 %collective-permute-start.5 = (bf16[2048,128]{1,0:T(8,128)(2,1)S(1)}, bf16[2048,128]{1,0:T(8,128)(2,1)S(1)}, u32[]{:S(2)}, u32[]{:S(2)}) collective-permute-start(bf16[2048,128]{1,0:T(8,128)(2,1)S(1)} %get-tuple-element.23), channel_id=1, source_target_pairs={{0,8},{1,9},{2,10},{3,11},{4,12},{5,13},{6,14},{7,15},{8,0},{9,1},... | collective-permute-start | bytes 1572872 | tf_op jit(solution)/shard_map/ppermute | solution.py:589
  33.2 25.6 %collective-permute-start.4 = (bf16[128,2048]{1,0:T(8,128)(2,1)S(1)}, bf16[128,2048]{1,0:T(8,128)(2,1)S(1)}, u32[]{:S(2)}, u32[]{:S(2)}) collective-permute-start(bf16[128,2048]{1,0:T(8,128)(2,1)S(1)} %collective-permute-done.2.b_ref.refs_1_.refs_3_), channel_id=1, source_target_pairs={{0,4},{1,5},{2,6},{3,7},{4,0},{5,1},{6,2},{7,3},{8,12},{9,13},{10,... | collective-permute-start | bytes 1572872 | tf_op jit(solution)/shard_map/ppermute | solution.py:589
  37.0 6.6 %copy-start.2 = (bf16[3072,128]{1,0:T(8,128)(2,1)}, bf16[3072,128]{1,0:T(8,128)(2,1)S(1)}, u32[]{:S(2)}) copy-start(bf16[3072,128]{1,0:T(8,128)(2,1)S(1)} %collective-permute-done.10.refs_3_.refs_10_.a_ref) | copy-start | bytes 2359300
  43.7 18.9 %collective-permute-start.11 = (bf16[2,512,2048]{2,1,0:T(8,128)(2,1)}, bf16[2,512,2048]{2,1,0:T(8,128)(2,1)}, u32[]{:S(2)}, u32[]{:S(2)}) collective-permute-start(bf16[2,512,2048]{2,1,0:T(8,128)(2,1)} %precondition.1.refs_1_.refs_11_), channel_id=1, source_target_pairs={{0,1},{1,0},{2,3},{3,2},{4,5},{5,4},{6,7},{7,6},{8,9},{9,8},{10,11... | collective-permute-start | bytes 12582920 | tf_op jit(solution)/shard_map/ppermute | solution.py:589
  44.8 37.2 %collective-permute-start.14 = (bf16[2048,128]{1,0:T(8,128)(2,1)}, bf16[2048,128]{1,0:T(8,128)(2,1)}, u32[]{:S(2)}, u32[]{:S(2)}) collective-permute-start(bf16[2048,128]{1,0:T(8,128)(2,1)} %get-tuple-element.35), channel_id=1, source_target_pairs={{0,4},{1,5},{2,6},{3,7},{4,0},{5,1},{6,2},{7,3},{8,12},{9,13},{10,... | collective-permute-start | bytes 1572872 | tf_op jit(solution)/shard_map/ppermute | solution.py:589
  56.2 3.8 %copy-start.5 = (bf16[2048,128]{1,0:T(8,128)(2,1)}, bf16[2048,128]{1,0:T(8,128)(2,1)S(1)}, u32[]{:S(2)}) copy-start(bf16[2048,128]{1,0:T(8,128)(2,1)S(1)} %collective-permute-done.5.m_ref.refs_8_) | copy-start | bytes 1572868
  56.2 5.9 %copy-start.8 = (s32[16]{0:T(128)S(1)}, s32[16]{0:T(128)}, u32[]{:S(2)}) copy-start(s32[16]{0:T(128)} %param.13) | copy-start | bytes 196
  56.2 25.8 %collective-permute-start.15 = (bf16[2048,128]{1,0:T(8,128)(2,1)}, bf16[2048,128]{1,0:T(8,128)(2,1)}, u32[]{:S(2)}, u32[]{:S(2)}) collective-permute-start(bf16[2048,128]{1,0:T(8,128)(2,1)} %get-tuple-element.36), channel_id=1, source_target_pairs={{0,12},{1,13},{2,14},{3,15},{4,8},{5,9},{6,10},{7,11},{8,4},{9,5},... | collective-permute-start | bytes 1572872 | tf_op jit(solution)/shard_map/ppermute | solution.py:589
  60.0 16.2 %collective-permute-start.12 = (bf16[1536,128]{1,0:T(8,128)(2,1)}, bf16[1536,128]{1,0:T(8,128)(2,1)}, u32[]{:S(2)}, u32[]{:S(2)}) collective-permute-start(bf16[1536,128]{1,0:T(8,128)(2,1)} %get-tuple-element.24.refs_6_), channel_id=1, source_target_pairs={{0,2},{1,3},{2,0},{3,1},{4,6},{5,7},{6,4},{7,5},{8,10},{9,11},{10,... | collective-permute-start | bytes 1179656 | tf_op jit(solution)/shard_map/ppermute | solution.py:589
  60.8 17.8 %collective-permute-start.13 = (bf16[1536,128]{1,0:T(8,128)(2,1)S(1)}, bf16[1536,128]{1,0:T(8,128)(2,1)S(1)}, u32[]{:S(2)}, u32[]{:S(2)}) collective-permute-start(bf16[1536,128]{1,0:T(8,128)(2,1)S(1)} %get-tuple-element.25.refs_7_), channel_id=1, source_target_pairs={{0,2},{1,3},{2,0},{3,1},{4,6},{5,7},{6,4},{7,5},{8,10},{9,11},{10,... | collective-permute-start | bytes 1179656 | tf_op jit(solution)/shard_map/ppermute | solution.py:589
  84.0 1.1 %collective-permute-start.16 = (f32[2,16]{1,0:T(2,128)S(1)}, f32[2,16]{1,0:T(2,128)S(1)}, u32[]{:S(2)}, u32[]{:S(2)}) collective-permute-start(f32[2,16]{1,0:T(2,128)S(1)} %reduce_sum.9), channel_id=1, source_target_pairs={{0,1},{1,0},{2,3},{3,2},{4,5},{5,4},{6,7},{7,6},{8,9},{9,8},{10,11... | collective-permute-start | bytes 392 | tf_op jit(solution)/shard_map/ppermute | solution.py:589
  85.1 3.6 %collective-permute-start.17 = (f32[2,16]{1,0:T(2,128)S(1)}, f32[2,16]{1,0:T(2,128)S(1)}, u32[]{:S(2)}, u32[]{:S(2)}) collective-permute-start(f32[2,16]{1,0:T(2,128)S(1)} %add.37), channel_id=1, source_target_pairs={{0,2},{1,3},{2,0},{3,1},{4,6},{5,7},{6,4},{7,5},{8,10},{9,11},{10,... | collective-permute-start | bytes 392 | tf_op jit(solution)/shard_map/ppermute | solution.py:589
  88.7 3.6 %collective-permute-start.18 = (f32[2,16]{1,0:T(2,128)S(1)}, f32[2,16]{1,0:T(2,128)S(1)}, u32[]{:S(2)}, u32[]{:S(2)}) collective-permute-start(f32[2,16]{1,0:T(2,128)S(1)} %add.38), channel_id=1, source_target_pairs={{0,4},{1,5},{2,6},{3,7},{4,0},{5,1},{6,2},{7,3},{8,12},{9,13},{10,... | collective-permute-start | bytes 392 | tf_op jit(solution)/shard_map/ppermute | solution.py:589
  92.3 4.5 %collective-permute-start.19 = (f32[2,16]{1,0:T(2,128)S(1)}, f32[2,16]{1,0:T(2,128)S(1)}, u32[]{:S(2)}, u32[]{:S(2)}) collective-permute-start(f32[2,16]{1,0:T(2,128)S(1)} %add.39), channel_id=1, source_target_pairs={{0,8},{1,9},{2,10},{3,11},{4,12},{5,13},{6,14},{7,15},{8,0},{9,1},... | collective-permute-start | bytes 392 | tf_op jit(solution)/shard_map/ppermute | solution.py:589

commit v5 on v4

--- a/solution.py
+++ b/solution.py
@@ -510,32 +510,33 @@
         o_ref[q] = total
 
 
-def project(high, low, both, after):
+def project(inputs, rows_of, both, after, base=None):
     cores, queries, rows, features = both.shape
-    cut, tokens = high.shape
+    tokens = inputs.shape[1]
+    first, end = rows_of
     block = math.gcd(rows, 512)
-
-    def body(h_ref, l_ref, p_ref, *refs):
-        x_all = refs[-1]
-        x_all[:cut, :] = h_ref[...]
-        x_all[cut:, :] = l_ref[: features - cut, :]
+    bases = [] if base is None else [base]
+
+    def body(x_ref, p_ref, *refs):
         for c in range(cores):
             for q in range(queries):
                 for r in range(0, rows, block):
                     span = slice(r, r + block)
-                    refs[-2][c, q, span, :] = jnp.dot(
-                        p_ref[c, q, span, :], x_all[...], preferred_element_type=F32
+                    turned = jnp.dot(
+                        p_ref[c, q, span, first:end],
+                        x_ref[: end - first, :],
+                        preferred_element_type=F32,
                     )
-
-    vmem = pl.BlockSpec(memory_space=pltpu.VMEM)
-    return call(
-        body,
-        in_specs=[vmem] * 3 + [pl.BlockSpec(memory_space=pl.ANY)] * len(after),
+                    refs[-1][c, q, span, :] = refs[0][c, q, span, :] + turned if bases else turned
+
+    vmem = pl.BlockSpec(memory_space=pltpu.VMEM)
+    return call(
+        body,
+        in_specs=[vmem] * (2 + len(bases)) + [pl.BlockSpec(memory_space=pl.ANY)] * len(after),
         out_specs=vmem,
         out_shape=jax.ShapeDtypeStruct((cores, queries, rows, tokens), F32),
-        scratch_shapes=[pltpu.VMEM((features, tokens), BF16)],
         name="project",
-    )(high, low, both, *after)
+    )(inputs, both, *bases, *after)
 
 
 def tally(where, projected, grads, starts, ends, running, order):
@@ -645,7 +646,8 @@
         ends,
         [layer_inputs, side_x, near_x, far_x, sides],
     )
-    kept.append(project(high, low, both, [running]))
+    part_way = project(high, (0, cut), both, [running])
+    kept.append(project(low, (cut, features), both, [], part_way))
     running = tally(
         where(2, 3, 6, 7, 5),
         kept,

time: 97.7 us -> 95.5 us (0.977)
  waiting for transfers between devices: 39.7 us -> 35.2 us
  starting transfers between devices: 20.4 us -> 22.5 us
    ppermute x20, waiting for transfers between devices: 39.7 us -> 35.2 us  [swap(): return lax.ppermute(value, 'dp', [(i, i ^ offset) for i in range(devices)])]
    ppermute x20, starting transfers between devices: 20.4 us -> 22.5 us  [swap(): return lax.ppermute(value, 'dp', [(i, i ^ offset) for i in range(devices)])]
    pallas_call x1 -> x2, Pallas kernels: 3.38 us -> 3.5 us  [project(): call(body, in_specs=[vmem] * (2 + len(bases)) + [pl.BlockSpec(memory_spac...]
  transfers between devices with their start and end apart: 20 -> 20, of which waited for: 10 -> 9; matrix products, arithmetic and copies ran while one was open for 1% -> 1% of each run, Pallas kernels for 33% -> 33%
where the time goes in v5:
time: 95.5 us; the launch traced here: 95.3 us
  waiting for transfers between devices  35.2 us (37%)
  Pallas kernels  33.7 us (35%)
  starting transfers between devices  22.5 us (24%)
  local copies, waits for them, and re-layouts  3.23 us (3%)
    ppermute x20, waiting for transfers between devices, swap(): return lax.ppermute(value, 'dp', [(i, i ^ offset) for i in range(devices)])  35.2 us
    ppermute x20, starting transfers between devices, swap(): return lax.ppermute(value, 'dp', [(i, i ^ offset) for i in range(devices)])  22.5 us
    pallas_call x1, Pallas kernels, join_and_tally(): call(body, in_specs=[pl.BlockSpec(memory_space=pltpu.SMEM)] + [hbm] * (le...  13.6 us
    pallas_call x1, Pallas kernels, precondition_rows(): call(body, grid_spec=grid_spec, out_shape=jax.ShapeDtypeStruct((queries,...  6.61 us
    pallas_call x2, Pallas kernels, rotate(): call(body, cost=cost, in_specs=[pl.BlockSpec(memory_space=pltpu.SMEM), hb...  5.18 us
    pallas_call x2, Pallas kernels, project(): call(body, in_specs=[vmem] * (2 + len(bases)) + [pl.BlockSpec(memory_spac...  3.5 us
    unnamed x18, local copies, waits for them, and re-layouts  2.23 us
  transfers between devices with their start and end apart: 20, of which 9 were waited for; matrix products, arithmetic and copies ran while one was open for 1% of the time, Pallas kernels for 33%

profile of v5, /device:TPU:0, one launch (start us, length us, event | category | flops | bytes accessed | tf_op | source)
XLA Modules:
  0.0 95.3 jit_solution(12906220972188472949)
XLA Ops:
  0.0 5.0 %collective-permute-start.2 = (bf16[128,2048]{1,0:T(8,128)(2,1)}, bf16[128,2048]{1,0:T(8,128)(2,1)S(1)}, u32[]{:S(2)}, u32[]{:S(2)}) collective-permute-start(bf16[128,2048]{1,0:T(8,128)(2,1)} %refs_0_.1), channel_id=1, source_target_pairs={{0,12},{1,13},{2,14},{3,15},{4,8},{5,9},{6,10},{7,11},{8,4},{9,5},... | collective-permute-start | bytes 1572872 | tf_op jit(solution)/shard_map/ppermute | solution.py:590
  5.0 1.5 %collective-permute-start = (bf16[128,2048]{1,0:T(8,128)(2,1)}, bf16[128,2048]{1,0:T(8,128)(2,1)S(1)}, u32[]{:S(2)}, u32[]{:S(2)}) collective-permute-start(bf16[128,2048]{1,0:T(8,128)(2,1)} %refs_0_.1), channel_id=1, source_target_pairs={{0,2},{1,3},{2,0},{3,1},{4,6},{5,7},{6,4},{7,5},{8,10},{9,11},{10,... | collective-permute-start | bytes 1572872 | tf_op jit(solution)/shard_map/ppermute | solution.py:590
  6.6 2.2 %copy-done = f32[8,512,256]{2,1,0:T(8,128)S(1)} copy-done((f32[8,512,256]{2,1,0:T(8,128)S(1)}, f32[8,512,256]{2,1,0:T(8,128)}, u32[]{:S(2)}) %copy-start) | copy-done | bytes 4194328
  8.8 0.7 sum_eigenvalues.1.refs_0_
  9.4 0.6 collective-permute-start.6
  10.0 1.9 %rotate.3 = bf16[3072,128]{1,0:T(8,128)(2,1)S(1)} custom-call(s32[1]{0:T(128)} %bitcast.9.chip_ref, bf16[128,8192]{1,0:T(8,128)(2,1)} %g_hbm.3, bf16[64,128,128]{2,1,0:T(8,128)(2,1)} %ob_ref.1, f32[8,128]{1,0:T(8,128)S(1)} %sum_eigenvalues.1.refs_0_), custom_call_target="tpu_custom_call" | custom-call | flops 1 | bytes 1 | tf_op jit(solution)/shard_map/rotate/pallas_call | solution.py:162
  11.9 0.0 copy-start.1
  11.9 0.0 copy-start.3
  11.9 0.0 copy-start.4
  12.0 0.0 copy-start.7
  12.0 1.6 %collective-permute-start.10 = (bf16[3072,128]{1,0:T(8,128)(2,1)S(1)}, bf16[3072,128]{1,0:T(8,128)(2,1)S(1)}, u32[]{:S(2)}, u32[]{:S(2)}) collective-permute-start(bf16[3072,128]{1,0:T(8,128)(2,1)S(1)} %rotate.3), channel_id=1, source_target_pairs={{0,2},{1,3},{2,0},{3,1},{4,6},{5,7},{6,4},{7,5},{8,10},{9,11},{10,... | collective-permute-start | bytes 2359304 | tf_op jit(solution)/shard_map/ppermute | solution.py:590
  13.6 3.3 %rotate.2 = (bf16[1024,128]{1,0:T(8,128)(2,1)S(1)}, bf16[2048,128]{1,0:T(8,128)(2,1)S(1)}, bf16[1024,128]{1,0:T(8,128)(2,1)S(1)}, bf16[1024,128]{1,0:T(8,128)(2,1)S(1)}) custom-call(s32[1]{0:T(128)} %bitcast.9.chip_ref, bf16[128,8192]{1,0:T(8,128)(2,1)} %g_hbm.3, bf16[64,128,128]{2,1,0:T(8,128)(2,1)} %ob_ref.1), custom_call_target="tpu_custom_call" | custom-call | flops 99999997952 | bytes 1 | tf_op jit(solution)/shard_map/rotate/pallas_call | solution.py:162
  16.8 3.4 %collective-permute-done.6 = f32[8,128]{1,0:T(8,128)S(1)} collective-permute-done((f32[8,128]{1,0:T(8,128)S(1)}, f32[8,128]{1,0:T(8,128)S(1)}, u32[]{:S(2)}, u32[]{:S(2)}) %collective-permute-start.6) | collective-permute-done | bytes 4128 | tf_op jit(solution)/shard_map/ppermute | solution.py:590
  20.2 1.2 %collective-permute-done.7 = f32[8,128]{1,0:T(8,128)S(1)} collective-permute-done((f32[8,128]{1,0:T(8,128)S(1)}, f32[8,128]{1,0:T(8,128)S(1)}, u32[]{:S(2)}, u32[]{:S(2)}) %collective-permute-start.7) | collective-permute-done | bytes 4128 | tf_op jit(solution)/shard_map/ppermute | solution.py:590
  21.4 7.2 %collective-permute-done.8 = f32[8,128]{1,0:T(8,128)S(1)} collective-permute-done((f32[8,128]{1,0:T(8,128)S(1)}, f32[8,128]{1,0:T(8,128)S(1)}, u32[]{:S(2)}, u32[]{:S(2)}) %collective-permute-start.8) | collective-permute-done | bytes 4128 | tf_op jit(solution)/shard_map/ppermute | solution.py:590
  28.6 0.1 pair_up.1
  28.7 1.1 %collective-permute-start.9 = (f32[8,128]{1,0:T(8,128)S(1)}, f32[8,128]{1,0:T(8,128)S(1)}, u32[]{:S(2)}, u32[]{:S(2)}) collective-permute-start(f32[8,128]{1,0:T(8,128)S(1)} %hold.3), channel_id=1, source_target_pairs={{0,8},{1,9},{2,10},{3,11},{4,12},{5,13},{6,14},{7,15},{8,0},{9,1},... | collective-permute-start | bytes 12296 | tf_op jit(solution)/shard_map/ppermute | solution.py:590
  29.8 1.0 %collective-permute-start.3 = (bf16[256,2048]{1,0:T(8,128)(2,1)S(1)}, bf16[256,2048]{1,0:T(8,128)(2,1)S(1)}, u32[]{:S(2)}, u32[]{:S(2)}) collective-permute-start(bf16[256,2048]{1,0:T(8,128)(2,1)S(1)} %get-tuple-element.22.refs_0_), channel_id=1, source_target_pairs={{0,2},{1,3},{2,0},{3,1},{4,6},{5,7},{6,4},{7,5},{8,10},{9,11},{10,... | collective-permute-start | bytes 3145736 | tf_op jit(solution)/shard_map/ppermute | solution.py:590
  30.9 2.4 %collective-permute-start.5 = (bf16[2048,128]{1,0:T(8,128)(2,1)S(1)}, bf16[2048,128]{1,0:T(8,128)(2,1)S(1)}, u32[]{:S(2)}, u32[]{:S(2)}) collective-permute-start(bf16[2048,128]{1,0:T(8,128)(2,1)S(1)} %get-tuple-element.23), channel_id=1, source_target_pairs={{0,8},{1,9},{2,10},{3,11},{4,12},{5,13},{6,14},{7,15},{8,0},{9,1},... | collective-permute-start | bytes 1572872 | tf_op jit(solution)/shard_map/ppermute | solution.py:590
  33.2 1.7 %collective-permute-start.4 = (bf16[128,2048]{1,0:T(8,128)(2,1)S(1)}, bf16[128,2048]{1,0:T(8,128)(2,1)S(1)}, u32[]{:S(2)}, u32[]{:S(2)}) collective-permute-start(bf16[128,2048]{1,0:T(8,128)(2,1)S(1)} %collective-permute-done.2.b_ref.refs_1_.refs_3_), channel_id=1, source_target_pairs={{0,4},{1,5},{2,6},{3,7},{4,0},{5,1},{6,2},{7,3},{8,12},{9,13},{10,... | collective-permute-start | bytes 1572872 | tf_op jit(solution)/shard_map/ppermute | solution.py:590
  34.9 2.1 %collective-permute-done.10.refs_3_.refs_10_.a_ref = bf16[3072,128]{1,0:T(8,128)(2,1)S(1)} collective-permute-done((bf16[3072,128]{1,0:T(8,128)(2,1)S(1)}, bf16[3072,128]{1,0:T(8,128)(2,1)S(1)}, u32[]{:S(2)}, u32[]{:S(2)}) %collective-permute-start.10) | collective-permute-done | bytes 786464 | tf_op jit(solution)/shard_map/ppermute | solution.py:590
  37.1 6.6 %precondition.1.refs_1_.refs_11_ = bf16[2,512,2048]{2,1,0:T(8,128)(2,1)} custom-call(s32[1]{0:T(128)} %bitcast.7.me_ref, bf16[8,2,512,256]{3,2,1,0:T(8,128)(2,1)S(1)} %copy-done.7, f32[8,512,256]{2,1,0:T(8,128)S(1)} %copy-done.1, f32[8,128]{1,0:T(8,128)S(1)} %add.36.s_ref, bf16[64,128,128]{2,1,0:T(8,128)(2,1)S(1)} %copy-done.3, ...), custom_call_target="tpu_custom_call" | custom-call | flops 99999997952 | bytes 1 | tf_op jit(solution)/shard_map/precondition/pallas_call | solution.py:373
  43.7 1.1 %pack_grads.1 = (bf16[2048,128]{1,0:T(8,128)(2,1)}, bf16[2048,128]{1,0:T(8,128)(2,1)}) custom-call(bf16[1024,128]{1,0:T(8,128)(2,1)S(1)} %get-tuple-element.33.n_ref, bf16[1024,128]{1,0:T(8,128)(2,1)S(1)} %get-tuple-element.34.f_ref, bf16[3072,128]{1,0:T(8,128)(2,1)S(1)} %collective-permute-done.10.refs_3_.refs_10_.a_ref), custom_call_target="tpu_custom_call" | custom-call | flops 1 | bytes 1 | tf_op jit(solution)/shard_map/pack_grads/pallas_call | solution.py:231
  44.8 0.1 collective-permute-start.14
  44.9 11.4 %collective-permute-done.5.m_ref.refs_8_ = bf16[2048,128]{1,0:T(8,128)(2,1)S(1)} collective-permute-done((bf16[2048,128]{1,0:T(8,128)(2,1)S(1)}, bf16[2048,128]{1,0:T(8,128)(2,1)S(1)}, u32[]{:S(2)}, u32[]{:S(2)}) %collective-permute-start.5) | collective-permute-done | bytes 524320 | tf_op jit(solution)/shard_map/ppermute | solution.py:590
  56.2 2.6 %collective-permute-start.15 = (bf16[2048,128]{1,0:T(8,128)(2,1)}, bf16[2048,128]{1,0:T(8,128)(2,1)}, u32[]{:S(2)}, u32[]{:S(2)}) collective-permute-start(bf16[2048,128]{1,0:T(8,128)(2,1)} %get-tuple-element.36), channel_id=1, source_target_pairs={{0,12},{1,13},{2,14},{3,15},{4,8},{5,9},{6,10},{7,11},{8,4},{9,5},... | collective-permute-start | bytes 1572872 | tf_op jit(solution)/shard_map/ppermute | solution.py:590
  58.9 1.1 %last_round.1 = (bf16[1536,128]{1,0:T(8,128)(2,1)}, bf16[1536,128]{1,0:T(8,128)(2,1)S(1)}) custom-call(bf16[128,2048]{1,0:T(8,128)(2,1)S(1)} %collective-permute-done.4.x_ref, bf16[2048,128]{1,0:T(8,128)(2,1)S(1)} %collective-permute-done.5.m_ref.refs_8_, bf16[16,128,128]{2,1,0:T(8,128)(2,1)S(1)} %copy-done.4, ...), custom_call_target="tpu_custom_call" | custom-call | flops 99999997952 | bytes 1 | tf_op jit(solution)/shard_map/last_round/pallas_call | solution.py:258
  60.0 0.8 collective-permute-start.13
  60.8 1.3 %collective-permute-start.12 = (bf16[1536,128]{1,0:T(8,128)(2,1)S(1)}, bf16[1536,128]{1,0:T(8,128)(2,1)S(1)}, u32[]{:S(2)}, u32[]{:S(2)}) collective-permute-start(bf16[1536,128]{1,0:T(8,128)(2,1)S(1)} %get-tuple-element.25.refs_7_), channel_id=1, source_target_pairs={{0,2},{1,3},{2,0},{3,1},{4,6},{5,7},{6,4},{7,5},{8,10},{9,11},{10,... | collective-permute-start | bytes 1179656 | tf_op jit(solution)/shard_map/ppermute | solution.py:590
  62.1 0.1 copy.12
  62.3 0.1 reduce
  62.4 0.1 stack.40.where_ref
  62.5 0.1 pad_add_fusion.where_ref
  62.6 0.1 broadcast_in_dim.7.refs_13_.refs_8_
  62.6 0.1 broadcast_in_dim.8.refs_14_.refs_9_
  62.7 13.6 %join_and_tally.1 = (f32[2,16,128]{2,1,0:T(8,128)S(1)}, bf16[2,2,512,2048]{3,2,1,0:T(8,128)(2,1)S(1)}, f32[2,2,512,128]{3,2,1,0:T(8,128)S(1)}, f32[2,2,512,128]{...) custom-call(s32[4]{0:T(128)S(1)} %pad_add_fusion.where_ref, ...), custom_call_target="tpu_custom_call" | custom-call | flops 1 | bytes 1 | tf_op jit(solution)/shard_map/join_and_tally/pallas_call | solution.py:478
  76.3 2.8 %project.2.refs_0_ = f32[2,2,512,128]{3,2,1,0:T(8,128)S(1)} custom-call(bf16[1536,128]{1,0:T(8,128)(2,1)} %collective-permute-done.13.x_ref, bf16[2,2,512,2048]{3,2,1,0:T(8,128)(2,1)S(1)} %get-tuple-element.31.p_ref, f32[2,16,128]{2,1,0:T(8,128)S(1)} %get-tuple-element.32.refs_0_.refs_10_), custom_call_target="tpu_custom_call" | custom-call | flops 1 | bytes 1 | tf_op jit(solution)/shard_map/project/pallas_call | solution.py:533
  79.1 0.7 project.3.refs_4_
  79.8 1.9 %tally.1 = f32[2,16,128]{2,1,0:T(8,128)S(1)} custom-call(s32[6]{0:T(128)S(1)} %stack.40.where_ref, f32[2,2,512,128]{3,2,1,0:T(8,128)S(1)} %get-tuple-element.27.refs_0_, f32[2,2,512,128]{3,2,1,0:T(8,128)S(1)} %get-tuple-element.28.refs_1_, f32[2,2,512,128]{3,2,1,0:T(8,128)S(1)} %get-tuple-element.29.refs_2_, ...), custom_call_target="tpu_custom_call" | custom-call | flops 1 | bytes 1 | tf_op jit(solution)/shard_map/tally/pallas_call | solution.py:568
  81.7 0.1 reduce_sum.9
  81.8 1.1 %collective-permute-done.16 = f32[2,16]{1,0:T(2,128)S(1)} collective-permute-done((f32[2,16]{1,0:T(2,128)S(1)}, f32[2,16]{1,0:T(2,128)S(1)}, u32[]{:S(2)}, u32[]{:S(2)}) %collective-permute-start.16) | collective-permute-done | bytes 160 | tf_op jit(solution)/shard_map/ppermute | solution.py:590
  83.0 1.2 %collective-permute-start.17 = (f32[2,16]{1,0:T(2,128)S(1)}, f32[2,16]{1,0:T(2,128)S(1)}, u32[]{:S(2)}, u32[]{:S(2)}) collective-permute-start(f32[2,16]{1,0:T(2,128)S(1)} %add.37), channel_id=1, source_target_pairs={{0,2},{1,3},{2,0},{3,1},{4,6},{5,7},{6,4},{7,5},{8,10},{9,11},{10,... | collective-permute-start | bytes 392 | tf_op jit(solution)/shard_map/ppermute | solution.py:590
  84.2 2.4 %collective-permute-done.17 = f32[2,16]{1,0:T(2,128)S(1)} collective-permute-done((f32[2,16]{1,0:T(2,128)S(1)}, f32[2,16]{1,0:T(2,128)S(1)}, u32[]{:S(2)}, u32[]{:S(2)}) %collective-permute-start.17) | collective-permute-done | bytes 160 | tf_op jit(solution)/shard_map/ppermute | solution.py:590
  86.5 0.7 collective-permute-start.18
  87.2 2.9 %collective-permute-done.18 = f32[2,16]{1,0:T(2,128)S(1)} collective-permute-done((f32[2,16]{1,0:T(2,128)S(1)}, f32[2,16]{1,0:T(2,128)S(1)}, u32[]{:S(2)}, u32[]{:S(2)}) %collective-permute-start.18) | collective-permute-done | bytes 160 | tf_op jit(solution)/shard_map/ppermute | solution.py:590
  90.1 0.9 collective-permute-start.19
  91.0 3.6 %collective-permute-done.19 = f32[2,16]{1,0:T(2,128)S(1)} collective-permute-done((f32[2,16]{1,0:T(2,128)S(1)}, f32[2,16]{1,0:T(2,128)S(1)}, u32[]{:S(2)}, u32[]{:S(2)}) %collective-permute-start.19) | collective-permute-done | bytes 160 | tf_op jit(solution)/shard_map/ppermute | solution.py:590
  94.6 0.7 dynamic-slice_reduce_fusion
  (41 shorter events, 0.1 us)
Async XLA Ops:
  0.0 28.6 %collective-permute-start.2 = (bf16[128,2048]{1,0:T(8,128)(2,1)}, bf16[128,2048]{1,0:T(8,128)(2,1)S(1)}, u32[]{:S(2)}, u32[]{:S(2)}) collective-permute-start(bf16[128,2048]{1,0:T(8,128)(2,1)} %refs_0_.1), channel_id=1, source_target_pairs={{0,12},{1,13},{2,14},{3,15},{4,8},{5,9},{6,10},{7,11},{8,4},{9,5},... | collective-permute-start | bytes 1572872 | tf_op jit(solution)/shard_map/ppermute | solution.py:590
  5.0 23.6 %collective-permute-start = (bf16[128,2048]{1,0:T(8,128)(2,1)}, bf16[128,2048]{1,0:T(8,128)(2,1)S(1)}, u32[]{:S(2)}, u32[]{:S(2)}) collective-permute-start(bf16[128,2048]{1,0:T(8,128)(2,1)} %refs_0_.1), channel_id=1, source_target_pairs={{0,2},{1,3},{2,0},{3,1},{4,6},{5,7},{6,4},{7,5},{8,10},{9,11},{10,... | collective-permute-start | bytes 1572872 | tf_op jit(solution)/shard_map/ppermute | solution.py:590
  6.6 22.1 %collective-permute-start.1 = (bf16[128,2048]{1,0:T(8,128)(2,1)}, bf16[128,2048]{1,0:T(8,128)(2,1)S(1)}, u32[]{:S(2)}, u32[]{:S(2)}) collective-permute-start(bf16[128,2048]{1,0:T(8,128)(2,1)} %refs_0_.1), channel_id=1, source_target_pairs={{0,4},{1,5},{2,6},{3,7},{4,0},{5,1},{6,2},{7,3},{8,12},{9,13},{10,... | collective-permute-start | bytes 1572872 | tf_op jit(solution)/shard_map/ppermute | solution.py:590
  6.6 2.2 %copy-start = (f32[8,512,256]{2,1,0:T(8,128)S(1)}, f32[8,512,256]{2,1,0:T(8,128)}, u32[]{:S(2)}) copy-start(f32[8,512,256]{2,1,0:T(8,128)} %e_ref.3) | copy-start | bytes 12582916
  9.4 10.8 %collective-permute-start.6 = (f32[8,128]{1,0:T(8,128)S(1)}, f32[8,128]{1,0:T(8,128)S(1)}, u32[]{:S(2)}, u32[]{:S(2)}) collective-permute-start(f32[8,128]{1,0:T(8,128)S(1)} %sum_eigenvalues.1.refs_0_), channel_id=1, source_target_pairs={{0,2},{1,3},{2,0},{3,1},{4,6},{5,7},{6,4},{7,5},{8,10},{9,11},{10,... | collective-permute-start | bytes 12296 | tf_op jit(solution)/shard_map/ppermute | solution.py:590
  11.9 25.1 %copy-start.1 = (f32[8,512,256]{2,1,0:T(8,128)S(1)}, f32[8,512,256]{2,1,0:T(8,128)}, u32[]{:S(2)}) copy-start(f32[8,512,256]{2,1,0:T(8,128)} %e_ref.3) | copy-start | bytes 12582916
  11.9 25.1 %copy-start.3 = (bf16[64,128,128]{2,1,0:T(8,128)(2,1)S(1)}, bf16[64,128,128]{2,1,0:T(8,128)(2,1)}, u32[]{:S(2)}) copy-start(bf16[64,128,128]{2,1,0:T(8,128)(2,1)} %ob_ref.1) | copy-start | bytes 6291460
  11.9 25.1 %copy-start.4 = (bf16[16,128,128]{2,1,0:T(8,128)(2,1)S(1)}, bf16[16,128,128]{2,1,0:T(8,128)(2,1)}, u32[]{:S(2)}) copy-start(bf16[16,128,128]{2,1,0:T(8,128)(2,1)} %refs_5_.1) | copy-start | bytes 1572868
  12.0 25.1 %copy-start.7 = (bf16[8,2,512,256]{3,2,1,0:T(8,128)(2,1)S(1)}, bf16[8,2,512,256]{3,2,1,0:T(8,128)(2,1)}, u32[]{:S(2)}) copy-start(bf16[8,2,512,256]{3,2,1,0:T(8,128)(2,1)} %q_ref.1) | copy-start | bytes 12582916
  12.0 25.1 %collective-permute-start.10 = (bf16[3072,128]{1,0:T(8,128)(2,1)S(1)}, bf16[3072,128]{1,0:T(8,128)(2,1)S(1)}, u32[]{:S(2)}, u32[]{:S(2)}) collective-permute-start(bf16[3072,128]{1,0:T(8,128)(2,1)S(1)} %rotate.3), channel_id=1, source_target_pairs={{0,2},{1,3},{2,0},{3,1},{4,6},{5,7},{6,4},{7,5},{8,10},{9,11},{10,... | collective-permute-start | bytes 2359304 | tf_op jit(solution)/shard_map/ppermute | solution.py:590
  16.8 26.9 %copy-start.6 = (bf16[1024,128]{1,0:T(8,128)(2,1)}, bf16[1024,128]{1,0:T(8,128)(2,1)S(1)}, u32[]{:S(2)}) copy-start(bf16[1024,128]{1,0:T(8,128)(2,1)S(1)} %get-tuple-element.26.refs_9_) | copy-start | bytes 786436
  20.2 1.2 %collective-permute-start.7 = (f32[8,128]{1,0:T(8,128)S(1)}, f32[8,128]{1,0:T(8,128)S(1)}, u32[]{:S(2)}, u32[]{:S(2)}) collective-permute-start(f32[8,128]{1,0:T(8,128)S(1)} %hold.2), channel_id=1, source_target_pairs={{0,1},{1,0},{2,3},{3,2},{4,5},{5,4},{6,7},{7,6},{8,9},{9,8},{10,11... | collective-permute-start | bytes 12296 | tf_op jit(solution)/shard_map/ppermute | solution.py:590
  21.4 7.2 %collective-permute-start.8 = (f32[8,128]{1,0:T(8,128)S(1)}, f32[8,128]{1,0:T(8,128)S(1)}, u32[]{:S(2)}, u32[]{:S(2)}) collective-permute-start(f32[8,128]{1,0:T(8,128)S(1)} %add.34), channel_id=1, source_target_pairs={{0,4},{1,5},{2,6},{3,7},{4,0},{5,1},{6,2},{7,3},{8,12},{9,13},{10,... | collective-permute-start | bytes 12296 | tf_op jit(solution)/shard_map/ppermute | solution.py:590
  28.7 6.2 %collective-permute-start.9 = (f32[8,128]{1,0:T(8,128)S(1)}, f32[8,128]{1,0:T(8,128)S(1)}, u32[]{:S(2)}, u32[]{:S(2)}) collective-permute-start(f32[8,128]{1,0:T(8,128)S(1)} %hold.3), channel_id=1, source_target_pairs={{0,8},{1,9},{2,10},{3,11},{4,12},{5,13},{6,14},{7,15},{8,0},{9,1},... | collective-permute-start | bytes 12296 | tf_op jit(solution)/shard_map/ppermute | solution.py:590
  29.8 29.1 %collective-permute-start.3 = (bf16[256,2048]{1,0:T(8,128)(2,1)S(1)}, bf16[256,2048]{1,0:T(8,128)(2,1)S(1)}, u32[]{:S(2)}, u32[]{:S(2)}) collective-permute-start(bf16[256,2048]{1,0:T(8,128)(2,1)S(1)} %get-tuple-element.22.refs_0_), channel_id=1, source_target_pairs={{0,2},{1,3},{2,0},{3,1},{4,6},{5,7},{6,4},{7,5},{8,10},{9,11},{10,... | collective-permute-start | bytes 3145736 | tf_op jit(solution)/shard_map/ppermute | solution.py:590
  30.9 25.4 %collective-permute-start.5 = (bf16[2048,128]{1,0:T(8,128)(2,1)S(1)}, bf16[2048,128]{1,0:T(8,128)(2,1)S(1)}, u32[]{:S(2)}, u32[]{:S(2)}) collective-permute-start(bf16[2048,128]{1,0:T(8,128)(2,1)S(1)} %get-tuple-element.23), channel_id=1, source_target_pairs={{0,8},{1,9},{2,10},{3,11},{4,12},{5,13},{6,14},{7,15},{8,0},{9,1},... | collective-permute-start | bytes 1572872 | tf_op jit(solution)/shard_map/ppermute | solution.py:590
  33.2 25.6 %collective-permute-start.4 = (bf16[128,2048]{1,0:T(8,128)(2,1)S(1)}, bf16[128,2048]{1,0:T(8,128)(2,1)S(1)}, u32[]{:S(2)}, u32[]{:S(2)}) collective-permute-start(bf16[128,2048]{1,0:T(8,128)(2,1)S(1)} %collective-permute-done.2.b_ref.refs_1_.refs_3_), channel_id=1, source_target_pairs={{0,4},{1,5},{2,6},{3,7},{4,0},{5,1},{6,2},{7,3},{8,12},{9,13},{10,... | collective-permute-start | bytes 1572872 | tf_op jit(solution)/shard_map/ppermute | solution.py:590
  37.0 6.6 %copy-start.2 = (bf16[3072,128]{1,0:T(8,128)(2,1)}, bf16[3072,128]{1,0:T(8,128)(2,1)S(1)}, u32[]{:S(2)}) copy-start(bf16[3072,128]{1,0:T(8,128)(2,1)S(1)} %collective-permute-done.10.refs_3_.refs_10_.a_ref) | copy-start | bytes 2359300
  43.7 18.9 %collective-permute-start.11 = (bf16[2,512,2048]{2,1,0:T(8,128)(2,1)}, bf16[2,512,2048]{2,1,0:T(8,128)(2,1)}, u32[]{:S(2)}, u32[]{:S(2)}) collective-permute-start(bf16[2,512,2048]{2,1,0:T(8,128)(2,1)} %precondition.1.refs_1_.refs_11_), channel_id=1, source_target_pairs={{0,1},{1,0},{2,3},{3,2},{4,5},{5,4},{6,7},{7,6},{8,9},{9,8},{10,11... | collective-permute-start | bytes 12582920 | tf_op jit(solution)/shard_map/ppermute | solution.py:590
  44.8 35.0 %collective-permute-start.14 = (bf16[2048,128]{1,0:T(8,128)(2,1)}, bf16[2048,128]{1,0:T(8,128)(2,1)}, u32[]{:S(2)}, u32[]{:S(2)}) collective-permute-start(bf16[2048,128]{1,0:T(8,128)(2,1)} %get-tuple-element.35), channel_id=1, source_target_pairs={{0,4},{1,5},{2,6},{3,7},{4,0},{5,1},{6,2},{7,3},{8,12},{9,13},{10,... | collective-permute-start | bytes 1572872 | tf_op jit(solution)/shard_map/ppermute | solution.py:590
  56.2 3.8 %copy-start.5 = (bf16[2048,128]{1,0:T(8,128)(2,1)}, bf16[2048,128]{1,0:T(8,128)(2,1)S(1)}, u32[]{:S(2)}) copy-start(bf16[2048,128]{1,0:T(8,128)(2,1)S(1)} %collective-permute-done.5.m_ref.refs_8_) | copy-start | bytes 1572868
  56.2 5.9 %copy-start.8 = (s32[16]{0:T(128)S(1)}, s32[16]{0:T(128)}, u32[]{:S(2)}) copy-start(s32[16]{0:T(128)} %param.13) | copy-start | bytes 196
  56.2 23.6 %collective-permute-start.15 = (bf16[2048,128]{1,0:T(8,128)(2,1)}, bf16[2048,128]{1,0:T(8,128)(2,1)}, u32[]{:S(2)}, u32[]{:S(2)}) collective-permute-start(bf16[2048,128]{1,0:T(8,128)(2,1)} %get-tuple-element.36), channel_id=1, source_target_pairs={{0,12},{1,13},{2,14},{3,15},{4,8},{5,9},{6,10},{7,11},{8,4},{9,5},... | collective-permute-start | bytes 1572872 | tf_op jit(solution)/shard_map/ppermute | solution.py:590
  60.0 16.2 %collective-permute-start.13 = (bf16[1536,128]{1,0:T(8,128)(2,1)}, bf16[1536,128]{1,0:T(8,128)(2,1)}, u32[]{:S(2)}, u32[]{:S(2)}) collective-permute-start(bf16[1536,128]{1,0:T(8,128)(2,1)} %get-tuple-element.24.refs_6_), channel_id=1, source_target_pairs={{0,2},{1,3},{2,0},{3,1},{4,6},{5,7},{6,4},{7,5},{8,10},{9,11},{10,... | collective-permute-start | bytes 1179656 | tf_op jit(solution)/shard_map/ppermute | solution.py:590
  60.8 18.3 %collective-permute-start.12 = (bf16[1536,128]{1,0:T(8,128)(2,1)S(1)}, bf16[1536,128]{1,0:T(8,128)(2,1)S(1)}, u32[]{:S(2)}, u32[]{:S(2)}) collective-permute-start(bf16[1536,128]{1,0:T(8,128)(2,1)S(1)} %get-tuple-element.25.refs_7_), channel_id=1, source_target_pairs={{0,2},{1,3},{2,0},{3,1},{4,6},{5,7},{6,4},{7,5},{8,10},{9,11},{10,... | collective-permute-start | bytes 1179656 | tf_op jit(solution)/shard_map/ppermute | solution.py:590
  81.8 1.1 %collective-permute-start.16 = (f32[2,16]{1,0:T(2,128)S(1)}, f32[2,16]{1,0:T(2,128)S(1)}, u32[]{:S(2)}, u32[]{:S(2)}) collective-permute-start(f32[2,16]{1,0:T(2,128)S(1)} %reduce_sum.9), channel_id=1, source_target_pairs={{0,1},{1,0},{2,3},{3,2},{4,5},{5,4},{6,7},{7,6},{8,9},{9,8},{10,11... | collective-permute-start | bytes 392 | tf_op jit(solution)/shard_map/ppermute | solution.py:590
  83.0 3.6 %collective-permute-start.17 = (f32[2,16]{1,0:T(2,128)S(1)}, f32[2,16]{1,0:T(2,128)S(1)}, u32[]{:S(2)}, u32[]{:S(2)}) collective-permute-start(f32[2,16]{1,0:T(2,128)S(1)} %add.37), channel_id=1, source_target_pairs={{0,2},{1,3},{2,0},{3,1},{4,6},{5,7},{6,4},{7,5},{8,10},{9,11},{10,... | collective-permute-start | bytes 392 | tf_op jit(solution)/shard_map/ppermute | solution.py:590
  86.5 3.6 %collective-permute-start.18 = (f32[2,16]{1,0:T(2,128)S(1)}, f32[2,16]{1,0:T(2,128)S(1)}, u32[]{:S(2)}, u32[]{:S(2)}) collective-permute-start(f32[2,16]{1,0:T(2,128)S(1)} %add.38), channel_id=1, source_target_pairs={{0,4},{1,5},{2,6},{3,7},{4,0},{5,1},{6,2},{7,3},{8,12},{9,13},{10,... | collective-permute-start | bytes 392 | tf_op jit(solution)/shard_map/ppermute | solution.py:590
  90.1 4.5 %collective-permute-start.19 = (f32[2,16]{1,0:T(2,128)S(1)}, f32[2,16]{1,0:T(2,128)S(1)}, u32[]{:S(2)}, u32[]{:S(2)}) collective-permute-start(f32[2,16]{1,0:T(2,128)S(1)} %add.39), channel_id=1, source_target_pairs={{0,8},{1,9},{2,10},{3,11},{4,12},{5,13},{6,14},{7,15},{8,0},{9,1},... | collective-permute-start | bytes 392 | tf_op jit(solution)/shard_map/ppermute | solution.py:590

commit v6 on v5

--- a/solution.py
+++ b/solution.py
@@ -189,6 +189,24 @@
             rest_ref[i * width - cut : (i + 1) * width - cut, :] = turned
 
 
+def turn_inputs(arrays, in_basis):
+    count, width, _ = in_basis.shape
+    tokens = arrays[0].shape[0]
+
+    def body(*refs):
+        for n in range(len(arrays)):
+            turn(refs[n], 0, tokens, refs[len(arrays)], refs[len(arrays) + 1 + n])
+
+    vmem = pl.BlockSpec(memory_space=pltpu.VMEM)
+    return call(
+        body,
+        in_specs=[vmem] * (len(arrays) + 1),
+        out_specs=[vmem] * len(arrays),
+        out_shape=[jax.ShapeDtypeStruct((count * width, tokens), BF16)] * len(arrays),
+        name="turn_inputs",
+    )(*arrays, in_basis)
+
+
 def pair_up(a, b, held, after):
     def body(a_ref, b_ref, *refs):
         o_ref = refs[1 + len(after)]
@@ -387,12 +405,13 @@
     all_pieces = [turned_piece] + list(pieces)
     count = len(all_pieces)
     raw = [x for x, _ in pieces] + list(early)
+    ready = [x.shape[0] == features for x, _ in raw]
     cut = turned_piece[0][0].shape[0]
     raw_place = [next(i for i, o in enumerate(order) if o is x) for x, _ in raw]
-    heights = [array.shape[0] for array in order]
+    heights = [0 if a.shape[0] == features else a.shape[0] for a in order]
     tops = [sum(heights[:i]) for i in range(len(heights))]
     grads = [g for _, (g, _) in all_pieces]
-    operands = list(order) + [in_hbm(in_basis), *turned_piece[0]]
+    operands = [in_hbm(a) for a in order] + [in_hbm(in_basis), *turned_piece[0]]
     operands += [in_hbm(g) for g in grads] + [own, sibling, starts, ends]
 
     def body(where_ref, *refs):
@@ -405,12 +424,14 @@
         t_refs = refs[len(operands) + 2 : -7]
         raw_all, basis_ref, x_all, g_all, x_sems, g_sems, p_sems = refs[-7:]
         x_copies = [pltpu.make_async_copy(basis_hbm, basis_ref, x_sems.at[len(order)])]
-        x_copies += [
-            pltpu.make_async_copy(
-                raw_refs[i], raw_all.at[pl.ds(tops[i], heights[i])], x_sems.at[i]
-            )
-            for i in range(len(order))
-        ]
+        for n, i in enumerate(raw_place):
+            if ready[n]:
+                place = x_all.at[:, pl.ds((n + 1) * tokens, tokens)]
+                x_copies.append(pltpu.make_async_copy(raw_refs[i], place, x_sems.at[i]))
+        for i in range(len(order)):
+            if heights[i]:
+                place = raw_all.at[pl.ds(tops[i], heights[i])]
+                x_copies.append(pltpu.make_async_copy(raw_refs[i], place, x_sems.at[i]))
         copies = [
             [
                 pltpu.make_async_copy(p_ref.at[q], both_ref.at[c, q], p_sems.at[c, q])
@@ -446,6 +467,8 @@
         for copy in x_copies:
             copy.wait()
         for n, (_, first) in enumerate(raw):
+            if ready[n]:
+                continue
             turn(raw_all, tops[raw_place[n]] + first, tokens, basis_ref, x_all, (n + 1) * tokens)
         scores = [[jnp.zeros((1, tokens), F32)] * queries for _ in all_pieces]
         for c in range(2):
@@ -621,7 +644,8 @@
     near_g = swap(near_g, 4)
     g_far = swap(g_far, 12)
     cut = features * 3 // 4
-    turned = last_round(middle_x, middle, in_basis, cut, [sides, own])
+    x0, x1, x2, x6 = turn_inputs([layer_inputs, side_x, near_x, far_x], in_basis)
+    turned = last_round(middle_x, middle, in_basis, cut, [sides, own, x0])
     high, low = [swap(value, 2) for value in turned]
 
     doc_ends = jnp.cumsum(doc_lengths)
@@ -633,18 +657,17 @@
     def where(*offsets):
         return jnp.stack([core] + [me ^ (2 * k) for k in offsets]).astype(jnp.int32)
 
-    layer_inputs = in_hbm(layer_inputs)
     running, both, *kept = join_and_tally(
         where(4, 0, 1),
         (turned, (middle, 0)),
-        [((layer_inputs, 0), (g_own, 0)), ((side_x, 0), (side_g, 0))],
-        [(near_x, 0), (sides, 0), (far_x, 0), (sides, tokens)],
+        [((x0, 0), (g_own, 0)), ((x1, 0), (side_g, 0))],
+        [(x2, 0), (sides, 0), (x6, 0), (sides, tokens)],
         in_basis,
         own,
         sibling,
         starts,
         ends,
-        [layer_inputs, side_x, near_x, far_x, sides],
+        [x0, x1, x2, x6, sides],
     )
     part_way = project(high, (0, cut), both, [running])
     kept.append(project(low, (cut, features), both, [], part_way))

time: 95.5 us -> 94.3 us (0.987)
  Pallas kernels: 33.7 us -> 32.2 us
  waiting for transfers between devices: 35.2 us -> 34 us
  starting transfers between devices: 22.5 us -> 23.6 us
    ppermute x20, waiting for transfers between devices: 35.2 us -> 34 us  [swap(): return lax.ppermute(value, 'dp', [(i, i ^ offset) for i in range(devices)])]
    ppermute x20, starting transfers between devices: 22.5 us -> 23.6 us  [swap(): return lax.ppermute(value, 'dp', [(i, i ^ offset) for i in range(devices)])]
    pallas_call x2, Pallas kernels: 3.5 us -> 2.51 us  [project(): call(body, in_specs=[vmem] * (2 + len(bases)) + [pl.BlockSpec(memory_spac...]
    unnamed x18 -> x30, local copies, waits for them, and re-layouts: 2.23 us -> 2.7 us
  transfers between devices with their start and end apart: 20 -> 20, of which waited for: 9 -> 10; matrix products, arithmetic and copies ran while one was open for 1% -> 1% of each run, Pallas kernels for 33% -> 33%
where the time goes in v6:
time: 94.3 us; the launch traced here: 94.1 us
  waiting for transfers between devices  34 us (36%)
  Pallas kernels  32.2 us (34%)
  starting transfers between devices  23.6 us (25%)
  local copies, waits for them, and re-layouts  3.7 us (4%)
    ppermute x20, waiting for transfers between devices, swap(): return lax.ppermute(value, 'dp', [(i, i ^ offset) for i in range(devices)])  34 us
    ppermute x20, starting transfers between devices, swap(): return lax.ppermute(value, 'dp', [(i, i ^ offset) for i in range(devices)])  23.6 us
    pallas_call x1, Pallas kernels, join_and_tally(): call(body, in_specs=[pl.BlockSpec(memory_space=pltpu.SMEM)] + [hbm] * (le...  14.1 us
    pallas_call x1, Pallas kernels, precondition_rows(): call(body, grid_spec=grid_spec, out_shape=jax.ShapeDtypeStruct((queries,...  6.64 us
    pallas_call x2, Pallas kernels, rotate(): call(body, cost=cost, in_specs=[pl.BlockSpec(memory_space=pltpu.SMEM), hb...  4.59 us
    unnamed x30, local copies, waits for them, and re-layouts  2.7 us
    pallas_call x2, Pallas kernels, project(): call(body, in_specs=[vmem] * (2 + len(bases)) + [pl.BlockSpec(memory_spac...  2.51 us
  transfers between devices with their start and end apart: 20, of which 10 were waited for; matrix products, arithmetic and copies ran while one was open for 1% of the time, Pallas kernels for 33%

profile of v6, /device:TPU:0, one launch (start us, length us, event | category | flops | bytes accessed | tf_op | source)
XLA Modules:
  0.0 94.1 jit_solution(13180417844773755383)
XLA Ops:
  0.0 5.0 %collective-permute-start.2 = (bf16[128,2048]{1,0:T(8,128)(2,1)}, bf16[128,2048]{1,0:T(8,128)(2,1)S(1)}, u32[]{:S(2)}, u32[]{:S(2)}) collective-permute-start(bf16[128,2048]{1,0:T(8,128)(2,1)} %refs_0_.1), channel_id=1, source_target_pairs={{0,12},{1,13},{2,14},{3,15},{4,8},{5,9},{6,10},{7,11},{8,4},{9,5},... | collective-permute-start | bytes 1572872 | tf_op jit(solution)/shard_map/ppermute | solution.py:613
  5.0 1.5 %collective-permute-start = (bf16[128,2048]{1,0:T(8,128)(2,1)}, bf16[128,2048]{1,0:T(8,128)(2,1)S(1)}, u32[]{:S(2)}, u32[]{:S(2)}) collective-permute-start(bf16[128,2048]{1,0:T(8,128)(2,1)} %refs_0_.1), channel_id=1, source_target_pairs={{0,2},{1,3},{2,0},{3,1},{4,6},{5,7},{6,4},{7,5},{8,10},{9,11},{10,... | collective-permute-start | bytes 1572872 | tf_op jit(solution)/shard_map/ppermute | solution.py:613
  6.6 2.2 %copy-done = f32[8,512,256]{2,1,0:T(8,128)S(1)} copy-done((f32[8,512,256]{2,1,0:T(8,128)S(1)}, f32[8,512,256]{2,1,0:T(8,128)}, u32[]{:S(2)}) %copy-start) | copy-done | bytes 4194328
  8.8 0.7 sum_eigenvalues.1.refs_0_
  9.4 0.6 collective-permute-start.6
  10.0 1.9 %rotate.3 = bf16[3072,128]{1,0:T(8,128)(2,1)S(1)} custom-call(s32[1]{0:T(128)} %bitcast.9.chip_ref, bf16[128,8192]{1,0:T(8,128)(2,1)} %g_hbm.3, bf16[64,128,128]{2,1,0:T(8,128)(2,1)} %ob_ref.1, f32[8,128]{1,0:T(8,128)S(1)} %sum_eigenvalues.1.refs_0_), custom_call_target="tpu_custom_call" | custom-call | flops 1 | bytes 1 | tf_op jit(solution)/shard_map/rotate/pallas_call | solution.py:162
  11.9 1.6 %collective-permute-start.10 = (bf16[3072,128]{1,0:T(8,128)(2,1)S(1)}, bf16[3072,128]{1,0:T(8,128)(2,1)S(1)}, u32[]{:S(2)}, u32[]{:S(2)}) collective-permute-start(bf16[3072,128]{1,0:T(8,128)(2,1)S(1)} %rotate.3), channel_id=1, source_target_pairs={{0,2},{1,3},{2,0},{3,1},{4,6},{5,7},{6,4},{7,5},{8,10},{9,11},{10,... | collective-permute-start | bytes 2359304 | tf_op jit(solution)/shard_map/ppermute | solution.py:613
  13.5 2.7 %rotate.2 = (bf16[1024,128]{1,0:T(8,128)(2,1)S(1)}, bf16[2048,128]{1,0:T(8,128)(2,1)S(1)}, bf16[1024,128]{1,0:T(8,128)(2,1)S(1)}, bf16[1024,128]{1,0:T(8,128)(2,1)S(1)}) custom-call(s32[1]{0:T(128)} %bitcast.9.chip_ref, bf16[128,8192]{1,0:T(8,128)(2,1)} %g_hbm.3, bf16[64,128,128]{2,1,0:T(8,128)(2,1)} %ob_ref.1), custom_call_target="tpu_custom_call" | custom-call | flops 99999997952 | bytes 1 | tf_op jit(solution)/shard_map/rotate/pallas_call | solution.py:162
  16.2 3.9 %collective-permute-done.6 = f32[8,128]{1,0:T(8,128)S(1)} collective-permute-done((f32[8,128]{1,0:T(8,128)S(1)}, f32[8,128]{1,0:T(8,128)S(1)}, u32[]{:S(2)}, u32[]{:S(2)}) %collective-permute-start.6) | collective-permute-done | bytes 4128 | tf_op jit(solution)/shard_map/ppermute | solution.py:613
  20.2 1.2 %collective-permute-done.7 = f32[8,128]{1,0:T(8,128)S(1)} collective-permute-done((f32[8,128]{1,0:T(8,128)S(1)}, f32[8,128]{1,0:T(8,128)S(1)}, u32[]{:S(2)}, u32[]{:S(2)}) %collective-permute-start.7) | collective-permute-done | bytes 4128 | tf_op jit(solution)/shard_map/ppermute | solution.py:613
  21.4 7.2 %collective-permute-done.8 = f32[8,128]{1,0:T(8,128)S(1)} collective-permute-done((f32[8,128]{1,0:T(8,128)S(1)}, f32[8,128]{1,0:T(8,128)S(1)}, u32[]{:S(2)}, u32[]{:S(2)}) %collective-permute-start.8) | collective-permute-done | bytes 4128 | tf_op jit(solution)/shard_map/ppermute | solution.py:613
  28.6 0.1 pair_up.1
  28.7 1.1 %collective-permute-start.9 = (f32[8,128]{1,0:T(8,128)S(1)}, f32[8,128]{1,0:T(8,128)S(1)}, u32[]{:S(2)}, u32[]{:S(2)}) collective-permute-start(f32[8,128]{1,0:T(8,128)S(1)} %hold.3), channel_id=1, source_target_pairs={{0,8},{1,9},{2,10},{3,11},{4,12},{5,13},{6,14},{7,15},{8,0},{9,1},... | collective-permute-start | bytes 12296 | tf_op jit(solution)/shard_map/ppermute | solution.py:613
  29.8 1.0 %collective-permute-start.3 = (bf16[256,2048]{1,0:T(8,128)(2,1)S(1)}, bf16[256,2048]{1,0:T(8,128)(2,1)S(1)}, u32[]{:S(2)}, u32[]{:S(2)}) collective-permute-start(bf16[256,2048]{1,0:T(8,128)(2,1)S(1)} %get-tuple-element.30.refs_0_), channel_id=1, source_target_pairs={{0,2},{1,3},{2,0},{3,1},{4,6},{5,7},{6,4},{7,5},{8,10},{9,11},{10,... | collective-permute-start | bytes 3145736 | tf_op jit(solution)/shard_map/ppermute | solution.py:613
  30.9 2.4 %collective-permute-start.5 = (bf16[2048,128]{1,0:T(8,128)(2,1)S(1)}, bf16[2048,128]{1,0:T(8,128)(2,1)S(1)}, u32[]{:S(2)}, u32[]{:S(2)}) collective-permute-start(bf16[2048,128]{1,0:T(8,128)(2,1)S(1)} %get-tuple-element.31), channel_id=1, source_target_pairs={{0,8},{1,9},{2,10},{3,11},{4,12},{5,13},{6,14},{7,15},{8,0},{9,1},... | collective-permute-start | bytes 1572872 | tf_op jit(solution)/shard_map/ppermute | solution.py:613
  33.2 1.7 %collective-permute-start.4 = (bf16[128,2048]{1,0:T(8,128)(2,1)S(1)}, bf16[128,2048]{1,0:T(8,128)(2,1)S(1)}, u32[]{:S(2)}, u32[]{:S(2)}) collective-permute-start(bf16[128,2048]{1,0:T(8,128)(2,1)S(1)} %collective-permute-done.2.refs_3_.b_ref.refs_1_), channel_id=1, source_target_pairs={{0,4},{1,5},{2,6},{3,7},{4,0},{5,1},{6,2},{7,3},{8,12},{9,13},{10,... | collective-permute-start | bytes 1572872 | tf_op jit(solution)/shard_map/ppermute | solution.py:613
  34.9 0.8 turn_inputs.1
  35.8 1.3 %collective-permute-done.10.refs_3_.refs_10_.a_ref = bf16[3072,128]{1,0:T(8,128)(2,1)S(1)} collective-permute-done((bf16[3072,128]{1,0:T(8,128)(2,1)S(1)}, bf16[3072,128]{1,0:T(8,128)(2,1)S(1)}, u32[]{:S(2)}, u32[]{:S(2)}) %collective-permute-start.10) | collective-permute-done | bytes 786464 | tf_op jit(solution)/shard_map/ppermute | solution.py:613
  37.1 6.6 %precondition.1.refs_1_.refs_11_ = bf16[2,512,2048]{2,1,0:T(8,128)(2,1)} custom-call(s32[1]{0:T(128)} %bitcast.7.me_ref, bf16[8,2,512,256]{3,2,1,0:T(8,128)(2,1)S(1)} %copy-done.13, f32[8,512,256]{2,1,0:T(8,128)S(1)} %copy-done.1, f32[8,128]{1,0:T(8,128)S(1)} %add.36.s_ref, bf16[64,128,128]{2,1,0:T(8,128)(2,1)S(1)} %copy-done.4, ...), custom_call_target="tpu_custom_call" | custom-call | flops 99999997952 | bytes 1 | tf_op jit(solution)/shard_map/precondition/pallas_call | solution.py:391
  43.7 0.1 collective-permute-start.11
  43.8 1.1 %pack_grads.1 = (bf16[2048,128]{1,0:T(8,128)(2,1)}, bf16[2048,128]{1,0:T(8,128)(2,1)}) custom-call(bf16[1024,128]{1,0:T(8,128)(2,1)S(1)} %get-tuple-element.41.n_ref, bf16[1024,128]{1,0:T(8,128)(2,1)S(1)} %get-tuple-element.42.f_ref, bf16[3072,128]{1,0:T(8,128)(2,1)S(1)} %collective-permute-done.10.refs_3_.refs_10_.a_ref), custom_call_target="tpu_custom_call" | custom-call | flops 1 | bytes 1 | tf_op jit(solution)/shard_map/pack_grads/pallas_call | solution.py:249
  44.9 0.1 collective-permute-start.14
  45.0 11.2 %collective-permute-done.5.m_ref.refs_8_ = bf16[2048,128]{1,0:T(8,128)(2,1)S(1)} collective-permute-done((bf16[2048,128]{1,0:T(8,128)(2,1)S(1)}, bf16[2048,128]{1,0:T(8,128)(2,1)S(1)}, u32[]{:S(2)}, u32[]{:S(2)}) %collective-permute-start.5) | collective-permute-done | bytes 524320 | tf_op jit(solution)/shard_map/ppermute | solution.py:613
  56.2 2.6 %collective-permute-start.15 = (bf16[2048,128]{1,0:T(8,128)(2,1)}, bf16[2048,128]{1,0:T(8,128)(2,1)S(1)}, u32[]{:S(2)}, u32[]{:S(2)}) collective-permute-start(bf16[2048,128]{1,0:T(8,128)(2,1)} %get-tuple-element.44), channel_id=1, source_target_pairs={{0,12},{1,13},{2,14},{3,15},{4,8},{5,9},{6,10},{7,11},{8,4},{9,5},... | collective-permute-start | bytes 1572872 | tf_op jit(solution)/shard_map/ppermute | solution.py:613
  58.9 0.6 last_round.1
  59.5 0.4 copy-done.5
  59.9 0.7 collective-permute-start.13
  60.6 1.3 %collective-permute-start.12 = (bf16[1536,128]{1,0:T(8,128)(2,1)S(1)}, bf16[1536,128]{1,0:T(8,128)(2,1)S(1)}, u32[]{:S(2)}, u32[]{:S(2)}) collective-permute-start(bf16[1536,128]{1,0:T(8,128)(2,1)S(1)} %get-tuple-element.33.refs_7_), channel_id=1, source_target_pairs={{0,2},{1,3},{2,0},{3,1},{4,6},{5,7},{6,4},{7,5},{8,10},{9,11},{10,... | collective-permute-start | bytes 1179656 | tf_op jit(solution)/shard_map/ppermute | solution.py:613
  62.0 0.1 copy.12
  62.1 0.1 reduce
  62.2 0.1 stack.40.where_ref
  62.3 0.1 pad_add_fusion.where_ref
  62.4 0.1 broadcast_in_dim.7.refs_13_.refs_8_
  62.5 0.1 broadcast_in_dim.8.refs_14_.refs_9_
  62.5 14.1 %join_and_tally.1 = (f32[2,16,128]{2,1,0:T(8,128)S(1)}, bf16[2,2,512,2048]{3,2,1,0:T(8,128)(2,1)S(1)}, f32[2,2,512,128]{3,2,1,0:T(8,128)S(1)}, f32[2,2,512,128]{...) custom-call(s32[4]{0:T(128)S(1)} %pad_add_fusion.where_ref, ...), custom_call_target="tpu_custom_call" | custom-call | flops 1 | bytes 1 | tf_op jit(solution)/shard_map/join_and_tally/pallas_call | solution.py:501
  76.6 1.8 %project.2.refs_0_ = f32[2,2,512,128]{3,2,1,0:T(8,128)S(1)} custom-call(bf16[1536,128]{1,0:T(8,128)(2,1)S(1)} %collective-permute-done.13.x_ref, bf16[2,2,512,2048]{3,2,1,0:T(8,128)(2,1)S(1)} %get-tuple-element.39.p_ref, f32[2,16,128]{2,1,0:T(8,128)S(1)} %get-tuple-element.40.refs_0_.refs_10_), custom_call_target="tpu_custom_call" | custom-call | flops 1 | bytes 1 | tf_op jit(solution)/shard_map/project/pallas_call | solution.py:556
  78.4 0.7 project.3.refs_4_
  79.2 0.2 collective-permute-done.15.refs_6_
  79.4 1.2 %tally.1 = f32[2,16,128]{2,1,0:T(8,128)S(1)} custom-call(s32[6]{0:T(128)S(1)} %stack.40.where_ref, f32[2,2,512,128]{3,2,1,0:T(8,128)S(1)} %get-tuple-element.35.refs_0_, f32[2,2,512,128]{3,2,1,0:T(8,128)S(1)} %get-tuple-element.36.refs_1_, f32[2,2,512,128]{3,2,1,0:T(8,128)S(1)} %get-tuple-element.37.refs_2_, ...), custom_call_target="tpu_custom_call" | custom-call | flops 1 | bytes 1 | tf_op jit(solution)/shard_map/tally/pallas_call | solution.py:591
  80.6 0.1 reduce_sum.9
  80.7 1.1 %collective-permute-done.16 = f32[2,16]{1,0:T(2,128)S(1)} collective-permute-done((f32[2,16]{1,0:T(2,128)S(1)}, f32[2,16]{1,0:T(2,128)S(1)}, u32[]{:S(2)}, u32[]{:S(2)}) %collective-permute-start.16) | collective-permute-done | bytes 160 | tf_op jit(solution)/shard_map/ppermute | solution.py:613
  81.8 1.6 %collective-permute-start.17 = (f32[2,16]{1,0:T(2,128)S(1)}, f32[2,16]{1,0:T(2,128)S(1)}, u32[]{:S(2)}, u32[]{:S(2)}) collective-permute-start(f32[2,16]{1,0:T(2,128)S(1)} %add.37), channel_id=1, source_target_pairs={{0,2},{1,3},{2,0},{3,1},{4,6},{5,7},{6,4},{7,5},{8,10},{9,11},{10,... | collective-permute-start | bytes 392 | tf_op jit(solution)/shard_map/ppermute | solution.py:613
  83.4 2.0 %collective-permute-done.17 = f32[2,16]{1,0:T(2,128)S(1)} collective-permute-done((f32[2,16]{1,0:T(2,128)S(1)}, f32[2,16]{1,0:T(2,128)S(1)}, u32[]{:S(2)}, u32[]{:S(2)}) %collective-permute-start.17) | collective-permute-done | bytes 160 | tf_op jit(solution)/shard_map/ppermute | solution.py:613
  85.4 1.1 %collective-permute-start.18 = (f32[2,16]{1,0:T(2,128)S(1)}, f32[2,16]{1,0:T(2,128)S(1)}, u32[]{:S(2)}, u32[]{:S(2)}) collective-permute-start(f32[2,16]{1,0:T(2,128)S(1)} %add.38), channel_id=1, source_target_pairs={{0,4},{1,5},{2,6},{3,7},{4,0},{5,1},{6,2},{7,3},{8,12},{9,13},{10,... | collective-permute-start | bytes 392 | tf_op jit(solution)/shard_map/ppermute | solution.py:613
  86.5 2.5 %collective-permute-done.18 = f32[2,16]{1,0:T(2,128)S(1)} collective-permute-done((f32[2,16]{1,0:T(2,128)S(1)}, f32[2,16]{1,0:T(2,128)S(1)}, u32[]{:S(2)}, u32[]{:S(2)}) %collective-permute-start.18) | collective-permute-done | bytes 160 | tf_op jit(solution)/shard_map/ppermute | solution.py:613
  89.0 1.2 %collective-permute-start.19 = (f32[2,16]{1,0:T(2,128)S(1)}, f32[2,16]{1,0:T(2,128)S(1)}, u32[]{:S(2)}, u32[]{:S(2)}) collective-permute-start(f32[2,16]{1,0:T(2,128)S(1)} %add.39), channel_id=1, source_target_pairs={{0,8},{1,9},{2,10},{3,11},{4,12},{5,13},{6,14},{7,15},{8,0},{9,1},... | collective-permute-start | bytes 392 | tf_op jit(solution)/shard_map/ppermute | solution.py:613
  90.2 3.2 %collective-permute-done.19 = f32[2,16]{1,0:T(2,128)S(1)} collective-permute-done((f32[2,16]{1,0:T(2,128)S(1)}, f32[2,16]{1,0:T(2,128)S(1)}, u32[]{:S(2)}, u32[]{:S(2)}) %collective-permute-start.19) | collective-permute-done | bytes 160 | tf_op jit(solution)/shard_map/ppermute | solution.py:613
  93.4 0.7 dynamic-slice_reduce_fusion
  (54 shorter events, 0.2 us)
Async XLA Ops:
  0.0 28.6 %collective-permute-start.2 = (bf16[128,2048]{1,0:T(8,128)(2,1)}, bf16[128,2048]{1,0:T(8,128)(2,1)S(1)}, u32[]{:S(2)}, u32[]{:S(2)}) collective-permute-start(bf16[128,2048]{1,0:T(8,128)(2,1)} %refs_0_.1), channel_id=1, source_target_pairs={{0,12},{1,13},{2,14},{3,15},{4,8},{5,9},{6,10},{7,11},{8,4},{9,5},... | collective-permute-start | bytes 1572872 | tf_op jit(solution)/shard_map/ppermute | solution.py:613
  5.0 23.6 %collective-permute-start = (bf16[128,2048]{1,0:T(8,128)(2,1)}, bf16[128,2048]{1,0:T(8,128)(2,1)S(1)}, u32[]{:S(2)}, u32[]{:S(2)}) collective-permute-start(bf16[128,2048]{1,0:T(8,128)(2,1)} %refs_0_.1), channel_id=1, source_target_pairs={{0,2},{1,3},{2,0},{3,1},{4,6},{5,7},{6,4},{7,5},{8,10},{9,11},{10,... | collective-permute-start | bytes 1572872 | tf_op jit(solution)/shard_map/ppermute | solution.py:613
  6.6 22.1 %collective-permute-start.1 = (bf16[128,2048]{1,0:T(8,128)(2,1)}, bf16[128,2048]{1,0:T(8,128)(2,1)S(1)}, u32[]{:S(2)}, u32[]{:S(2)}) collective-permute-start(bf16[128,2048]{1,0:T(8,128)(2,1)} %refs_0_.1), channel_id=1, source_target_pairs={{0,4},{1,5},{2,6},{3,7},{4,0},{5,1},{6,2},{7,3},{8,12},{9,13},{10,... | collective-permute-start | bytes 1572872 | tf_op jit(solution)/shard_map/ppermute | solution.py:613
  6.6 2.2 %copy-start = (f32[8,512,256]{2,1,0:T(8,128)S(1)}, f32[8,512,256]{2,1,0:T(8,128)}, u32[]{:S(2)}) copy-start(f32[8,512,256]{2,1,0:T(8,128)} %e_ref.3) | copy-start | bytes 12582916
  9.4 10.8 %collective-permute-start.6 = (f32[8,128]{1,0:T(8,128)S(1)}, f32[8,128]{1,0:T(8,128)S(1)}, u32[]{:S(2)}, u32[]{:S(2)}) collective-permute-start(f32[8,128]{1,0:T(8,128)S(1)} %sum_eigenvalues.1.refs_0_), channel_id=1, source_target_pairs={{0,2},{1,3},{2,0},{3,1},{4,6},{5,7},{6,4},{7,5},{8,10},{9,11},{10,... | collective-permute-start | bytes 12296 | tf_op jit(solution)/shard_map/ppermute | solution.py:613
  11.9 23.0 %copy-start.3 = (bf16[16,128,128]{2,1,0:T(8,128)(2,1)S(1)}, bf16[16,128,128]{2,1,0:T(8,128)(2,1)}, u32[]{:S(2)}) copy-start(bf16[16,128,128]{2,1,0:T(8,128)(2,1)} %refs_5_.1) | copy-start | bytes 1572868
  11.9 23.0 %copy-start.11 = (bf16[128,2048]{1,0:T(8,128)(2,1)S(1)}, bf16[128,2048]{1,0:T(8,128)(2,1)}, u32[]{:S(2)}) copy-start(bf16[128,2048]{1,0:T(8,128)(2,1)} %refs_0_.1) | copy-start | bytes 1572868
  11.9 25.1 %collective-permute-start.10 = (bf16[3072,128]{1,0:T(8,128)(2,1)S(1)}, bf16[3072,128]{1,0:T(8,128)(2,1)S(1)}, u32[]{:S(2)}, u32[]{:S(2)}) collective-permute-start(bf16[3072,128]{1,0:T(8,128)(2,1)S(1)} %rotate.3), channel_id=1, source_target_pairs={{0,2},{1,3},{2,0},{3,1},{4,6},{5,7},{6,4},{7,5},{8,10},{9,11},{10,... | collective-permute-start | bytes 2359304 | tf_op jit(solution)/shard_map/ppermute | solution.py:613
  13.5 23.5 %copy-start.13 = (bf16[8,2,512,256]{3,2,1,0:T(8,128)(2,1)S(1)}, bf16[8,2,512,256]{3,2,1,0:T(8,128)(2,1)}, u32[]{:S(2)}) copy-start(bf16[8,2,512,256]{3,2,1,0:T(8,128)(2,1)} %q_ref.1) | copy-start | bytes 12582916
  16.2 27.5 %copy-start.12 = (bf16[1024,128]{1,0:T(8,128)(2,1)}, bf16[1024,128]{1,0:T(8,128)(2,1)S(1)}, u32[]{:S(2)}) copy-start(bf16[1024,128]{1,0:T(8,128)(2,1)S(1)} %get-tuple-element.34.refs_9_) | copy-start | bytes 786436
  16.2 20.8 %copy-start.1 = (f32[8,512,256]{2,1,0:T(8,128)S(1)}, f32[8,512,256]{2,1,0:T(8,128)}, u32[]{:S(2)}) copy-start(f32[8,512,256]{2,1,0:T(8,128)} %e_ref.3) | copy-start | bytes 12582916
  16.2 20.8 %copy-start.4 = (bf16[64,128,128]{2,1,0:T(8,128)(2,1)S(1)}, bf16[64,128,128]{2,1,0:T(8,128)(2,1)}, u32[]{:S(2)}) copy-start(bf16[64,128,128]{2,1,0:T(8,128)(2,1)} %ob_ref.1) | copy-start | bytes 6291460
  20.2 1.2 %collective-permute-start.7 = (f32[8,128]{1,0:T(8,128)S(1)}, f32[8,128]{1,0:T(8,128)S(1)}, u32[]{:S(2)}, u32[]{:S(2)}) collective-permute-start(f32[8,128]{1,0:T(8,128)S(1)} %hold.2), channel_id=1, source_target_pairs={{0,1},{1,0},{2,3},{3,2},{4,5},{5,4},{6,7},{7,6},{8,9},{9,8},{10,11... | collective-permute-start | bytes 12296 | tf_op jit(solution)/shard_map/ppermute | solution.py:613
  21.4 7.2 %collective-permute-start.8 = (f32[8,128]{1,0:T(8,128)S(1)}, f32[8,128]{1,0:T(8,128)S(1)}, u32[]{:S(2)}, u32[]{:S(2)}) collective-permute-start(f32[8,128]{1,0:T(8,128)S(1)} %add.34), channel_id=1, source_target_pairs={{0,4},{1,5},{2,6},{3,7},{4,0},{5,1},{6,2},{7,3},{8,12},{9,13},{10,... | collective-permute-start | bytes 12296 | tf_op jit(solution)/shard_map/ppermute | solution.py:613
  28.7 7.0 %collective-permute-start.9 = (f32[8,128]{1,0:T(8,128)S(1)}, f32[8,128]{1,0:T(8,128)S(1)}, u32[]{:S(2)}, u32[]{:S(2)}) collective-permute-start(f32[8,128]{1,0:T(8,128)S(1)} %hold.3), channel_id=1, source_target_pairs={{0,8},{1,9},{2,10},{3,11},{4,12},{5,13},{6,14},{7,15},{8,0},{9,1},... | collective-permute-start | bytes 12296 | tf_op jit(solution)/shard_map/ppermute | solution.py:613
  29.8 29.1 %collective-permute-start.3 = (bf16[256,2048]{1,0:T(8,128)(2,1)S(1)}, bf16[256,2048]{1,0:T(8,128)(2,1)S(1)}, u32[]{:S(2)}, u32[]{:S(2)}) collective-permute-start(bf16[256,2048]{1,0:T(8,128)(2,1)S(1)} %get-tuple-element.30.refs_0_), channel_id=1, source_target_pairs={{0,2},{1,3},{2,0},{3,1},{4,6},{5,7},{6,4},{7,5},{8,10},{9,11},{10,... | collective-permute-start | bytes 3145736 | tf_op jit(solution)/shard_map/ppermute | solution.py:613
  30.9 25.4 %collective-permute-start.5 = (bf16[2048,128]{1,0:T(8,128)(2,1)S(1)}, bf16[2048,128]{1,0:T(8,128)(2,1)S(1)}, u32[]{:S(2)}, u32[]{:S(2)}) collective-permute-start(bf16[2048,128]{1,0:T(8,128)(2,1)S(1)} %get-tuple-element.31), channel_id=1, source_target_pairs={{0,8},{1,9},{2,10},{3,11},{4,12},{5,13},{6,14},{7,15},{8,0},{9,1},... | collective-permute-start | bytes 1572872 | tf_op jit(solution)/shard_map/ppermute | solution.py:613
  33.2 25.6 %collective-permute-start.4 = (bf16[128,2048]{1,0:T(8,128)(2,1)S(1)}, bf16[128,2048]{1,0:T(8,128)(2,1)S(1)}, u32[]{:S(2)}, u32[]{:S(2)}) collective-permute-start(bf16[128,2048]{1,0:T(8,128)(2,1)S(1)} %collective-permute-done.2.refs_3_.b_ref.refs_1_), channel_id=1, source_target_pairs={{0,4},{1,5},{2,6},{3,7},{4,0},{5,1},{6,2},{7,3},{8,12},{9,13},{10,... | collective-permute-start | bytes 1572872 | tf_op jit(solution)/shard_map/ppermute | solution.py:613
  35.7 8.0 %copy-start.8 = (bf16[2048,128]{1,0:T(8,128)(2,1)}, bf16[2048,128]{1,0:T(8,128)(2,1)S(1)}, u32[]{:S(2)}) copy-start(bf16[2048,128]{1,0:T(8,128)(2,1)S(1)} %get-tuple-element.26.refs_1_) | copy-start | bytes 1572868
  35.7 8.0 %copy-start.9 = (bf16[2048,128]{1,0:T(8,128)(2,1)}, bf16[2048,128]{1,0:T(8,128)(2,1)S(1)}, u32[]{:S(2)}) copy-start(bf16[2048,128]{1,0:T(8,128)(2,1)S(1)} %get-tuple-element.27.refs_2_) | copy-start | bytes 1572868
  35.7 8.0 %copy-start.10 = (bf16[2048,128]{1,0:T(8,128)(2,1)}, bf16[2048,128]{1,0:T(8,128)(2,1)S(1)}, u32[]{:S(2)}) copy-start(bf16[2048,128]{1,0:T(8,128)(2,1)S(1)} %get-tuple-element.28.refs_3_) | copy-start | bytes 1572868
  35.7 23.2 %copy-start.7 = (bf16[2048,128]{1,0:T(8,128)(2,1)}, bf16[2048,128]{1,0:T(8,128)(2,1)S(1)}, u32[]{:S(2)}) copy-start(bf16[2048,128]{1,0:T(8,128)(2,1)S(1)} %get-tuple-element.25.refs_2_.refs_0_) | copy-start | bytes 1572868
  37.0 6.8 %copy-start.2 = (bf16[3072,128]{1,0:T(8,128)(2,1)}, bf16[3072,128]{1,0:T(8,128)(2,1)S(1)}, u32[]{:S(2)}) copy-start(bf16[3072,128]{1,0:T(8,128)(2,1)S(1)} %collective-permute-done.10.refs_3_.refs_10_.a_ref) | copy-start | bytes 2359300
  43.7 18.7 %collective-permute-start.11 = (bf16[2,512,2048]{2,1,0:T(8,128)(2,1)}, bf16[2,512,2048]{2,1,0:T(8,128)(2,1)}, u32[]{:S(2)}, u32[]{:S(2)}) collective-permute-start(bf16[2,512,2048]{2,1,0:T(8,128)(2,1)} %precondition.1.refs_1_.refs_11_), channel_id=1, source_target_pairs={{0,1},{1,0},{2,3},{3,2},{4,5},{5,4},{6,7},{7,6},{8,9},{9,8},{10,11... | collective-permute-start | bytes 12582920 | tf_op jit(solution)/shard_map/ppermute | solution.py:613
  44.9 34.2 %collective-permute-start.14 = (bf16[2048,128]{1,0:T(8,128)(2,1)}, bf16[2048,128]{1,0:T(8,128)(2,1)S(1)}, u32[]{:S(2)}, u32[]{:S(2)}) collective-permute-start(bf16[2048,128]{1,0:T(8,128)(2,1)} %get-tuple-element.43), channel_id=1, source_target_pairs={{0,4},{1,5},{2,6},{3,7},{4,0},{5,1},{6,2},{7,3},{8,12},{9,13},{10,... | collective-permute-start | bytes 1572872 | tf_op jit(solution)/shard_map/ppermute | solution.py:613
  56.2 3.2 %copy-start.6 = (bf16[2048,128]{1,0:T(8,128)(2,1)}, bf16[2048,128]{1,0:T(8,128)(2,1)S(1)}, u32[]{:S(2)}) copy-start(bf16[2048,128]{1,0:T(8,128)(2,1)S(1)} %collective-permute-done.5.m_ref.refs_8_) | copy-start | bytes 1572868
  56.2 23.1 %collective-permute-start.15 = (bf16[2048,128]{1,0:T(8,128)(2,1)}, bf16[2048,128]{1,0:T(8,128)(2,1)S(1)}, u32[]{:S(2)}, u32[]{:S(2)}) collective-permute-start(bf16[2048,128]{1,0:T(8,128)(2,1)} %get-tuple-element.44), channel_id=1, source_target_pairs={{0,12},{1,13},{2,14},{3,15},{4,8},{5,9},{6,10},{7,11},{8,4},{9,5},... | collective-permute-start | bytes 1572872 | tf_op jit(solution)/shard_map/ppermute | solution.py:613
  58.9 1.1 %copy-start.5 = (bf16[256,2048]{1,0:T(8,128)(2,1)}, bf16[256,2048]{1,0:T(8,128)(2,1)S(1)}, u32[]{:S(2)}) copy-start(bf16[256,2048]{1,0:T(8,128)(2,1)S(1)} %collective-permute-done.3.refs_0_.refs_4_) | copy-start | bytes 3145732
  58.9 3.1 %copy-start.14 = (s32[16]{0:T(128)S(1)}, s32[16]{0:T(128)}, u32[]{:S(2)}) copy-start(s32[16]{0:T(128)} %param.13) | copy-start | bytes 196
  59.9 16.7 %collective-permute-start.13 = (bf16[1536,128]{1,0:T(8,128)(2,1)S(1)}, bf16[1536,128]{1,0:T(8,128)(2,1)S(1)}, u32[]{:S(2)}, u32[]{:S(2)}) collective-permute-start(bf16[1536,128]{1,0:T(8,128)(2,1)S(1)} %get-tuple-element.32.refs_6_), channel_id=1, source_target_pairs={{0,2},{1,3},{2,0},{3,1},{4,6},{5,7},{6,4},{7,5},{8,10},{9,11},{10,... | collective-permute-start | bytes 1179656 | tf_op jit(solution)/shard_map/ppermute | solution.py:613
  60.6 17.8 %collective-permute-start.12 = (bf16[1536,128]{1,0:T(8,128)(2,1)S(1)}, bf16[1536,128]{1,0:T(8,128)(2,1)S(1)}, u32[]{:S(2)}, u32[]{:S(2)}) collective-permute-start(bf16[1536,128]{1,0:T(8,128)(2,1)S(1)} %get-tuple-element.33.refs_7_), channel_id=1, source_target_pairs={{0,2},{1,3},{2,0},{3,1},{4,6},{5,7},{6,4},{7,5},{8,10},{9,11},{10,... | collective-permute-start | bytes 1179656 | tf_op jit(solution)/shard_map/ppermute | solution.py:613
  80.7 1.1 %collective-permute-start.16 = (f32[2,16]{1,0:T(2,128)S(1)}, f32[2,16]{1,0:T(2,128)S(1)}, u32[]{:S(2)}, u32[]{:S(2)}) collective-permute-start(f32[2,16]{1,0:T(2,128)S(1)} %reduce_sum.9), channel_id=1, source_target_pairs={{0,1},{1,0},{2,3},{3,2},{4,5},{5,4},{6,7},{7,6},{8,9},{9,8},{10,11... | collective-permute-start | bytes 392 | tf_op jit(solution)/shard_map/ppermute | solution.py:613
  81.8 3.6 %collective-permute-start.17 = (f32[2,16]{1,0:T(2,128)S(1)}, f32[2,16]{1,0:T(2,128)S(1)}, u32[]{:S(2)}, u32[]{:S(2)}) collective-permute-start(f32[2,16]{1,0:T(2,128)S(1)} %add.37), channel_id=1, source_target_pairs={{0,2},{1,3},{2,0},{3,1},{4,6},{5,7},{6,4},{7,5},{8,10},{9,11},{10,... | collective-permute-start | bytes 392 | tf_op jit(solution)/shard_map/ppermute | solution.py:613
  85.4 3.6 %collective-permute-start.18 = (f32[2,16]{1,0:T(2,128)S(1)}, f32[2,16]{1,0:T(2,128)S(1)}, u32[]{:S(2)}, u32[]{:S(2)}) collective-permute-start(f32[2,16]{1,0:T(2,128)S(1)} %add.38), channel_id=1, source_target_pairs={{0,4},{1,5},{2,6},{3,7},{4,0},{5,1},{6,2},{7,3},{8,12},{9,13},{10,... | collective-permute-start | bytes 392 | tf_op jit(solution)/shard_map/ppermute | solution.py:613
  89.0 4.5 %collective-permute-start.19 = (f32[2,16]{1,0:T(2,128)S(1)}, f32[2,16]{1,0:T(2,128)S(1)}, u32[]{:S(2)}, u32[]{:S(2)}) collective-permute-start(f32[2,16]{1,0:T(2,128)S(1)} %add.39), channel_id=1, source_target_pairs={{0,8},{1,9},{2,10},{3,11},{4,12},{5,13},{6,14},{7,15},{8,0},{9,1},... | collective-permute-start | bytes 392 | tf_op jit(solution)/shard_map/ppermute | solution.py:613

commit v7 on v6

--- a/solution.py
+++ b/solution.py
@@ -401,7 +401,7 @@
     queries, rows, features = own.shape
     docs, tokens = starts.shape
     width = in_basis.shape[1]
-    block = math.gcd(rows, 512)
+    block = math.gcd(rows, 256)
     all_pieces = [turned_piece] + list(pieces)
     count = len(all_pieces)
     raw = [x for x, _ in pieces] + list(early)
@@ -643,7 +643,7 @@
     near_g, g_far = pack_grads(near_g, g_far, side_g)
     near_g = swap(near_g, 4)
     g_far = swap(g_far, 12)
-    cut = features * 3 // 4
+    cut = features * 7 // 8
     x0, x1, x2, x6 = turn_inputs([layer_inputs, side_x, near_x, far_x], in_basis)
     turned = last_round(middle_x, middle, in_basis, cut, [sides, own, x0])
     high, low = [swap(value, 2) for value in turned]

time: 94.3 us -> 94.3 us (level)
  no operation moved by 1% of the time
where the time goes in v7:
time: 94.3 us; the launch traced here: 94.1 us
  waiting for transfers between devices  33.9 us (36%)
  Pallas kernels  32.3 us (34%)
  starting transfers between devices  23.6 us (25%)
  local copies, waits for them, and re-layouts  3.7 us (4%)
    ppermute x20, waiting for transfers between devices, swap(): return lax.ppermute(value, 'dp', [(i, i ^ offset) for i in range(devices)])  33.9 us
    ppermute x20, starting transfers between devices, swap(): return lax.ppermute(value, 'dp', [(i, i ^ offset) for i in range(devices)])  23.6 us
    pallas_call x1, Pallas kernels, join_and_tally(): call(body, in_specs=[pl.BlockSpec(memory_space=pltpu.SMEM)] + [hbm] * (le...  14.2 us
    pallas_call x1, Pallas kernels, precondition_rows(): call(body, grid_spec=grid_spec, out_shape=jax.ShapeDtypeStruct((queries,...  6.64 us
    pallas_call x2, Pallas kernels, rotate(): call(body, cost=cost, in_specs=[pl.BlockSpec(memory_space=pltpu.SMEM), hb...  4.59 us
    unnamed x30, local copies, waits for them, and re-layouts  2.7 us
    pallas_call x2, Pallas kernels, project(): call(body, in_specs=[vmem] * (2 + len(bases)) + [pl.BlockSpec(memory_spac...  2.5 us
  transfers between devices with their start and end apart: 20, of which 10 were waited for; matrix products, arithmetic and copies ran while one was open for 1% of the time, Pallas kernels for 33%

profile of v7, /device:TPU:0, one launch (start us, length us, event | category | flops | bytes accessed | tf_op | source)
XLA Modules:
  0.0 94.1 jit_solution(2565899881514902747)
XLA Ops:
  0.0 5.0 %collective-permute-start.2 = (bf16[128,2048]{1,0:T(8,128)(2,1)}, bf16[128,2048]{1,0:T(8,128)(2,1)S(1)}, u32[]{:S(2)}, u32[]{:S(2)}) collective-permute-start(bf16[128,2048]{1,0:T(8,128)(2,1)} %refs_0_.1), channel_id=1, source_target_pairs={{0,12},{1,13},{2,14},{3,15},{4,8},{5,9},{6,10},{7,11},{8,4},{9,5},... | collective-permute-start | bytes 1572872 | tf_op jit(solution)/shard_map/ppermute | solution.py:613
  5.0 1.5 %collective-permute-start = (bf16[128,2048]{1,0:T(8,128)(2,1)}, bf16[128,2048]{1,0:T(8,128)(2,1)S(1)}, u32[]{:S(2)}, u32[]{:S(2)}) collective-permute-start(bf16[128,2048]{1,0:T(8,128)(2,1)} %refs_0_.1), channel_id=1, source_target_pairs={{0,2},{1,3},{2,0},{3,1},{4,6},{5,7},{6,4},{7,5},{8,10},{9,11},{10,... | collective-permute-start | bytes 1572872 | tf_op jit(solution)/shard_map/ppermute | solution.py:613
  6.6 2.2 %copy-done = f32[8,512,256]{2,1,0:T(8,128)S(1)} copy-done((f32[8,512,256]{2,1,0:T(8,128)S(1)}, f32[8,512,256]{2,1,0:T(8,128)}, u32[]{:S(2)}) %copy-start) | copy-done | bytes 4194328
  8.8 0.7 sum_eigenvalues.1.refs_0_
  9.4 0.6 collective-permute-start.6
  10.0 1.9 %rotate.3 = bf16[3072,128]{1,0:T(8,128)(2,1)S(1)} custom-call(s32[1]{0:T(128)} %bitcast.9.chip_ref, bf16[128,8192]{1,0:T(8,128)(2,1)} %g_hbm.3, bf16[64,128,128]{2,1,0:T(8,128)(2,1)} %ob_ref.1, f32[8,128]{1,0:T(8,128)S(1)} %sum_eigenvalues.1.refs_0_), custom_call_target="tpu_custom_call" | custom-call | flops 1 | bytes 1 | tf_op jit(solution)/shard_map/rotate/pallas_call | solution.py:162
  11.9 1.6 %collective-permute-start.10 = (bf16[3072,128]{1,0:T(8,128)(2,1)S(1)}, bf16[3072,128]{1,0:T(8,128)(2,1)S(1)}, u32[]{:S(2)}, u32[]{:S(2)}) collective-permute-start(bf16[3072,128]{1,0:T(8,128)(2,1)S(1)} %rotate.3), channel_id=1, source_target_pairs={{0,2},{1,3},{2,0},{3,1},{4,6},{5,7},{6,4},{7,5},{8,10},{9,11},{10,... | collective-permute-start | bytes 2359304 | tf_op jit(solution)/shard_map/ppermute | solution.py:613
  13.5 2.7 %rotate.2 = (bf16[1024,128]{1,0:T(8,128)(2,1)S(1)}, bf16[2048,128]{1,0:T(8,128)(2,1)S(1)}, bf16[1024,128]{1,0:T(8,128)(2,1)S(1)}, bf16[1024,128]{1,0:T(8,128)(2,1)S(1)}) custom-call(s32[1]{0:T(128)} %bitcast.9.chip_ref, bf16[128,8192]{1,0:T(8,128)(2,1)} %g_hbm.3, bf16[64,128,128]{2,1,0:T(8,128)(2,1)} %ob_ref.1), custom_call_target="tpu_custom_call" | custom-call | flops 99999997952 | bytes 1 | tf_op jit(solution)/shard_map/rotate/pallas_call | solution.py:162
  16.2 3.9 %collective-permute-done.6 = f32[8,128]{1,0:T(8,128)S(1)} collective-permute-done((f32[8,128]{1,0:T(8,128)S(1)}, f32[8,128]{1,0:T(8,128)S(1)}, u32[]{:S(2)}, u32[]{:S(2)}) %collective-permute-start.6) | collective-permute-done | bytes 4128 | tf_op jit(solution)/shard_map/ppermute | solution.py:613
  20.2 1.2 %collective-permute-done.7 = f32[8,128]{1,0:T(8,128)S(1)} collective-permute-done((f32[8,128]{1,0:T(8,128)S(1)}, f32[8,128]{1,0:T(8,128)S(1)}, u32[]{:S(2)}, u32[]{:S(2)}) %collective-permute-start.7) | collective-permute-done | bytes 4128 | tf_op jit(solution)/shard_map/ppermute | solution.py:613
  21.4 7.2 %collective-permute-done.8 = f32[8,128]{1,0:T(8,128)S(1)} collective-permute-done((f32[8,128]{1,0:T(8,128)S(1)}, f32[8,128]{1,0:T(8,128)S(1)}, u32[]{:S(2)}, u32[]{:S(2)}) %collective-permute-start.8) | collective-permute-done | bytes 4128 | tf_op jit(solution)/shard_map/ppermute | solution.py:613
  28.6 0.1 pair_up.1
  28.7 1.1 %collective-permute-start.9 = (f32[8,128]{1,0:T(8,128)S(1)}, f32[8,128]{1,0:T(8,128)S(1)}, u32[]{:S(2)}, u32[]{:S(2)}) collective-permute-start(f32[8,128]{1,0:T(8,128)S(1)} %hold.3), channel_id=1, source_target_pairs={{0,8},{1,9},{2,10},{3,11},{4,12},{5,13},{6,14},{7,15},{8,0},{9,1},... | collective-permute-start | bytes 12296 | tf_op jit(solution)/shard_map/ppermute | solution.py:613
  29.8 1.0 %collective-permute-start.3 = (bf16[256,2048]{1,0:T(8,128)(2,1)S(1)}, bf16[256,2048]{1,0:T(8,128)(2,1)S(1)}, u32[]{:S(2)}, u32[]{:S(2)}) collective-permute-start(bf16[256,2048]{1,0:T(8,128)(2,1)S(1)} %get-tuple-element.30.refs_0_), channel_id=1, source_target_pairs={{0,2},{1,3},{2,0},{3,1},{4,6},{5,7},{6,4},{7,5},{8,10},{9,11},{10,... | collective-permute-start | bytes 3145736 | tf_op jit(solution)/shard_map/ppermute | solution.py:613
  30.9 2.4 %collective-permute-start.5 = (bf16[2048,128]{1,0:T(8,128)(2,1)S(1)}, bf16[2048,128]{1,0:T(8,128)(2,1)S(1)}, u32[]{:S(2)}, u32[]{:S(2)}) collective-permute-start(bf16[2048,128]{1,0:T(8,128)(2,1)S(1)} %get-tuple-element.31), channel_id=1, source_target_pairs={{0,8},{1,9},{2,10},{3,11},{4,12},{5,13},{6,14},{7,15},{8,0},{9,1},... | collective-permute-start | bytes 1572872 | tf_op jit(solution)/shard_map/ppermute | solution.py:613
  33.2 1.7 %collective-permute-start.4 = (bf16[128,2048]{1,0:T(8,128)(2,1)S(1)}, bf16[128,2048]{1,0:T(8,128)(2,1)S(1)}, u32[]{:S(2)}, u32[]{:S(2)}) collective-permute-start(bf16[128,2048]{1,0:T(8,128)(2,1)S(1)} %collective-permute-done.2.refs_3_.b_ref.refs_1_), channel_id=1, source_target_pairs={{0,4},{1,5},{2,6},{3,7},{4,0},{5,1},{6,2},{7,3},{8,12},{9,13},{10,... | collective-permute-start | bytes 1572872 | tf_op jit(solution)/shard_map/ppermute | solution.py:613
  34.9 0.8 turn_inputs.1
  35.8 1.3 %collective-permute-done.10.refs_3_.refs_10_.a_ref = bf16[3072,128]{1,0:T(8,128)(2,1)S(1)} collective-permute-done((bf16[3072,128]{1,0:T(8,128)(2,1)S(1)}, bf16[3072,128]{1,0:T(8,128)(2,1)S(1)}, u32[]{:S(2)}, u32[]{:S(2)}) %collective-permute-start.10) | collective-permute-done | bytes 786464 | tf_op jit(solution)/shard_map/ppermute | solution.py:613
  37.1 6.6 %precondition.1.refs_1_.refs_11_ = bf16[2,512,2048]{2,1,0:T(8,128)(2,1)} custom-call(s32[1]{0:T(128)} %bitcast.7.me_ref, bf16[8,2,512,256]{3,2,1,0:T(8,128)(2,1)S(1)} %copy-done.13, f32[8,512,256]{2,1,0:T(8,128)S(1)} %copy-done.1, f32[8,128]{1,0:T(8,128)S(1)} %add.36.s_ref, bf16[64,128,128]{2,1,0:T(8,128)(2,1)S(1)} %copy-done.4, ...), custom_call_target="tpu_custom_call" | custom-call | flops 99999997952 | bytes 1 | tf_op jit(solution)/shard_map/precondition/pallas_call | solution.py:391
  43.7 0.1 collective-permute-start.11
  43.8 1.1 %pack_grads.1 = (bf16[2048,128]{1,0:T(8,128)(2,1)}, bf16[2048,128]{1,0:T(8,128)(2,1)}) custom-call(bf16[1024,128]{1,0:T(8,128)(2,1)S(1)} %get-tuple-element.41.n_ref, bf16[1024,128]{1,0:T(8,128)(2,1)S(1)} %get-tuple-element.42.f_ref, bf16[3072,128]{1,0:T(8,128)(2,1)S(1)} %collective-permute-done.10.refs_3_.refs_10_.a_ref), custom_call_target="tpu_custom_call" | custom-call | flops 1 | bytes 1 | tf_op jit(solution)/shard_map/pack_grads/pallas_call | solution.py:249
  44.9 0.1 collective-permute-start.14
  45.0 11.2 %collective-permute-done.5.m_ref.refs_8_ = bf16[2048,128]{1,0:T(8,128)(2,1)S(1)} collective-permute-done((bf16[2048,128]{1,0:T(8,128)(2,1)S(1)}, bf16[2048,128]{1,0:T(8,128)(2,1)S(1)}, u32[]{:S(2)}, u32[]{:S(2)}) %collective-permute-start.5) | collective-permute-done | bytes 524320 | tf_op jit(solution)/shard_map/ppermute | solution.py:613
  56.2 2.6 %collective-permute-start.15 = (bf16[2048,128]{1,0:T(8,128)(2,1)}, bf16[2048,128]{1,0:T(8,128)(2,1)S(1)}, u32[]{:S(2)}, u32[]{:S(2)}) collective-permute-start(bf16[2048,128]{1,0:T(8,128)(2,1)} %get-tuple-element.44), channel_id=1, source_target_pairs={{0,12},{1,13},{2,14},{3,15},{4,8},{5,9},{6,10},{7,11},{8,4},{9,5},... | collective-permute-start | bytes 1572872 | tf_op jit(solution)/shard_map/ppermute | solution.py:613
  58.9 0.6 last_round.1
  59.5 0.4 copy-done.5
  59.9 0.7 collective-permute-start.13
  60.6 1.3 %collective-permute-start.12 = (bf16[1280,128]{1,0:T(8,128)(2,1)S(1)}, bf16[1280,128]{1,0:T(8,128)(2,1)S(1)}, u32[]{:S(2)}, u32[]{:S(2)}) collective-permute-start(bf16[1280,128]{1,0:T(8,128)(2,1)S(1)} %get-tuple-element.33.refs_7_), channel_id=1, source_target_pairs={{0,2},{1,3},{2,0},{3,1},{4,6},{5,7},{6,4},{7,5},{8,10},{9,11},{10,... | collective-permute-start | bytes 983048 | tf_op jit(solution)/shard_map/ppermute | solution.py:613
  62.0 0.1 copy.12
  62.1 0.1 reduce
  62.2 0.1 stack.40.where_ref
  62.3 0.1 pad_add_fusion.where_ref
  62.4 0.1 broadcast_in_dim.7.refs_13_.refs_8_
  62.5 0.1 broadcast_in_dim.8.refs_14_.refs_9_
  62.5 14.2 %join_and_tally.1 = (f32[2,16,128]{2,1,0:T(8,128)S(1)}, bf16[2,2,512,2048]{3,2,1,0:T(8,128)(2,1)S(1)}, f32[2,2,512,128]{3,2,1,0:T(8,128)S(1)}, f32[2,2,512,128]{...) custom-call(s32[4]{0:T(128)S(1)} %pad_add_fusion.where_ref, ...), custom_call_target="tpu_custom_call" | custom-call | flops 1 | bytes 1 | tf_op jit(solution)/shard_map/join_and_tally/pallas_call | solution.py:501
  76.7 2.1 %project.2.refs_0_ = f32[2,2,512,128]{3,2,1,0:T(8,128)S(1)} custom-call(bf16[1792,128]{1,0:T(8,128)(2,1)S(1)} %collective-permute-done.13.x_ref, bf16[2,2,512,2048]{3,2,1,0:T(8,128)(2,1)S(1)} %get-tuple-element.39.p_ref, f32[2,16,128]{2,1,0:T(8,128)S(1)} %get-tuple-element.40.refs_0_.refs_10_), custom_call_target="tpu_custom_call" | custom-call | flops 1 | bytes 1 | tf_op jit(solution)/shard_map/project/pallas_call | solution.py:556
  78.8 0.4 project.3.refs_4_
  79.3 0.1 collective-permute-done.15.refs_6_
  79.4 1.2 %tally.1 = f32[2,16,128]{2,1,0:T(8,128)S(1)} custom-call(s32[6]{0:T(128)S(1)} %stack.40.where_ref, f32[2,2,512,128]{3,2,1,0:T(8,128)S(1)} %get-tuple-element.35.refs_0_, f32[2,2,512,128]{3,2,1,0:T(8,128)S(1)} %get-tuple-element.36.refs_1_, f32[2,2,512,128]{3,2,1,0:T(8,128)S(1)} %get-tuple-element.37.refs_2_, ...), custom_call_target="tpu_custom_call" | custom-call | flops 1 | bytes 1 | tf_op jit(solution)/shard_map/tally/pallas_call | solution.py:591
  80.6 0.1 reduce_sum.9
  80.7 1.1 %collective-permute-done.16 = f32[2,16]{1,0:T(2,128)S(1)} collective-permute-done((f32[2,16]{1,0:T(2,128)S(1)}, f32[2,16]{1,0:T(2,128)S(1)}, u32[]{:S(2)}, u32[]{:S(2)}) %collective-permute-start.16) | collective-permute-done | bytes 160 | tf_op jit(solution)/shard_map/ppermute | solution.py:613
  81.8 1.6 %collective-permute-start.17 = (f32[2,16]{1,0:T(2,128)S(1)}, f32[2,16]{1,0:T(2,128)S(1)}, u32[]{:S(2)}, u32[]{:S(2)}) collective-permute-start(f32[2,16]{1,0:T(2,128)S(1)} %add.37), channel_id=1, source_target_pairs={{0,2},{1,3},{2,0},{3,1},{4,6},{5,7},{6,4},{7,5},{8,10},{9,11},{10,... | collective-permute-start | bytes 392 | tf_op jit(solution)/shard_map/ppermute | solution.py:613
  83.4 2.0 %collective-permute-done.17 = f32[2,16]{1,0:T(2,128)S(1)} collective-permute-done((f32[2,16]{1,0:T(2,128)S(1)}, f32[2,16]{1,0:T(2,128)S(1)}, u32[]{:S(2)}, u32[]{:S(2)}) %collective-permute-start.17) | collective-permute-done | bytes 160 | tf_op jit(solution)/shard_map/ppermute | solution.py:613
  85.4 1.1 %collective-permute-start.18 = (f32[2,16]{1,0:T(2,128)S(1)}, f32[2,16]{1,0:T(2,128)S(1)}, u32[]{:S(2)}, u32[]{:S(2)}) collective-permute-start(f32[2,16]{1,0:T(2,128)S(1)} %add.38), channel_id=1, source_target_pairs={{0,4},{1,5},{2,6},{3,7},{4,0},{5,1},{6,2},{7,3},{8,12},{9,13},{10,... | collective-permute-start | bytes 392 | tf_op jit(solution)/shard_map/ppermute | solution.py:613
  86.5 2.5 %collective-permute-done.18 = f32[2,16]{1,0:T(2,128)S(1)} collective-permute-done((f32[2,16]{1,0:T(2,128)S(1)}, f32[2,16]{1,0:T(2,128)S(1)}, u32[]{:S(2)}, u32[]{:S(2)}) %collective-permute-start.18) | collective-permute-done | bytes 160 | tf_op jit(solution)/shard_map/ppermute | solution.py:613
  89.0 1.2 %collective-permute-start.19 = (f32[2,16]{1,0:T(2,128)S(1)}, f32[2,16]{1,0:T(2,128)S(1)}, u32[]{:S(2)}, u32[]{:S(2)}) collective-permute-start(f32[2,16]{1,0:T(2,128)S(1)} %add.39), channel_id=1, source_target_pairs={{0,8},{1,9},{2,10},{3,11},{4,12},{5,13},{6,14},{7,15},{8,0},{9,1},... | collective-permute-start | bytes 392 | tf_op jit(solution)/shard_map/ppermute | solution.py:613
  90.2 3.2 %collective-permute-done.19 = f32[2,16]{1,0:T(2,128)S(1)} collective-permute-done((f32[2,16]{1,0:T(2,128)S(1)}, f32[2,16]{1,0:T(2,128)S(1)}, u32[]{:S(2)}, u32[]{:S(2)}) %collective-permute-start.19) | collective-permute-done | bytes 160 | tf_op jit(solution)/shard_map/ppermute | solution.py:613
  93.4 0.7 dynamic-slice_reduce_fusion
  (54 shorter events, 0.2 us)
Async XLA Ops:
  0.0 28.6 %collective-permute-start.2 = (bf16[128,2048]{1,0:T(8,128)(2,1)}, bf16[128,2048]{1,0:T(8,128)(2,1)S(1)}, u32[]{:S(2)}, u32[]{:S(2)}) collective-permute-start(bf16[128,2048]{1,0:T(8,128)(2,1)} %refs_0_.1), channel_id=1, source_target_pairs={{0,12},{1,13},{2,14},{3,15},{4,8},{5,9},{6,10},{7,11},{8,4},{9,5},... | collective-permute-start | bytes 1572872 | tf_op jit(solution)/shard_map/ppermute | solution.py:613
  5.0 23.6 %collective-permute-start = (bf16[128,2048]{1,0:T(8,128)(2,1)}, bf16[128,2048]{1,0:T(8,128)(2,1)S(1)}, u32[]{:S(2)}, u32[]{:S(2)}) collective-permute-start(bf16[128,2048]{1,0:T(8,128)(2,1)} %refs_0_.1), channel_id=1, source_target_pairs={{0,2},{1,3},{2,0},{3,1},{4,6},{5,7},{6,4},{7,5},{8,10},{9,11},{10,... | collective-permute-start | bytes 1572872 | tf_op jit(solution)/shard_map/ppermute | solution.py:613
  6.6 22.1 %collective-permute-start.1 = (bf16[128,2048]{1,0:T(8,128)(2,1)}, bf16[128,2048]{1,0:T(8,128)(2,1)S(1)}, u32[]{:S(2)}, u32[]{:S(2)}) collective-permute-start(bf16[128,2048]{1,0:T(8,128)(2,1)} %refs_0_.1), channel_id=1, source_target_pairs={{0,4},{1,5},{2,6},{3,7},{4,0},{5,1},{6,2},{7,3},{8,12},{9,13},{10,... | collective-permute-start | bytes 1572872 | tf_op jit(solution)/shard_map/ppermute | solution.py:613
  6.6 2.2 %copy-start = (f32[8,512,256]{2,1,0:T(8,128)S(1)}, f32[8,512,256]{2,1,0:T(8,128)}, u32[]{:S(2)}) copy-start(f32[8,512,256]{2,1,0:T(8,128)} %e_ref.3) | copy-start | bytes 12582916
  9.4 10.8 %collective-permute-start.6 = (f32[8,128]{1,0:T(8,128)S(1)}, f32[8,128]{1,0:T(8,128)S(1)}, u32[]{:S(2)}, u32[]{:S(2)}) collective-permute-start(f32[8,128]{1,0:T(8,128)S(1)} %sum_eigenvalues.1.refs_0_), channel_id=1, source_target_pairs={{0,2},{1,3},{2,0},{3,1},{4,6},{5,7},{6,4},{7,5},{8,10},{9,11},{10,... | collective-permute-start | bytes 12296 | tf_op jit(solution)/shard_map/ppermute | solution.py:613
  11.9 23.0 %copy-start.3 = (bf16[16,128,128]{2,1,0:T(8,128)(2,1)S(1)}, bf16[16,128,128]{2,1,0:T(8,128)(2,1)}, u32[]{:S(2)}) copy-start(bf16[16,128,128]{2,1,0:T(8,128)(2,1)} %refs_5_.1) | copy-start | bytes 1572868
  11.9 23.0 %copy-start.11 = (bf16[128,2048]{1,0:T(8,128)(2,1)S(1)}, bf16[128,2048]{1,0:T(8,128)(2,1)}, u32[]{:S(2)}) copy-start(bf16[128,2048]{1,0:T(8,128)(2,1)} %refs_0_.1) | copy-start | bytes 1572868
  11.9 25.1 %collective-permute-start.10 = (bf16[3072,128]{1,0:T(8,128)(2,1)S(1)}, bf16[3072,128]{1,0:T(8,128)(2,1)S(1)}, u32[]{:S(2)}, u32[]{:S(2)}) collective-permute-start(bf16[3072,128]{1,0:T(8,128)(2,1)S(1)} %rotate.3), channel_id=1, source_target_pairs={{0,2},{1,3},{2,0},{3,1},{4,6},{5,7},{6,4},{7,5},{8,10},{9,11},{10,... | collective-permute-start | bytes 2359304 | tf_op jit(solution)/shard_map/ppermute | solution.py:613
  13.5 23.5 %copy-start.13 = (bf16[8,2,512,256]{3,2,1,0:T(8,128)(2,1)S(1)}, bf16[8,2,512,256]{3,2,1,0:T(8,128)(2,1)}, u32[]{:S(2)}) copy-start(bf16[8,2,512,256]{3,2,1,0:T(8,128)(2,1)} %q_ref.1) | copy-start | bytes 12582916
  16.2 27.5 %copy-start.12 = (bf16[1024,128]{1,0:T(8,128)(2,1)}, bf16[1024,128]{1,0:T(8,128)(2,1)S(1)}, u32[]{:S(2)}) copy-start(bf16[1024,128]{1,0:T(8,128)(2,1)S(1)} %get-tuple-element.34.refs_9_) | copy-start | bytes 786436
  16.2 20.8 %copy-start.1 = (f32[8,512,256]{2,1,0:T(8,128)S(1)}, f32[8,512,256]{2,1,0:T(8,128)}, u32[]{:S(2)}) copy-start(f32[8,512,256]{2,1,0:T(8,128)} %e_ref.3) | copy-start | bytes 12582916
  16.2 20.8 %copy-start.4 = (bf16[64,128,128]{2,1,0:T(8,128)(2,1)S(1)}, bf16[64,128,128]{2,1,0:T(8,128)(2,1)}, u32[]{:S(2)}) copy-start(bf16[64,128,128]{2,1,0:T(8,128)(2,1)} %ob_ref.1) | copy-start | bytes 6291460
  20.2 1.2 %collective-permute-start.7 = (f32[8,128]{1,0:T(8,128)S(1)}, f32[8,128]{1,0:T(8,128)S(1)}, u32[]{:S(2)}, u32[]{:S(2)}) collective-permute-start(f32[8,128]{1,0:T(8,128)S(1)} %hold.2), channel_id=1, source_target_pairs={{0,1},{1,0},{2,3},{3,2},{4,5},{5,4},{6,7},{7,6},{8,9},{9,8},{10,11... | collective-permute-start | bytes 12296 | tf_op jit(solution)/shard_map/ppermute | solution.py:613
  21.4 7.2 %collective-permute-start.8 = (f32[8,128]{1,0:T(8,128)S(1)}, f32[8,128]{1,0:T(8,128)S(1)}, u32[]{:S(2)}, u32[]{:S(2)}) collective-permute-start(f32[8,128]{1,0:T(8,128)S(1)} %add.34), channel_id=1, source_target_pairs={{0,4},{1,5},{2,6},{3,7},{4,0},{5,1},{6,2},{7,3},{8,12},{9,13},{10,... | collective-permute-start | bytes 12296 | tf_op jit(solution)/shard_map/ppermute | solution.py:613
  28.7 7.0 %collective-permute-start.9 = (f32[8,128]{1,0:T(8,128)S(1)}, f32[8,128]{1,0:T(8,128)S(1)}, u32[]{:S(2)}, u32[]{:S(2)}) collective-permute-start(f32[8,128]{1,0:T(8,128)S(1)} %hold.3), channel_id=1, source_target_pairs={{0,8},{1,9},{2,10},{3,11},{4,12},{5,13},{6,14},{7,15},{8,0},{9,1},... | collective-permute-start | bytes 12296 | tf_op jit(solution)/shard_map/ppermute | solution.py:613
  29.8 29.1 %collective-permute-start.3 = (bf16[256,2048]{1,0:T(8,128)(2,1)S(1)}, bf16[256,2048]{1,0:T(8,128)(2,1)S(1)}, u32[]{:S(2)}, u32[]{:S(2)}) collective-permute-start(bf16[256,2048]{1,0:T(8,128)(2,1)S(1)} %get-tuple-element.30.refs_0_), channel_id=1, source_target_pairs={{0,2},{1,3},{2,0},{3,1},{4,6},{5,7},{6,4},{7,5},{8,10},{9,11},{10,... | collective-permute-start | bytes 3145736 | tf_op jit(solution)/shard_map/ppermute | solution.py:613
  30.9 25.4 %collective-permute-start.5 = (bf16[2048,128]{1,0:T(8,128)(2,1)S(1)}, bf16[2048,128]{1,0:T(8,128)(2,1)S(1)}, u32[]{:S(2)}, u32[]{:S(2)}) collective-permute-start(bf16[2048,128]{1,0:T(8,128)(2,1)S(1)} %get-tuple-element.31), channel_id=1, source_target_pairs={{0,8},{1,9},{2,10},{3,11},{4,12},{5,13},{6,14},{7,15},{8,0},{9,1},... | collective-permute-start | bytes 1572872 | tf_op jit(solution)/shard_map/ppermute | solution.py:613
  33.2 25.6 %collective-permute-start.4 = (bf16[128,2048]{1,0:T(8,128)(2,1)S(1)}, bf16[128,2048]{1,0:T(8,128)(2,1)S(1)}, u32[]{:S(2)}, u32[]{:S(2)}) collective-permute-start(bf16[128,2048]{1,0:T(8,128)(2,1)S(1)} %collective-permute-done.2.refs_3_.b_ref.refs_1_), channel_id=1, source_target_pairs={{0,4},{1,5},{2,6},{3,7},{4,0},{5,1},{6,2},{7,3},{8,12},{9,13},{10,... | collective-permute-start | bytes 1572872 | tf_op jit(solution)/shard_map/ppermute | solution.py:613
  35.7 8.0 %copy-start.8 = (bf16[2048,128]{1,0:T(8,128)(2,1)}, bf16[2048,128]{1,0:T(8,128)(2,1)S(1)}, u32[]{:S(2)}) copy-start(bf16[2048,128]{1,0:T(8,128)(2,1)S(1)} %get-tuple-element.26.refs_1_) | copy-start | bytes 1572868
  35.7 8.0 %copy-start.9 = (bf16[2048,128]{1,0:T(8,128)(2,1)}, bf16[2048,128]{1,0:T(8,128)(2,1)S(1)}, u32[]{:S(2)}) copy-start(bf16[2048,128]{1,0:T(8,128)(2,1)S(1)} %get-tuple-element.27.refs_2_) | copy-start | bytes 1572868
  35.7 8.0 %copy-start.10 = (bf16[2048,128]{1,0:T(8,128)(2,1)}, bf16[2048,128]{1,0:T(8,128)(2,1)S(1)}, u32[]{:S(2)}) copy-start(bf16[2048,128]{1,0:T(8,128)(2,1)S(1)} %get-tuple-element.28.refs_3_) | copy-start | bytes 1572868
  35.7 23.2 %copy-start.7 = (bf16[2048,128]{1,0:T(8,128)(2,1)}, bf16[2048,128]{1,0:T(8,128)(2,1)S(1)}, u32[]{:S(2)}) copy-start(bf16[2048,128]{1,0:T(8,128)(2,1)S(1)} %get-tuple-element.25.refs_2_.refs_0_) | copy-start | bytes 1572868
  37.0 6.8 %copy-start.2 = (bf16[3072,128]{1,0:T(8,128)(2,1)}, bf16[3072,128]{1,0:T(8,128)(2,1)S(1)}, u32[]{:S(2)}) copy-start(bf16[3072,128]{1,0:T(8,128)(2,1)S(1)} %collective-permute-done.10.refs_3_.refs_10_.a_ref) | copy-start | bytes 2359300
  43.7 18.7 %collective-permute-start.11 = (bf16[2,512,2048]{2,1,0:T(8,128)(2,1)}, bf16[2,512,2048]{2,1,0:T(8,128)(2,1)}, u32[]{:S(2)}, u32[]{:S(2)}) collective-permute-start(bf16[2,512,2048]{2,1,0:T(8,128)(2,1)} %precondition.1.refs_1_.refs_11_), channel_id=1, source_target_pairs={{0,1},{1,0},{2,3},{3,2},{4,5},{5,4},{6,7},{7,6},{8,9},{9,8},{10,11... | collective-permute-start | bytes 12582920 | tf_op jit(solution)/shard_map/ppermute | solution.py:613
  44.9 34.3 %collective-permute-start.14 = (bf16[2048,128]{1,0:T(8,128)(2,1)}, bf16[2048,128]{1,0:T(8,128)(2,1)S(1)}, u32[]{:S(2)}, u32[]{:S(2)}) collective-permute-start(bf16[2048,128]{1,0:T(8,128)(2,1)} %get-tuple-element.43), channel_id=1, source_target_pairs={{0,4},{1,5},{2,6},{3,7},{4,0},{5,1},{6,2},{7,3},{8,12},{9,13},{10,... | collective-permute-start | bytes 1572872 | tf_op jit(solution)/shard_map/ppermute | solution.py:613
  56.2 3.2 %copy-start.6 = (bf16[2048,128]{1,0:T(8,128)(2,1)}, bf16[2048,128]{1,0:T(8,128)(2,1)S(1)}, u32[]{:S(2)}) copy-start(bf16[2048,128]{1,0:T(8,128)(2,1)S(1)} %collective-permute-done.5.m_ref.refs_8_) | copy-start | bytes 1572868
  56.2 23.1 %collective-permute-start.15 = (bf16[2048,128]{1,0:T(8,128)(2,1)}, bf16[2048,128]{1,0:T(8,128)(2,1)S(1)}, u32[]{:S(2)}, u32[]{:S(2)}) collective-permute-start(bf16[2048,128]{1,0:T(8,128)(2,1)} %get-tuple-element.44), channel_id=1, source_target_pairs={{0,12},{1,13},{2,14},{3,15},{4,8},{5,9},{6,10},{7,11},{8,4},{9,5},... | collective-permute-start | bytes 1572872 | tf_op jit(solution)/shard_map/ppermute | solution.py:613
  58.9 1.1 %copy-start.5 = (bf16[256,2048]{1,0:T(8,128)(2,1)}, bf16[256,2048]{1,0:T(8,128)(2,1)S(1)}, u32[]{:S(2)}) copy-start(bf16[256,2048]{1,0:T(8,128)(2,1)S(1)} %collective-permute-done.3.refs_0_.refs_4_) | copy-start | bytes 3145732
  58.9 3.1 %copy-start.14 = (s32[16]{0:T(128)S(1)}, s32[16]{0:T(128)}, u32[]{:S(2)}) copy-start(s32[16]{0:T(128)} %param.13) | copy-start | bytes 196
  59.9 16.8 %collective-permute-start.13 = (bf16[1792,128]{1,0:T(8,128)(2,1)S(1)}, bf16[1792,128]{1,0:T(8,128)(2,1)S(1)}, u32[]{:S(2)}, u32[]{:S(2)}) collective-permute-start(bf16[1792,128]{1,0:T(8,128)(2,1)S(1)} %get-tuple-element.32.refs_6_), channel_id=1, source_target_pairs={{0,2},{1,3},{2,0},{3,1},{4,6},{5,7},{6,4},{7,5},{8,10},{9,11},{10,... | collective-permute-start | bytes 1376264 | tf_op jit(solution)/shard_map/ppermute | solution.py:613
  60.6 18.2 %collective-permute-start.12 = (bf16[1280,128]{1,0:T(8,128)(2,1)S(1)}, bf16[1280,128]{1,0:T(8,128)(2,1)S(1)}, u32[]{:S(2)}, u32[]{:S(2)}) collective-permute-start(bf16[1280,128]{1,0:T(8,128)(2,1)S(1)} %get-tuple-element.33.refs_7_), channel_id=1, source_target_pairs={{0,2},{1,3},{2,0},{3,1},{4,6},{5,7},{6,4},{7,5},{8,10},{9,11},{10,... | collective-permute-start | bytes 983048 | tf_op jit(solution)/shard_map/ppermute | solution.py:613
  80.7 1.1 %collective-permute-start.16 = (f32[2,16]{1,0:T(2,128)S(1)}, f32[2,16]{1,0:T(2,128)S(1)}, u32[]{:S(2)}, u32[]{:S(2)}) collective-permute-start(f32[2,16]{1,0:T(2,128)S(1)} %reduce_sum.9), channel_id=1, source_target_pairs={{0,1},{1,0},{2,3},{3,2},{4,5},{5,4},{6,7},{7,6},{8,9},{9,8},{10,11... | collective-permute-start | bytes 392 | tf_op jit(solution)/shard_map/ppermute | solution.py:613
  81.8 3.6 %collective-permute-start.17 = (f32[2,16]{1,0:T(2,128)S(1)}, f32[2,16]{1,0:T(2,128)S(1)}, u32[]{:S(2)}, u32[]{:S(2)}) collective-permute-start(f32[2,16]{1,0:T(2,128)S(1)} %add.37), channel_id=1, source_target_pairs={{0,2},{1,3},{2,0},{3,1},{4,6},{5,7},{6,4},{7,5},{8,10},{9,11},{10,... | collective-permute-start | bytes 392 | tf_op jit(solution)/shard_map/ppermute | solution.py:613
  85.4 3.6 %collective-permute-start.18 = (f32[2,16]{1,0:T(2,128)S(1)}, f32[2,16]{1,0:T(2,128)S(1)}, u32[]{:S(2)}, u32[]{:S(2)}) collective-permute-start(f32[2,16]{1,0:T(2,128)S(1)} %add.38), channel_id=1, source_target_pairs={{0,4},{1,5},{2,6},{3,7},{4,0},{5,1},{6,2},{7,3},{8,12},{9,13},{10,... | collective-permute-start | bytes 392 | tf_op jit(solution)/shard_map/ppermute | solution.py:613
  89.0 4.5 %collective-permute-start.19 = (f32[2,16]{1,0:T(2,128)S(1)}, f32[2,16]{1,0:T(2,128)S(1)}, u32[]{:S(2)}, u32[]{:S(2)}) collective-permute-start(f32[2,16]{1,0:T(2,128)S(1)} %add.39), channel_id=1, source_target_pairs={{0,8},{1,9},{2,10},{3,11},{4,12},{5,13},{6,14},{7,15},{8,0},{9,1},... | collective-permute-start | bytes 392 | tf_op jit(solution)/shard_map/ppermute | solution.py:613
